TPU v7x, 128 devices: a whole 4x4x4 slice. The times are simulated.
128 devices in a mesh: ia: 4 (over x), ja: 8 (over y_lo, z), ka: 4 (over y_hi, core).
Axes of the slice: x: 4, y: 4 (y_hi: 2, y_lo: 2; y = y_hi * 2 + y_lo), z: 4, core: 2. Of those that a mesh axis runs over, the one named last changes fastest.
Arguments:
- tokens: bfloat16 [1536, 6144], P('ja', ('ka', 'ia')), may hold values from -6 to 6
- weight: bfloat16 [6144, 24576], P('ka', ('ia', 'ja')), may hold values from -0.078125 to 0.078125
- grad_out: bfloat16 [1536, 24576], P('ja', ('ia', 'ka')), may hold values from -6 to 6
Outputs:
- activated: bfloat16 [1536, 24576], P('ja', ('ia', 'ka'))
- grad_input: bfloat16 [1536, 6144], P('ja', ('ka', 'ia'))
- grad_weight: bfloat16 [6144, 24576], P('ka', ('ia', 'ja'))
All inputs are finite; a program needn't handle non-finite values.
Results may differ from a plain program's by a relative error of at most 0.022.
Values may be sent and summed in bfloat16 or wider, within the bound.
No kernel may reach another device: no remote copies, remote signals or barrier semaphores. Data moves between devices by JAX's collectives and lax.ppermute only.
A program may use at most 128 MiB of HBM per device.

v0:
```python
import jax
import jax.numpy as jnp
from jax import lax
from jax.sharding import PartitionSpec as P

coef_root = 0.7978845608028654
coef_cube = 0.044715


def gelu_pair(hidden):
    tanh_value = jnp.tanh(coef_root * (hidden + coef_cube * hidden * hidden * hidden))
    activ = 0.5 * hidden * (1.0 + tanh_value)
    derivative = 0.5 * (1.0 + tanh_value) + 0.5 * hidden * (
        1.0 - tanh_value * tanh_value
    ) * coef_root * (1.0 + 3.0 * coef_cube * hidden * hidden)
    return (activ, derivative)


def on_device(tokens, weight, grad_out):
    full_rows = lax.all_gather(tokens, "ia", axis=1, tiled=True)
    weight_block = lax.all_gather(weight, "ja", axis=1, tiled=True)
    hidden_part = jnp.dot(full_rows, weight_block, preferred_element_type=jnp.float32)
    hidden = lax.psum_scatter(
        hidden_part.astype(jnp.bfloat16), "ka", scatter_dimension=1, tiled=True
    ).astype(jnp.float32)
    activ, derivative = gelu_pair(hidden)
    activated = activ.astype(jnp.bfloat16)
    grad_hidden = (grad_out.astype(jnp.float32) * derivative).astype(jnp.bfloat16)
    grad_block = lax.all_gather(grad_hidden, "ka", axis=1, tiled=True)
    input_part = lax.dot_general(
        grad_block, weight_block, (((1,), (1,)), ((), ())), preferred_element_type=jnp.float32
    )
    grad_input = lax.psum_scatter(
        input_part.astype(jnp.bfloat16), "ia", scatter_dimension=1, tiled=True
    )
    weight_term = lax.dot_general(
        full_rows, grad_block, (((0,), (0,)), ((), ())), preferred_element_type=jnp.float32
    ).astype(jnp.bfloat16)
    grad_weight = (
        lax.psum_scatter(weight_term, "ja", scatter_dimension=1, tiled=True)
        .astype(jnp.float32)
        .astype(jnp.bfloat16)
    )
    return (activated, grad_input, grad_weight)


def solution(mesh):
    placed = (P("ja", ("ka", "ia")), P("ka", ("ia", "ja")), P("ja", ("ia", "ka")))
    return jax.shard_map(
        on_device,
        mesh=mesh,
        in_specs=placed,
        out_specs=(P("ja", ("ia", "ka")), P("ja", ("ka", "ia")), P("ka", ("ia", "ja"))),
        check_vma=False,
    )
```

profile of v0, /device:TPU:40, one launch (start us, length us, event | category | flops | bytes accessed | tf_op | source)
XLA Modules:
  0.0 521.8 jit_solution(346610079312009704)
XLA Ops:
  7.2 0.0 copy-start.2
  7.2 0.0 all-gather.3.cloned.1.call-start
  7.2 0.7 all-gather.3.cloned.1.call-update
  7.9 0.0 reduce-scatter.6.cloned.1.call-start
  8.0 0.1 copy-done.2
  8.1 13.5 %all_gather.9 = bf16[192,1536]{1,0:T(8,128)(2,1)S(1)} all-gather(bf16[192,384]{1,0:T(8,128)(2,1)S(1)} %copy-done.2), channel_id=1, replica_groups=mesh['ia'=4,'ja'=8,'ka'=4] {'ia'}, dimensions={1}, use_global_device_ids=true | all-gather | bytes 737280 | tf_op jit(solution)/shard_map/all_gather | solution.py:20
  21.6 178.1 %all-gather.3.cloned.1.call-done = bf16[1536,6144]{1,0:T(8,128)(2,1)} async-done(((bf16[1536,768]{1,0:T(8,128)(2,1)}), bf16[1536,6144]{1,0:T(8,128)(2,1)}) %all-gather.3.cloned.1.call-update) | async-done | bytes 18874384 | tf_op jit(solution)/shard_map/all_gather | solution.py:21
  199.7 11.6 %convolution_convert_fusion.1 = bf16[192,6144]{1,0:T(8,128)(2,1)} fusion(bf16[192,1536]{1,0:T(8,128)(2,1)S(1)} %all_gather.9, bf16[1536,6144]{1,0:T(8,128)(2,1)} %all-gather.3.cloned.1.call-done), kind=kOutput, calls=%fused_computation.2 | convolution fusion | flops 3625058304 | bytes 21823488 | tf_op jit(solution)/shard_map/dot_general | solution.py:22
  211.3 0.0 copy-start.1
  211.3 0.0 reduce-scatter.6.cloned.1.call-update
  211.3 0.0 all-gather.5.cloned.1.call-start
  211.4 40.2 %reduce-scatter.6.cloned.1.call-done = bf16[192,1536]{1,0:T(8,128)(2,1)} async-done(((bf16[192,6144]{1,0:T(8,128)(2,1)}), bf16[192,1536]{1,0:T(8,128)(2,1)}) %reduce-scatter.6.cloned.1.call-update) | async-done | bytes 589840 | tf_op jit(solution)/shard_map/reduce_scatter | solution.py:23
  251.6 0.0 copy-done.1
  251.6 3.0 fusion.8
  254.5 0.0 all-gather.5.cloned.1.call-update
  254.5 0.0 reduce-scatter.10.cloned.1.call-start
  254.6 27.6 %all-gather.5.cloned.1.call-done = bf16[192,6144]{1,0:T(8,128)(2,1)} async-done(((bf16[192,1536]{1,0:T(8,128)(2,1)}), bf16[192,6144]{1,0:T(8,128)(2,1)}) %all-gather.5.cloned.1.call-update) | async-done | bytes 2359312 | tf_op jit(solution)/shard_map/all_gather | solution.py:29
  282.2 0.0 copy-start
  282.2 13.6 %convolution_convert_fusion.2 = bf16[192,1536]{1,0:T(8,128)(2,1)S(1)} fusion(bf16[192,6144]{1,0:T(8,128)(2,1)} %all-gather.5.cloned.1.call-done, bf16[1536,6144]{1,0:T(8,128)(2,1)} %all-gather.3.cloned.1.call-done), kind=kOutput, calls=%fused_computation.10 | convolution fusion | flops 3624173568 | bytes 21823488 | tf_op jit(solution)/shard_map/dot_general | solution.py:30
  295.8 1.2 copy.8
  297.0 0.0 reduce-scatter.10.cloned.1.call-update
  297.0 0.2 reduce-scatter.8.cloned.1.call-start
  297.2 0.0 copy-done
  297.2 9.3 %fusion = bf16[1536,6144]{0,1:T(8,128)(2,1)} fusion(bf16[192,6144]{1,0:T(8,128)(2,1)S(1)} %copy-done, bf16[192,1536]{1,0:T(8,128)(2,1)S(1)} %all_gather.9), kind=kOutput, calls=%fused_computation.1 | convolution fusion | flops 3633315840 | bytes 21823488 | tf_op jit(solution)/shard_map/dot_general | solution.py:36
  306.5 0.0 reduce-scatter.8.cloned.1.call-update
  306.5 13.3 %reduce-scatter.10.cloned.1.call-done = bf16[384,192]{1,0:T(8,128)(2,1)} async-done(((bf16[1536,192]{1,0:T(8,128)(2,1)}), bf16[384,192]{1,0:T(8,128)(2,1)}) %reduce-scatter.10.cloned.1.call-update) | async-done | bytes 147472
  319.8 1.7 copy.9
  321.5 189.5 %reduce-scatter.8.cloned.1.call-done = bf16[1536,768]{0,1:T(8,128)(2,1)} async-done(((bf16[1536,6144]{0,1:T(8,128)(2,1)}), bf16[1536,768]{0,1:T(8,128)(2,1)}) %reduce-scatter.8.cloned.1.call-update) | async-done | bytes 2359312 | tf_op jit(solution)/shard_map/reduce_scatter | solution.py:40
  511.0 4.3 copy.7
Async XLA Ops:
  7.2 0.9 copy-start.2
  7.2 192.5 %all-gather.3.cloned.1.call-start = ((), (), s32[]{:S(2)}) async-start(), calls=%async_computation.3 | async-start | bytes 21233664 | tf_op jit(solution)/shard_map/all_gather | solution.py:21
  7.9 243.7 %reduce-scatter.6.cloned.1.call-start = ((), (), s32[]{:S(2)}) async-start(), calls=%async_computation.4 | async-start | bytes 2949120 | tf_op jit(solution)/shard_map/reduce_scatter | solution.py:23
  211.3 40.2 %copy-start.1 = (bf16[192,1536]{1,0:T(8,128)(2,1)S(1)}, bf16[192,1536]{1,0:T(8,128)(2,1)}, u32[]{:S(2)}) copy-start(bf16[192,1536]{1,0:T(8,128)(2,1)} %param.5) | copy-start | bytes 1769476
  211.3 70.9 %all-gather.5.cloned.1.call-start = ((), (), s32[]{:S(2)}) async-start(), calls=%async_computation.5 | async-start | bytes 2949120 | tf_op jit(solution)/shard_map/all_gather | solution.py:29
  254.5 65.3 %reduce-scatter.10.cloned.1.call-start = ((), (), s32[]{:S(2)}) async-start(), calls=%async_computation.7 | async-start | bytes 983040
  282.2 15.0 %copy-start = (bf16[192,6144]{1,0:T(8,128)(2,1)S(1)}, bf16[192,6144]{1,0:T(8,128)(2,1)}, u32[]{:S(2)}) copy-start(bf16[192,6144]{1,0:T(8,128)(2,1)} %all-gather.5.cloned.1.call-done) | copy-start | bytes 7077892
  297.0 214.0 %reduce-scatter.8.cloned.1.call-start = ((), (), s32[]{:S(2)}) async-start(), calls=%async_computation.6 | async-start | bytes 21233664 | tf_op jit(solution)/shard_map/reduce_scatter | solution.py:40
Sparse Core Ops, SparseCore 0:
  9.7 190.0 all-gather.2
  211.5 40.0 reduce-scatter.5
  254.7 27.5 all-gather.4
  297.1 22.6 reduce-scatter.9
  322.3 188.6 reduce-scatter.7
where the time goes:
time: 526 us; the launch traced here: 522 us
  waiting for transfers between devices  449 us (85%)
  matrix products  34.5 us (7%)
  between operations  13.8 us (3%)
  blocking collectives  13.5 us (3%)
  local copies, waits for them, and re-layouts  7.26 us (1%)
    reduce_scatter x1, waiting for transfers between devices, on_device(): lax.psum_scatter(weight_term, 'ja', scatter_dimension=1, tiled=True)  189 us
    all_gather x1, waiting for transfers between devices, on_device(): weight_block = lax.all_gather(weight, 'ja', axis=1, tiled=True)  178 us
    reduce_scatter x1, waiting for transfers between devices, on_device(): lax.psum_scatter(hidden_part.astype(jnp.bfloat16), 'ka', scatter_dimensio...  40.2 us
    all_gather x1, waiting for transfers between devices, on_device(): grad_block = lax.all_gather(grad_hidden, 'ka', axis=1, tiled=True)  27.6 us
    unnamed x6, waiting for transfers between devices  14 us
    dot_general x1, matrix products, on_device(): lax.dot_general(grad_block, weight_block, (((1,), (1,)), ((), ())), prefe...  13.6 us
    all_gather x1, blocking collectives, on_device(): full_rows = lax.all_gather(tokens, 'ia', axis=1, tiled=True)  13.5 us
    dot_general x1, matrix products, on_device(): jnp.dot(full_rows, weight_block, preferred_element_type=jnp.float32)  11.6 us
  transfers between devices with their start and end apart: 5, of which 5 were waited for; matrix products, arithmetic and copies ran while one was open for 2% of the time, Pallas kernels for 0%

commit v1 on v0

v1 whole, which is shorter than its diff:
```python
import jax
import jax.numpy as jnp
from jax import lax
from jax.sharding import PartitionSpec as P

coef_root = 0.7978845608028654
coef_cube = 0.044715
bf16, f32 = jnp.bfloat16, jnp.float32

N_X, N_Z = 4, 4


def gelu_pair(hidden):
    tanh_value = jnp.tanh(coef_root * (hidden + coef_cube * hidden * hidden * hidden))
    activ = 0.5 * hidden * (1.0 + tanh_value)
    derivative = 0.5 * (1.0 + tanh_value) + 0.5 * hidden * (
        1.0 - tanh_value * tanh_value
    ) * coef_root * (1.0 + 3.0 * coef_cube * hidden * hidden)
    return (activ, derivative)


def from_x(v, r):
    return lax.ppermute(v, "ia", [((i + r) % N_X, i) for i in range(N_X)])


def to_x(v, r):
    return from_x(v, N_X - r)


def from_z(v, r):
    return lax.ppermute(
        v, "ja", [(y * N_Z + (z + r) % N_Z, y * N_Z + z) for y in range(2) for z in range(N_Z)]
    )


def to_z(v, r):
    return from_z(v, N_Z - r)


def swap_y_lo(v):
    return lax.ppermute(v, "ja", [(j, (j + N_Z) % (2 * N_Z)) for j in range(2 * N_Z)])


def swap_y_hi(v):
    return lax.ppermute(v, "ka", [(k, (k + 2) % 4) for k in range(4)])


def swap_core(v):
    return lax.ppermute(v, "ka", [(k, k ^ 1) for k in range(4)])


def exchange_pairs(slot):
    pairs = []
    for y_lo in range(2):
        for z in range(N_Z):
            for y_hi in range(2):
                for core in range(2):
                    half = (z + slot) % 2
                    to_z_index = 2 * core + half
                    to_y_lo, to_y_hi = y_hi, y_hi ^ y_lo
                    to_core = ((z - to_z_index) % N_Z) // 2
                    pairs.append(
                        (
                            (y_lo * N_Z + z) * 4 + y_hi * 2 + core,
                            (to_y_lo * N_Z + to_z_index) * 4 + to_y_hi * 2 + to_core,
                        )
                    )
    return pairs


def dot(a, b, dims=(1, 0)):
    return lax.dot_general(
        a, b, (((dims[0],), (dims[1],)), ((), ())), preferred_element_type=f32
    )


def on_device(tokens, weight, grad_out):
    rows, cols = tokens.shape
    half = rows // 2
    units = weight.shape[1]
    x = lax.axis_index("ia")
    z = lax.axis_index("ja") % N_Z
    y_hi, core = lax.axis_index("ka") // 2, lax.axis_index("ka") % 2

    other = swap_y_lo(tokens)
    tok_a = jnp.concatenate([tokens[:half], other[:half]], 0)
    tok_b = jnp.concatenate([tokens[half:], other[half:]], 0)
    a_x = [tok_a] + [from_x(tok_a, r) for r in (1, 2, 3)]
    b_z = [tok_b] + [from_z(tok_b, r) for r in (1, 2, 3)]
    tok_a = jnp.concatenate(a_x, 1)
    tok_b = jnp.concatenate(b_z, 0)
    a_z = [tok_a] + [from_z(tok_a, r) for r in (1, 2, 3)]
    b_x = [tok_b] + [from_x(tok_b, r) for r in (1, 2, 3)]
    tok_a = jnp.concatenate(a_z, 0)
    tok_b = jnp.concatenate(b_x, 1)

    sent = []
    for slot in range(2):
        start = ((z + slot) % 2) * units
        piece = lax.dynamic_slice_in_dim(grad_out, start, units, 1)
        sent.append(lax.ppermute(piece, ("ja", "ka"), exchange_pairs(slot)))

    turned = jnp.concatenate(
        [lax.dynamic_slice_in_dim(weight, ((x + r) % N_X) * cols, cols, 0) for r in range(N_X)], 0
    )

    def middle(tok, go):
        pair = tok.shape[0] // 2
        away = lax.dynamic_slice_in_dim(tok, (1 - core) * pair, pair, 0)
        keep = lax.dynamic_slice_in_dim(tok, core * pair, pair, 0)
        got = swap_core(dot(away, turned).astype(bf16))
        summed = (dot(keep, turned) + got.astype(f32)).reshape(2, 2, half, units)
        away = lax.dynamic_slice_in_dim(summed, 1 - y_hi, 1, 1)[:, 0]
        keep = lax.dynamic_slice_in_dim(summed, y_hi, 1, 1)[:, 0]
        hidden = keep + swap_y_hi(away.astype(bf16)).astype(f32)
        activ, derivative = gelu_pair(hidden)
        grad = (go.astype(f32) * derivative).astype(bf16)
        there = swap_y_hi(grad)
        first = jnp.where(y_hi == 0, grad, there)
        second = jnp.where(y_hi == 0, there, grad)
        grad = jnp.stack([first, second], 1).reshape(pair, units)
        there = swap_core(grad)
        first = jnp.where(core == 0, grad, there)
        second = jnp.where(core == 0, there, grad)
        return activ.astype(bf16), jnp.concatenate([first, second], 0)

    act_a, grad_a = middle(tok_a, jnp.stack([s[:half] for s in sent]))
    act_b, grad_b = middle(tok_b, jnp.stack([s[half:] for s in sent]))

    back = []
    for slot in range(2):
        piece = jnp.concatenate([act_a[slot], act_b[slot]], 0)
        back.append(
            lax.ppermute(piece, ("ja", "ka"), [(t, s) for s, t in exchange_pairs(slot)])
        )
    even = z % 2 == 0
    activated = jnp.concatenate(
        [jnp.where(even, back[0], back[1]), jnp.where(even, back[1], back[0])], 1
    )

    def split_sum(parts, send):
        got = [send(parts[r].astype(bf16), r) for r in (2, 1, 3)]
        total = parts[0]
        for g in got:
            total = total + g.astype(f32)
        return total

    n = grad_a.shape[0] // N_Z
    part_a = split_sum(
        [dot(grad_a[r * n : (r + 1) * n], turned, (1, 1)) for r in range(N_Z)], to_z
    )
    part_b = split_sum(
        [dot(grad_b, turned[r * cols : (r + 1) * cols], (1, 1)) for r in range(N_X)], to_x
    )
    part_a = split_sum([part_a[:, r * cols : (r + 1) * cols] for r in range(N_X)], to_x)
    part_b = split_sum([part_b[r * n : (r + 1) * n] for r in range(N_Z)], to_z)
    got = swap_y_lo(jnp.concatenate([part_a[half:], part_b[half:]], 0).astype(bf16))
    grad_input = jnp.concatenate([part_a[:half], part_b[:half]], 0) + got.astype(f32)

    grad_weight = jnp.zeros_like(weight)
    for r in range(N_X):
        block = dot(tok_a[:, r * cols : (r + 1) * cols], grad_a, (0, 0)) + dot(
            tok_b[:, r * cols : (r + 1) * cols], grad_b, (0, 0)
        )
        grad_weight = lax.dynamic_update_slice_in_dim(
            grad_weight, block.astype(bf16), ((x + r) % N_X) * cols, 0
        )
    return (activated, grad_input.astype(bf16), grad_weight)


def solution(mesh):
    placed = (P("ja", ("ka", "ia")), P("ka", ("ia", "ja")), P("ja", ("ia", "ka")))
    return jax.shard_map(
        on_device,
        mesh=mesh,
        in_specs=placed,
        out_specs=(P("ja", ("ia", "ka")), P("ja", ("ka", "ia")), P("ka", ("ia", "ja"))),
        check_vma=False,
    )
```

time: 526 us -> 197 us (0.37)
  waiting for transfers between devices: 449 us -> 99.2 us
  starting transfers between devices: 0.38 us -> 60.6 us
  matrix products: 34.5 us -> 20 us
  blocking collectives: 13.5 us -> 0 us
  between operations: 13.8 us -> 1.21 us
  other arithmetic: 2.96 us -> 9.51 us
    reduce_scatter x2 -> x0, waiting for transfers between devices: 230 us -> none  [the longest x1 189 us: on_device(): lax.psum_scatter(weight_term, 'ja', scatter_dimension=1, tiled=True)]
    all_gather x2 -> x0, waiting for transfers between devices: 206 us -> none  [the longest x1 178 us: on_device(): weight_block = lax.all_gather(weight, 'ja', axis=1, tiled=True)]
    ppermute x0 -> x38, waiting for transfers between devices: none -> 99.2 us  [the longest x12 34.7 us: from_x(): return lax.ppermute(v, 'ia', [((i + r) % N_X, i) for i in range(N_X)])]
    ppermute x0 -> x38, starting transfers between devices: none -> 60.6 us  [the longest x12 23.9 us: from_x(): return lax.ppermute(v, 'ia', [((i + r) % N_X, i) for i in range(N_X)])]
    dot_general x3 -> x20, matrix products: 34.5 us -> 20 us  [dot(): lax.dot_general(a, b, (((dims[0],), (dims[1],)), ((), ())), preferred_ele...]
    unnamed x6 -> x0, waiting for transfers between devices: 14 us -> none
    all_gather x1 -> x0, blocking collectives: 13.5 us -> none  [on_device(): full_rows = lax.all_gather(tokens, 'ia', axis=1, tiled=True)]
    concatenate x0 -> x9, other arithmetic: none -> 7.23 us  [the longest x1 3.29 us: on_device(): tok_a = jnp.concatenate(a_z, 0)]
  transfers between devices with their start and end apart: 5 -> 38, of which waited for: 5 -> 16; matrix products, arithmetic and copies ran while one was open for 2% -> 16% of each run, Pallas kernels for 0% -> 0%
where the time goes in v1:
time: 197 us
  waiting for transfers between devices  99.2 us (50%)
  starting transfers between devices  60.6 us (31%)
  matrix products  20 us (10%)
  other arithmetic  9.51 us (5%)
  local copies, waits for them, and re-layouts  6.07 us (3%)
    ppermute x12, waiting for transfers between devices, from_x(): return lax.ppermute(v, 'ia', [((i + r) % N_X, i) for i in range(N_X)])  34.7 us
    ppermute x4, waiting for transfers between devices, swap_y_hi(): return lax.ppermute(v, 'ka', [(k, (k + 2) % 4) for k in range(4)])  30.8 us
    ppermute x12, waiting for transfers between devices, from_z(): lax.ppermute(v, 'ja', [(y * N_Z + (z + r) % N_Z, y * N_Z + z) for y in ra...  25.1 us
    ppermute x12, starting transfers between devices, from_x(): return lax.ppermute(v, 'ia', [((i + r) % N_X, i) for i in range(N_X)])  23.9 us
    dot_general x20, matrix products, dot(): lax.dot_general(a, b, (((dims[0],), (dims[1],)), ((), ())), preferred_ele...  20 us
    ppermute x12, starting transfers between devices, from_z(): lax.ppermute(v, 'ja', [(y * N_Z + (z + r) % N_Z, y * N_Z + z) for y in ra...  18.9 us
    ppermute x2, waiting for transfers between devices, swap_y_lo(): lax.ppermute(v, 'ja', [(j, (j + N_Z) % (2 * N_Z)) for j in range(2 * N_Z)])  8.62 us
    ppermute x2, starting transfers between devices, on_device(): sent.append(lax.ppermute(piece, ('ja', 'ka'), exchange_pairs(slot)))  7.57 us
  transfers between devices with their start and end apart: 38, of which 16 were waited for; matrix products, arithmetic and copies ran while one was open for 16% of the time, Pallas kernels for 0%

profile of v1, /device:TPU:40, one launch (start us, length us, event | category | flops | bytes accessed | tf_op | source)
XLA Modules:
  0.0 196.6 jit_solution(2550328593303774809)
XLA Ops:
  1.2 1.1 fusion.55
  2.3 4.2 %collective-permute-done = bf16[192,384]{1,0:T(8,128)(2,1)S(1)} collective-permute-done((bf16[192,384]{1,0:T(8,128)(2,1)}, bf16[192,384]{1,0:T(8,128)(2,1)S(1)}, u32[]{:S(2)}, u32[]{:S(2)}) %collective-permute-start) | collective-permute-done | bytes 147488 | tf_op jit(solution)/shard_map/ppermute | solution.py:41
  7.3 1.9 constant_dynamic-slice_fusion.1
  9.2 5.0 %collective-permute-start.20 = (bf16[192,768]{1,0:T(8,128)(2,1)}, bf16[192,768]{1,0:T(8,128)(2,1)}, u32[]{:S(2)}, u32[]{:S(2)}) collective-permute-start(bf16[192,768]{1,0:T(8,128)(2,1)} %get-tuple-element.26), channel_id=1, source_target_pairs={{0,5},{1,12},{2,23},{3,30},{4,0},{5,9},{6,18},{7,27},{8,4},{9,13},... | collective-permute-start | bytes 884744 | tf_op jit(solution)/shard_map/ppermute | solution.py:101
  15.4 1.5 collective-permute-start.3
  16.9 2.7 %collective-permute-start.2 = (bf16[192,384]{1,0:T(8,128)(2,1)}, bf16[192,384]{1,0:T(8,128)(2,1)S(1)}, u32[]{:S(2)}, u32[]{:S(2)}) collective-permute-start(bf16[192,384]{1,0:T(8,128)(2,1)} %pad_maximum_fusion.11), channel_id=1, source_target_pairs={{64,0},{96,32},{0,64},{32,96},{65,1},{97,33},{1,65},{33,97},{66,2}... | collective-permute-start | bytes 442376 | tf_op jit(solution)/shard_map/ppermute | solution.py:23
  19.7 2.5 %collective-permute-done.10 = bf16[192,384]{1,0:T(8,128)(2,1)S(1)} collective-permute-done((bf16[192,384]{1,0:T(8,128)(2,1)}, bf16[192,384]{1,0:T(8,128)(2,1)S(1)}, u32[]{:S(2)}, u32[]{:S(2)}) %collective-permute-start.10) | collective-permute-done | bytes 147488 | tf_op jit(solution)/shard_map/ppermute | solution.py:31
  22.2 2.8 %collective-permute-start.1 = (bf16[192,384]{1,0:T(8,128)(2,1)}, bf16[192,384]{1,0:T(8,128)(2,1)S(1)}, u32[]{:S(2)}, u32[]{:S(2)}) collective-permute-start(bf16[192,384]{1,0:T(8,128)(2,1)} %pad_maximum_fusion.11), channel_id=1, source_target_pairs={{32,0},{64,32},{96,64},{0,96},{33,1},{65,33},{97,65},{1,97},{34,2}... | collective-permute-start | bytes 442376 | tf_op jit(solution)/shard_map/ppermute | solution.py:23
  25.4 1.6 collective-permute-start.14
  26.9 2.7 %collective-permute-start.13 = (bf16[768,384]{1,0:T(8,128)(2,1)S(1)}, bf16[768,384]{1,0:T(8,128)(2,1)}, u32[]{:S(2)}, u32[]{:S(2)}) collective-permute-start(bf16[768,384]{1,0:T(8,128)(2,1)S(1)} %constant_dynamic-update-slice_fusion), channel_id=1, source_target_pairs={{64,0},{96,32},{0,64},{32,96},{65,1},{97,33},{1,65},{33,97},{66,2}... | collective-permute-start | bytes 1769480 | tf_op jit(solution)/shard_map/ppermute | solution.py:23
  29.7 1.4 collective-permute-start.12
  31.1 1.4 constant_dynamic-slice_fusion.5
  32.6 2.5 %collective-permute-start.19 = (bf16[192,768]{1,0:T(8,128)(2,1)}, bf16[192,768]{1,0:T(8,128)(2,1)S(1)}, u32[]{:S(2)}, u32[]{:S(2)}) collective-permute-start(bf16[192,768]{1,0:T(8,128)(2,1)} %get-tuple-element.25), channel_id=1, source_target_pairs={{0,0},{1,9},{2,18},{3,27},{4,4},{5,13},{6,22},{7,31},{8,1},{9,8},{... | collective-permute-start | bytes 884744 | tf_op jit(solution)/shard_map/ppermute | solution.py:101
  35.1 7.2 %collective-permute-start.6 = (bf16[192,1536]{1,0:T(8,128)(2,1)S(1)}, bf16[192,1536]{1,0:T(8,128)(2,1)S(1)}, u32[]{:S(2)}, u32[]{:S(2)}) collective-permute-start(bf16[192,1536]{1,0:T(8,128)(2,1)S(1)} %pad_maximum_fusion.5), channel_id=1, source_target_pairs={{12,0},{0,4},{4,8},{8,12},{28,16},{16,20},{20,24},{24,28},{13,1},{... | collective-permute-start | bytes 1769480 | tf_op jit(solution)/shard_map/ppermute | solution.py:31
  43.4 1.0 collective-permute-start.5
  44.4 11.1 %collective-permute-done.13 = bf16[768,384]{1,0:T(8,128)(2,1)} collective-permute-done((bf16[768,384]{1,0:T(8,128)(2,1)S(1)}, bf16[768,384]{1,0:T(8,128)(2,1)}, u32[]{:S(2)}, u32[]{:S(2)}) %collective-permute-start.13) | collective-permute-done | bytes 589856 | tf_op jit(solution)/shard_map/ppermute | solution.py:23
  55.5 2.8 %collective-permute-start.4 = (bf16[192,1536]{1,0:T(8,128)(2,1)S(1)}, bf16[192,1536]{1,0:T(8,128)(2,1)S(1)}, u32[]{:S(2)}, u32[]{:S(2)}) collective-permute-start(bf16[192,1536]{1,0:T(8,128)(2,1)S(1)} %pad_maximum_fusion.5), channel_id=1, source_target_pairs={{4,0},{8,4},{12,8},{0,12},{20,16},{24,20},{28,24},{16,28},{5,1},{9... | collective-permute-start | bytes 1769480 | tf_op jit(solution)/shard_map/ppermute | solution.py:31
  58.3 1.6 pad_maximum_fusion.2
  60.0 1.1 convolution_convert_fusion.3
  61.2 2.1 %collective-permute-done.5 = bf16[192,1536]{1,0:T(8,128)(2,1)S(1)} collective-permute-done((bf16[192,1536]{1,0:T(8,128)(2,1)S(1)}, bf16[192,1536]{1,0:T(8,128)(2,1)S(1)}, u32[]{:S(2)}, u32[]{:S(2)}) %collective-permute-start.5) | collective-permute-done | bytes 589856 | tf_op jit(solution)/shard_map/ppermute | solution.py:31
  63.3 11.8 %collective-permute-done.4 = bf16[192,1536]{1,0:T(8,128)(2,1)S(1)} collective-permute-done((bf16[192,1536]{1,0:T(8,128)(2,1)S(1)}, bf16[192,1536]{1,0:T(8,128)(2,1)S(1)}, u32[]{:S(2)}, u32[]{:S(2)}) %collective-permute-start.4) | collective-permute-done | bytes 589856 | tf_op jit(solution)/shard_map/ppermute | solution.py:31
  75.2 3.3 %pad_maximum_fusion = bf16[768,1536]{1,0:T(8,128)(2,1)S(1)} fusion(bf16[192,1536]{1,0:T(8,128)(2,1)S(1)} %collective-permute-done.6, bf16[192,1536]{1,0:T(8,128)(2,1)S(1)} %collective-permute-done.5, bf16[192,1536]{1,0:T(8,128)(2,1)S(1)} %collective-permute-done.4, bf16[192,384]{1,0:T(8,128)(2,1)S(1)} %collective-permute-done.3, ...), kind=kLoop, calls=%fused_computation.6 | loop fusion | flops 18874368 | bytes 4718592 | tf_op jit(solution)/shard_map/concatenate | solution.py:94
  78.5 1.1 convolution_convert_fusion.4
  79.7 1.1 convolution_add_fusion.6
  81.9 1.1 convolution_add_fusion.7
  83.0 2.9 %collective-permute-start.8 = (bf16[2,96,768]{2,1,0:T(8,128)(2,1)S(1)}, bf16[2,96,768]{2,1,0:T(8,128)(2,1)S(1)}, u32[]{:S(2)}, u32[]{:S(2)}) collective-permute-start(bf16[2,96,768]{2,1,0:T(8,128)(2,1)S(1)} %fusion.34), channel_id=1, source_target_pairs={{0,2},{1,3},{2,0},{3,1},{4,6},{5,7},{6,4},{7,5},{8,10},{9,11},{10,... | collective-permute-start | bytes 884744 | tf_op jit(solution)/shard_map/ppermute | solution.py:45
  85.9 6.4 %collective-permute-done.16 = bf16[2,96,768]{2,1,0:T(8,128)(2,1)S(1)} collective-permute-done((bf16[2,96,768]{2,1,0:T(8,128)(2,1)S(1)}, bf16[2,96,768]{2,1,0:T(8,128)(2,1)S(1)}, u32[]{:S(2)}, u32[]{:S(2)}) %collective-permute-start.16) | collective-permute-done | bytes 294944 | tf_op jit(solution)/shard_map/ppermute | solution.py:45
  93.7 4.8 %collective-permute-done.8 = bf16[2,96,768]{2,1,0:T(8,128)(2,1)S(1)} collective-permute-done((bf16[2,96,768]{2,1,0:T(8,128)(2,1)S(1)}, bf16[2,96,768]{2,1,0:T(8,128)(2,1)S(1)}, u32[]{:S(2)}, u32[]{:S(2)}) %collective-permute-start.8) | collective-permute-done | bytes 294944 | tf_op jit(solution)/shard_map/ppermute | solution.py:45
  99.1 2.8 %collective-permute-start.17 = (bf16[192,768]{1,0:T(8,128)(2,1)S(1)}, bf16[192,768]{1,0:T(8,128)(2,1)S(1)}, u32[]{:S(2)}, u32[]{:S(2)}) collective-permute-start(bf16[192,768]{1,0:T(8,128)(2,1)S(1)} %pad_maximum_fusion.9), channel_id=1, source_target_pairs={{0,0},{9,1},{18,2},{27,3},{4,4},{13,5},{22,6},{31,7},{1,8},{8,9},{... | collective-permute-start | bytes 884744 | tf_op jit(solution)/shard_map/ppermute | solution.py:134
  102.1 1.5 collective-permute-start.21
  103.6 1.3 collective-permute-done.29
  105.1 18.3 %collective-permute-done.21 = bf16[2,96,768]{2,1,0:T(8,128)(2,1)S(1)} collective-permute-done((bf16[2,96,768]{2,1,0:T(8,128)(2,1)S(1)}, bf16[2,96,768]{2,1,0:T(8,128)(2,1)S(1)}, u32[]{:S(2)}, u32[]{:S(2)}) %collective-permute-start.21) | collective-permute-done | bytes 294944 | tf_op jit(solution)/shard_map/ppermute | solution.py:45
  129.8 4.3 %collective-permute-start.33 = (bf16[768,384]{1,0:T(8,128)(2,1)S(1)}, bf16[768,384]{1,0:T(8,128)(2,1)S(1)}, u32[]{:S(2)}, u32[]{:S(2)}) collective-permute-start(bf16[768,384]{1,0:T(8,128)(2,1)S(1)} %convolution_convert_fusion.5), channel_id=1, source_target_pairs={{32,0},{64,32},{96,64},{0,96},{33,1},{65,33},{97,65},{1,97},{34,2}... | collective-permute-start | bytes 1769480 | tf_op jit(solution)/shard_map/ppermute | solution.py:23
  134.1 1.5 collective-permute-start.31
  136.7 1.9 collective-permute-start.24
  139.5 1.7 fusion.51
  141.9 1.7 fusion.50
  144.4 15.6 %collective-permute-done.33 = bf16[768,384]{1,0:T(8,128)(2,1)S(1)} collective-permute-done((bf16[768,384]{1,0:T(8,128)(2,1)S(1)}, bf16[768,384]{1,0:T(8,128)(2,1)S(1)}, u32[]{:S(2)}, u32[]{:S(2)}) %collective-permute-start.33) | collective-permute-done | bytes 589856 | tf_op jit(solution)/shard_map/ppermute | solution.py:23
  160.0 1.7 fusion.49
  161.7 1.7 collective-permute-done.32
  164.3 1.5 collective-permute-start.36
  166.4 3.1 %collective-permute-start.34 = (bf16[192,384]{1,0:T(8,128)(2,1)S(1)}, bf16[192,384]{1,0:T(8,128)(2,1)S(1)}, u32[]{:S(2)}, u32[]{:S(2)}) collective-permute-start(bf16[192,384]{1,0:T(8,128)(2,1)S(1)} %get-tuple-element.20), channel_id=1, source_target_pairs={{8,0},{12,4},{0,8},{4,12},{24,16},{28,20},{16,24},{20,28},{9,1},{1... | collective-permute-start | bytes 442376 | tf_op jit(solution)/shard_map/ppermute | solution.py:31
  169.5 8.2 %collective-permute-done.23 = bf16[192,1536]{1,0:T(8,128)(2,1)S(1)} collective-permute-done((bf16[192,1536]{1,0:T(8,128)(2,1)S(1)}, bf16[192,1536]{1,0:T(8,128)(2,1)S(1)}, u32[]{:S(2)}, u32[]{:S(2)}) %collective-permute-start.23) | collective-permute-done | bytes 589856 | tf_op jit(solution)/shard_map/ppermute | solution.py:31
  178.8 3.8 %collective-permute-start.28 = (bf16[192,384]{1,0:T(8,128)(2,1)S(1)}, bf16[192,384]{1,0:T(8,128)(2,1)S(1)}, u32[]{:S(2)}, u32[]{:S(2)}) collective-permute-start(bf16[192,384]{1,0:T(8,128)(2,1)S(1)} %get-tuple-element.16), channel_id=1, source_target_pairs={{32,0},{64,32},{96,64},{0,96},{33,1},{65,33},{97,65},{1,97},{34,2}... | collective-permute-start | bytes 442376 | tf_op jit(solution)/shard_map/ppermute | solution.py:23
  182.6 1.5 collective-permute-start.26
  184.2 2.6 %collective-permute-done.28 = bf16[192,384]{1,0:T(8,128)(2,1)S(1)} collective-permute-done((bf16[192,384]{1,0:T(8,128)(2,1)S(1)}, bf16[192,384]{1,0:T(8,128)(2,1)S(1)}, u32[]{:S(2)}, u32[]{:S(2)}) %collective-permute-start.28) | collective-permute-done | bytes 147488 | tf_op jit(solution)/shard_map/ppermute | solution.py:23
  186.9 3.7 %collective-permute-done.27 = bf16[192,384]{1,0:T(8,128)(2,1)S(1)} collective-permute-done((bf16[192,384]{1,0:T(8,128)(2,1)S(1)}, bf16[192,384]{1,0:T(8,128)(2,1)S(1)}, u32[]{:S(2)}, u32[]{:S(2)}) %collective-permute-start.27) | collective-permute-done | bytes 147488 | tf_op jit(solution)/shard_map/ppermute | solution.py:23
  191.5 4.4 %collective-permute-done.37 = bf16[192,384]{1,0:T(8,128)(2,1)S(1)} collective-permute-done((bf16[192,384]{1,0:T(8,128)(2,1)S(1)}, bf16[192,384]{1,0:T(8,128)(2,1)S(1)}, u32[]{:S(2)}, u32[]{:S(2)}) %collective-permute-start.37) | collective-permute-done | bytes 147488 | tf_op jit(solution)/shard_map/ppermute | solution.py:41
  (102 shorter events, 21.5 us)
Async XLA Ops:
  0.6 30.5 %copy-start.1 = (bf16[1536,768]{1,0:T(8,128)(2,1)S(1)}, bf16[1536,768]{1,0:T(8,128)(2,1)}, u32[]{:S(2)}) copy-start(bf16[1536,768]{1,0:T(8,128)(2,1)} %param.4) | copy-start | bytes 7077892
  0.6 5.9 %collective-permute-start = (bf16[192,384]{1,0:T(8,128)(2,1)}, bf16[192,384]{1,0:T(8,128)(2,1)S(1)}, u32[]{:S(2)}, u32[]{:S(2)}) collective-permute-start(bf16[192,384]{1,0:T(8,128)(2,1)} %param.3), channel_id=1, source_target_pairs={{0,16},{4,20},{8,24},{12,28},{16,0},{20,4},{24,8},{28,12},{1,17},{... | collective-permute-start | bytes 442376 | tf_op jit(solution)/shard_map/ppermute | solution.py:41
  7.2 9.7 %collective-permute-start.9 = (bf16[192,384]{1,0:T(8,128)(2,1)}, bf16[192,384]{1,0:T(8,128)(2,1)S(1)}, u32[]{:S(2)}, u32[]{:S(2)}) collective-permute-start(bf16[192,384]{1,0:T(8,128)(2,1)} %pad_maximum_fusion.12), channel_id=1, source_target_pairs={{4,0},{8,4},{12,8},{0,12},{20,16},{24,20},{28,24},{16,28},{5,1},{9... | collective-permute-start | bytes 442376 | tf_op jit(solution)/shard_map/ppermute | solution.py:31
  9.2 25.9 %collective-permute-start.20 = (bf16[192,768]{1,0:T(8,128)(2,1)}, bf16[192,768]{1,0:T(8,128)(2,1)}, u32[]{:S(2)}, u32[]{:S(2)}) collective-permute-start(bf16[192,768]{1,0:T(8,128)(2,1)} %get-tuple-element.26), channel_id=1, source_target_pairs={{0,5},{1,12},{2,23},{3,30},{4,0},{5,9},{6,18},{7,27},{8,4},{9,13},... | collective-permute-start | bytes 884744 | tf_op jit(solution)/shard_map/ppermute | solution.py:101
  14.3 7.9 %collective-permute-start.10 = (bf16[192,384]{1,0:T(8,128)(2,1)}, bf16[192,384]{1,0:T(8,128)(2,1)S(1)}, u32[]{:S(2)}, u32[]{:S(2)}) collective-permute-start(bf16[192,384]{1,0:T(8,128)(2,1)} %pad_maximum_fusion.12), channel_id=1, source_target_pairs={{8,0},{12,4},{0,8},{4,12},{24,16},{28,20},{16,24},{20,28},{9,1},{1... | collective-permute-start | bytes 442376 | tf_op jit(solution)/shard_map/ppermute | solution.py:31
  14.6 10.7 %collective-permute-start.11 = (bf16[192,384]{1,0:T(8,128)(2,1)}, bf16[192,384]{1,0:T(8,128)(2,1)S(1)}, u32[]{:S(2)}, u32[]{:S(2)}) collective-permute-start(bf16[192,384]{1,0:T(8,128)(2,1)} %pad_maximum_fusion.12), channel_id=1, source_target_pairs={{12,0},{0,4},{4,8},{8,12},{28,16},{16,20},{20,24},{24,28},{13,1},{... | collective-permute-start | bytes 442376 | tf_op jit(solution)/shard_map/ppermute | solution.py:31
  15.4 11.5 %collective-permute-start.3 = (bf16[192,384]{1,0:T(8,128)(2,1)}, bf16[192,384]{1,0:T(8,128)(2,1)S(1)}, u32[]{:S(2)}, u32[]{:S(2)}) collective-permute-start(bf16[192,384]{1,0:T(8,128)(2,1)} %pad_maximum_fusion.11), channel_id=1, source_target_pairs={{96,0},{0,32},{32,64},{64,96},{97,1},{1,33},{33,65},{65,97},{98,2}... | collective-permute-start | bytes 442376 | tf_op jit(solution)/shard_map/ppermute | solution.py:23
  16.9 12.8 %collective-permute-start.2 = (bf16[192,384]{1,0:T(8,128)(2,1)}, bf16[192,384]{1,0:T(8,128)(2,1)S(1)}, u32[]{:S(2)}, u32[]{:S(2)}) collective-permute-start(bf16[192,384]{1,0:T(8,128)(2,1)} %pad_maximum_fusion.11), channel_id=1, source_target_pairs={{64,0},{96,32},{0,64},{32,96},{65,1},{97,33},{1,65},{33,97},{66,2}... | collective-permute-start | bytes 442376 | tf_op jit(solution)/shard_map/ppermute | solution.py:23
  22.2 10.4 %collective-permute-start.1 = (bf16[192,384]{1,0:T(8,128)(2,1)}, bf16[192,384]{1,0:T(8,128)(2,1)S(1)}, u32[]{:S(2)}, u32[]{:S(2)}) collective-permute-start(bf16[192,384]{1,0:T(8,128)(2,1)} %pad_maximum_fusion.11), channel_id=1, source_target_pairs={{32,0},{64,32},{96,64},{0,96},{33,1},{65,33},{97,65},{1,97},{34,2}... | collective-permute-start | bytes 442376 | tf_op jit(solution)/shard_map/ppermute | solution.py:23
  25.4 18.0 %collective-permute-start.14 = (bf16[768,384]{1,0:T(8,128)(2,1)S(1)}, bf16[768,384]{1,0:T(8,128)(2,1)}, u32[]{:S(2)}, u32[]{:S(2)}) collective-permute-start(bf16[768,384]{1,0:T(8,128)(2,1)S(1)} %constant_dynamic-update-slice_fusion), channel_id=1, source_target_pairs={{96,0},{0,32},{32,64},{64,96},{97,1},{1,33},{33,65},{65,97},{98,2}... | collective-permute-start | bytes 1769480 | tf_op jit(solution)/shard_map/ppermute | solution.py:23
  26.9 28.6 %collective-permute-start.13 = (bf16[768,384]{1,0:T(8,128)(2,1)S(1)}, bf16[768,384]{1,0:T(8,128)(2,1)}, u32[]{:S(2)}, u32[]{:S(2)}) collective-permute-start(bf16[768,384]{1,0:T(8,128)(2,1)S(1)} %constant_dynamic-update-slice_fusion), channel_id=1, source_target_pairs={{64,0},{96,32},{0,64},{32,96},{65,1},{97,33},{1,65},{33,97},{66,2}... | collective-permute-start | bytes 1769480 | tf_op jit(solution)/shard_map/ppermute | solution.py:23
  29.7 28.7 %collective-permute-start.12 = (bf16[768,384]{1,0:T(8,128)(2,1)S(1)}, bf16[768,384]{1,0:T(8,128)(2,1)}, u32[]{:S(2)}, u32[]{:S(2)}) collective-permute-start(bf16[768,384]{1,0:T(8,128)(2,1)S(1)} %constant_dynamic-update-slice_fusion), channel_id=1, source_target_pairs={{32,0},{64,32},{96,64},{0,96},{33,1},{65,33},{97,65},{1,97},{34,2}... | collective-permute-start | bytes 1769480 | tf_op jit(solution)/shard_map/ppermute | solution.py:23
  32.6 47.1 %collective-permute-start.19 = (bf16[192,768]{1,0:T(8,128)(2,1)}, bf16[192,768]{1,0:T(8,128)(2,1)S(1)}, u32[]{:S(2)}, u32[]{:S(2)}) collective-permute-start(bf16[192,768]{1,0:T(8,128)(2,1)} %get-tuple-element.25), channel_id=1, source_target_pairs={{0,0},{1,9},{2,18},{3,27},{4,4},{5,13},{6,22},{7,31},{8,1},{9,8},{... | collective-permute-start | bytes 884744 | tf_op jit(solution)/shard_map/ppermute | solution.py:101
  35.1 26.0 %collective-permute-start.6 = (bf16[192,1536]{1,0:T(8,128)(2,1)S(1)}, bf16[192,1536]{1,0:T(8,128)(2,1)S(1)}, u32[]{:S(2)}, u32[]{:S(2)}) collective-permute-start(bf16[192,1536]{1,0:T(8,128)(2,1)S(1)} %pad_maximum_fusion.5), channel_id=1, source_target_pairs={{12,0},{0,4},{4,8},{8,12},{28,16},{16,20},{20,24},{24,28},{13,1},{... | collective-permute-start | bytes 1769480 | tf_op jit(solution)/shard_map/ppermute | solution.py:31
  43.3 16.6 %copy-start.2 = (bf16[384,768]{1,0:T(8,128)(2,1)S(1)}, bf16[384,768]{1,0:T(8,128)(2,1)}, u32[]{:S(2)}) copy-start(bf16[384,768]{1,0:T(8,128)(2,1)} %get-tuple-element.3) | copy-start | bytes 1769476
  43.3 16.6 %copy-start.3 = (bf16[384,768]{1,0:T(8,128)(2,1)S(1)}, bf16[384,768]{1,0:T(8,128)(2,1)}, u32[]{:S(2)}) copy-start(bf16[384,768]{1,0:T(8,128)(2,1)} %get-tuple-element.4) | copy-start | bytes 1769476
  43.3 16.6 %copy-start.4 = (bf16[384,768]{1,0:T(8,128)(2,1)S(1)}, bf16[384,768]{1,0:T(8,128)(2,1)}, u32[]{:S(2)}) copy-start(bf16[384,768]{1,0:T(8,128)(2,1)} %get-tuple-element.5) | copy-start | bytes 1769476
  43.4 16.6 %copy-start.5 = (bf16[384,768]{1,0:T(8,128)(2,1)S(1)}, bf16[384,768]{1,0:T(8,128)(2,1)}, u32[]{:S(2)}) copy-start(bf16[384,768]{1,0:T(8,128)(2,1)} %get-tuple-element.6) | copy-start | bytes 1769476
  43.4 20.0 %collective-permute-start.5 = (bf16[192,1536]{1,0:T(8,128)(2,1)S(1)}, bf16[192,1536]{1,0:T(8,128)(2,1)S(1)}, u32[]{:S(2)}, u32[]{:S(2)}) collective-permute-start(bf16[192,1536]{1,0:T(8,128)(2,1)S(1)} %pad_maximum_fusion.5), channel_id=1, source_target_pairs={{8,0},{12,4},{0,8},{4,12},{24,16},{28,20},{16,24},{20,28},{9,1},{1... | collective-permute-start | bytes 1769480 | tf_op jit(solution)/shard_map/ppermute | solution.py:31
  55.5 19.7 %collective-permute-start.4 = (bf16[192,1536]{1,0:T(8,128)(2,1)S(1)}, bf16[192,1536]{1,0:T(8,128)(2,1)S(1)}, u32[]{:S(2)}, u32[]{:S(2)}) collective-permute-start(bf16[192,1536]{1,0:T(8,128)(2,1)S(1)} %pad_maximum_fusion.5), channel_id=1, source_target_pairs={{4,0},{8,4},{12,8},{0,12},{20,16},{24,20},{28,24},{16,28},{5,1},{9... | collective-permute-start | bytes 1769480 | tf_op jit(solution)/shard_map/ppermute | solution.py:31
  61.1 18.6 %collective-permute-start.15 = (bf16[384,768]{1,0:T(8,128)(2,1)S(1)}, bf16[384,768]{1,0:T(8,128)(2,1)S(1)}, u32[]{:S(2)}, u32[]{:S(2)}) collective-permute-start(bf16[384,768]{1,0:T(8,128)(2,1)S(1)} %convolution_convert_fusion.3), channel_id=1, source_target_pairs={{0,1},{1,0},{2,3},{3,2},{4,5},{5,4},{6,7},{7,6},{8,9},{9,8},{10,11... | collective-permute-start | bytes 1769480 | tf_op jit(solution)/shard_map/ppermute | solution.py:49
  79.6 2.3 %collective-permute-start.7 = (bf16[384,768]{1,0:T(8,128)(2,1)S(1)}, bf16[384,768]{1,0:T(8,128)(2,1)S(1)}, u32[]{:S(2)}, u32[]{:S(2)}) collective-permute-start(bf16[384,768]{1,0:T(8,128)(2,1)S(1)} %convolution_convert_fusion.4), channel_id=1, source_target_pairs={{0,1},{1,0},{2,3},{3,2},{4,5},{5,4},{6,7},{7,6},{8,9},{9,8},{10,11... | collective-permute-start | bytes 1769480 | tf_op jit(solution)/shard_map/ppermute | solution.py:49
  80.8 11.4 %collective-permute-start.16 = (bf16[2,96,768]{2,1,0:T(8,128)(2,1)S(1)}, bf16[2,96,768]{2,1,0:T(8,128)(2,1)S(1)}, u32[]{:S(2)}, u32[]{:S(2)}) collective-permute-start(bf16[2,96,768]{2,1,0:T(8,128)(2,1)S(1)} %fusion.35), channel_id=1, source_target_pairs={{0,2},{1,3},{2,0},{3,1},{4,6},{5,7},{6,4},{7,5},{8,10},{9,11},{10,... | collective-permute-start | bytes 884744 | tf_op jit(solution)/shard_map/ppermute | solution.py:45
  83.0 15.6 %collective-permute-start.8 = (bf16[2,96,768]{2,1,0:T(8,128)(2,1)S(1)}, bf16[2,96,768]{2,1,0:T(8,128)(2,1)S(1)}, u32[]{:S(2)}, u32[]{:S(2)}) collective-permute-start(bf16[2,96,768]{2,1,0:T(8,128)(2,1)S(1)} %fusion.34), channel_id=1, source_target_pairs={{0,2},{1,3},{2,0},{3,1},{4,6},{5,7},{6,4},{7,5},{8,10},{9,11},{10,... | collective-permute-start | bytes 884744 | tf_op jit(solution)/shard_map/ppermute | solution.py:45
  92.7 12.2 %collective-permute-start.29 = (bf16[2,96,768]{2,1,0:T(8,128)(2,1)S(1)}, bf16[2,96,768]{2,1,0:T(8,128)(2,1)S(1)}, u32[]{:S(2)}, u32[]{:S(2)}) collective-permute-start(bf16[2,96,768]{2,1,0:T(8,128)(2,1)S(1)} %get-tuple-element.9), channel_id=1, source_target_pairs={{0,2},{1,3},{2,0},{3,1},{4,6},{5,7},{6,4},{7,5},{8,10},{9,11},{10,... | collective-permute-start | bytes 884744 | tf_op jit(solution)/shard_map/ppermute | solution.py:45
  99.1 24.5 %collective-permute-start.17 = (bf16[192,768]{1,0:T(8,128)(2,1)S(1)}, bf16[192,768]{1,0:T(8,128)(2,1)S(1)}, u32[]{:S(2)}, u32[]{:S(2)}) collective-permute-start(bf16[192,768]{1,0:T(8,128)(2,1)S(1)} %pad_maximum_fusion.9), channel_id=1, source_target_pairs={{0,0},{9,1},{18,2},{27,3},{4,4},{13,5},{22,6},{31,7},{1,8},{8,9},{... | collective-permute-start | bytes 884744 | tf_op jit(solution)/shard_map/ppermute | solution.py:134
  102.0 21.7 %collective-permute-start.18 = (bf16[192,768]{1,0:T(8,128)(2,1)S(1)}, bf16[192,768]{1,0:T(8,128)(2,1)S(1)}, u32[]{:S(2)}, u32[]{:S(2)}) collective-permute-start(bf16[192,768]{1,0:T(8,128)(2,1)S(1)} %pad_maximum_fusion.10), channel_id=1, source_target_pairs={{5,0},{12,1},{23,2},{30,3},{0,4},{9,5},{18,6},{27,7},{4,8},{13,9},... | collective-permute-start | bytes 884744 | tf_op jit(solution)/shard_map/ppermute | solution.py:134
  102.1 21.4 %collective-permute-start.21 = (bf16[2,96,768]{2,1,0:T(8,128)(2,1)S(1)}, bf16[2,96,768]{2,1,0:T(8,128)(2,1)S(1)}, u32[]{:S(2)}, u32[]{:S(2)}) collective-permute-start(bf16[2,96,768]{2,1,0:T(8,128)(2,1)S(1)} %get-tuple-element.7), channel_id=1, source_target_pairs={{0,2},{1,3},{2,0},{3,1},{4,6},{5,7},{6,4},{7,5},{8,10},{9,11},{10,... | collective-permute-start | bytes 884744 | tf_op jit(solution)/shard_map/ppermute | solution.py:45
  105.0 19.5 %collective-permute-start.30 = (bf16[384,768]{1,0:T(8,128)(2,1)S(1)}, bf16[384,768]{1,0:T(8,128)(2,1)S(1)}, u32[]{:S(2)}, u32[]{:S(2)}) collective-permute-start(bf16[384,768]{1,0:T(8,128)(2,1)S(1)} %bitcast.66), channel_id=1, source_target_pairs={{0,1},{1,0},{2,3},{3,2},{4,5},{5,4},{6,7},{7,6},{8,9},{9,8},{10,11... | collective-permute-start | bytes 1769480 | tf_op jit(solution)/shard_map/ppermute | solution.py:49
  123.5 3.6 %collective-permute-start.22 = (bf16[384,768]{1,0:T(8,128)(2,1)S(1)}, bf16[384,768]{1,0:T(8,128)(2,1)S(1)}, u32[]{:S(2)}, u32[]{:S(2)}) collective-permute-start(bf16[384,768]{1,0:T(8,128)(2,1)S(1)} %bitcast.67), channel_id=1, source_target_pairs={{0,1},{1,0},{2,3},{3,2},{4,5},{5,4},{6,7},{7,6},{8,9},{9,8},{10,11... | collective-permute-start | bytes 1769480 | tf_op jit(solution)/shard_map/ppermute | solution.py:49
  129.8 30.2 %collective-permute-start.33 = (bf16[768,384]{1,0:T(8,128)(2,1)S(1)}, bf16[768,384]{1,0:T(8,128)(2,1)S(1)}, u32[]{:S(2)}, u32[]{:S(2)}) collective-permute-start(bf16[768,384]{1,0:T(8,128)(2,1)S(1)} %convolution_convert_fusion.5), channel_id=1, source_target_pairs={{32,0},{64,32},{96,64},{0,96},{33,1},{65,33},{97,65},{1,97},{34,2}... | collective-permute-start | bytes 1769480 | tf_op jit(solution)/shard_map/ppermute | solution.py:23
  134.1 29.3 %collective-permute-start.32 = (bf16[768,384]{1,0:T(8,128)(2,1)S(1)}, bf16[768,384]{1,0:T(8,128)(2,1)S(1)}, u32[]{:S(2)}, u32[]{:S(2)}) collective-permute-start(bf16[768,384]{1,0:T(8,128)(2,1)S(1)} %convolution_convert_fusion.6), channel_id=1, source_target_pairs={{96,0},{0,32},{32,64},{64,96},{97,1},{1,33},{33,65},{65,97},{98,2}... | collective-permute-start | bytes 1769480 | tf_op jit(solution)/shard_map/ppermute | solution.py:23
  134.1 29.3 %collective-permute-start.31 = (bf16[768,384]{1,0:T(8,128)(2,1)S(1)}, bf16[768,384]{1,0:T(8,128)(2,1)S(1)}, u32[]{:S(2)}, u32[]{:S(2)}) collective-permute-start(bf16[768,384]{1,0:T(8,128)(2,1)S(1)} %convolution_convert_fusion.7), channel_id=1, source_target_pairs={{64,0},{96,32},{0,64},{32,96},{65,1},{97,33},{1,65},{33,97},{66,2}... | collective-permute-start | bytes 1769480 | tf_op jit(solution)/shard_map/ppermute | solution.py:23
  135.6 30.8 %collective-permute-start.25 = (bf16[192,1536]{1,0:T(8,128)(2,1)S(1)}, bf16[192,1536]{1,0:T(8,128)(2,1)S(1)}, u32[]{:S(2)}, u32[]{:S(2)}) collective-permute-start(bf16[192,1536]{1,0:T(8,128)(2,1)S(1)} %convolution_convert_fusion), channel_id=1, source_target_pairs={{4,0},{8,4},{12,8},{0,12},{20,16},{24,20},{28,24},{16,28},{5,1},{9... | collective-permute-start | bytes 1769480 | tf_op jit(solution)/shard_map/ppermute | solution.py:31
  136.7 32.8 %collective-permute-start.24 = (bf16[192,1536]{1,0:T(8,128)(2,1)S(1)}, bf16[192,1536]{1,0:T(8,128)(2,1)S(1)}, u32[]{:S(2)}, u32[]{:S(2)}) collective-permute-start(bf16[192,1536]{1,0:T(8,128)(2,1)S(1)} %convolution_convert_fusion.1), channel_id=1, source_target_pairs={{12,0},{0,4},{4,8},{8,12},{28,16},{16,20},{20,24},{24,28},{13,1},{... | collective-permute-start | bytes 1769480 | tf_op jit(solution)/shard_map/ppermute | solution.py:31
  160.0 17.8 %collective-permute-start.23 = (bf16[192,1536]{1,0:T(8,128)(2,1)S(1)}, bf16[192,1536]{1,0:T(8,128)(2,1)S(1)}, u32[]{:S(2)}, u32[]{:S(2)}) collective-permute-start(bf16[192,1536]{1,0:T(8,128)(2,1)S(1)} %convolution_convert_fusion.2), channel_id=1, source_target_pairs={{8,0},{12,4},{0,8},{4,12},{24,16},{28,20},{16,24},{20,28},{9,1},{1... | collective-permute-start | bytes 1769480 | tf_op jit(solution)/shard_map/ppermute | solution.py:31
  164.3 18.2 %collective-permute-start.36 = (bf16[192,384]{1,0:T(8,128)(2,1)S(1)}, bf16[192,384]{1,0:T(8,128)(2,1)S(1)}, u32[]{:S(2)}, u32[]{:S(2)}) collective-permute-start(bf16[192,384]{1,0:T(8,128)(2,1)S(1)} %get-tuple-element.21), channel_id=1, source_target_pairs={{4,0},{8,4},{12,8},{0,12},{20,16},{24,20},{28,24},{16,28},{5,1},{9... | collective-permute-start | bytes 442376 | tf_op jit(solution)/shard_map/ppermute | solution.py:31
  165.9 18.3 %collective-permute-start.35 = (bf16[192,384]{1,0:T(8,128)(2,1)S(1)}, bf16[192,384]{1,0:T(8,128)(2,1)S(1)}, u32[]{:S(2)}, u32[]{:S(2)}) collective-permute-start(bf16[192,384]{1,0:T(8,128)(2,1)S(1)} %get-tuple-element.22), channel_id=1, source_target_pairs={{12,0},{0,4},{4,8},{8,12},{28,16},{16,20},{20,24},{24,28},{13,1},{... | collective-permute-start | bytes 442376 | tf_op jit(solution)/shard_map/ppermute | solution.py:31
  166.4 17.7 %collective-permute-start.34 = (bf16[192,384]{1,0:T(8,128)(2,1)S(1)}, bf16[192,384]{1,0:T(8,128)(2,1)S(1)}, u32[]{:S(2)}, u32[]{:S(2)}) collective-permute-start(bf16[192,384]{1,0:T(8,128)(2,1)S(1)} %get-tuple-element.20), channel_id=1, source_target_pairs={{8,0},{12,4},{0,8},{4,12},{24,16},{28,20},{16,24},{20,28},{9,1},{1... | collective-permute-start | bytes 442376 | tf_op jit(solution)/shard_map/ppermute | solution.py:31
  178.8 8.0 %collective-permute-start.28 = (bf16[192,384]{1,0:T(8,128)(2,1)S(1)}, bf16[192,384]{1,0:T(8,128)(2,1)S(1)}, u32[]{:S(2)}, u32[]{:S(2)}) collective-permute-start(bf16[192,384]{1,0:T(8,128)(2,1)S(1)} %get-tuple-element.16), channel_id=1, source_target_pairs={{32,0},{64,32},{96,64},{0,96},{33,1},{65,33},{97,65},{1,97},{34,2}... | collective-permute-start | bytes 442376 | tf_op jit(solution)/shard_map/ppermute | solution.py:23
  182.6 7.9 %collective-permute-start.27 = (bf16[192,384]{1,0:T(8,128)(2,1)S(1)}, bf16[192,384]{1,0:T(8,128)(2,1)S(1)}, u32[]{:S(2)}, u32[]{:S(2)}) collective-permute-start(bf16[192,384]{1,0:T(8,128)(2,1)S(1)} %get-tuple-element.17), channel_id=1, source_target_pairs={{96,0},{0,32},{32,64},{64,96},{97,1},{1,33},{33,65},{65,97},{98,2}... | collective-permute-start | bytes 442376 | tf_op jit(solution)/shard_map/ppermute | solution.py:23
  182.6 7.9 %collective-permute-start.26 = (bf16[192,384]{1,0:T(8,128)(2,1)S(1)}, bf16[192,384]{1,0:T(8,128)(2,1)S(1)}, u32[]{:S(2)}, u32[]{:S(2)}) collective-permute-start(bf16[192,384]{1,0:T(8,128)(2,1)S(1)} %get-tuple-element.15), channel_id=1, source_target_pairs={{64,0},{96,32},{0,64},{32,96},{65,1},{97,33},{1,65},{33,97},{66,2}... | collective-permute-start | bytes 442376 | tf_op jit(solution)/shard_map/ppermute | solution.py:23
  190.6 5.2 %collective-permute-start.37 = (bf16[192,384]{1,0:T(8,128)(2,1)S(1)}, bf16[192,384]{1,0:T(8,128)(2,1)S(1)}, u32[]{:S(2)}, u32[]{:S(2)}) collective-permute-start(bf16[192,384]{1,0:T(8,128)(2,1)S(1)} %pad_maximum_fusion.13), channel_id=1, source_target_pairs={{0,16},{4,20},{8,24},{12,28},{16,0},{20,4},{24,8},{28,12},{1,17},{... | collective-permute-start | bytes 442376 | tf_op jit(solution)/shard_map/ppermute | solution.py:41
  191.4 5.1 %copy-start = (bf16[1536,768]{1,0:T(8,128)(2,1)}, bf16[1536,768]{1,0:T(8,128)(2,1)S(1)}, u32[]{:S(2)}) copy-start(bf16[1536,768]{1,0:T(8,128)(2,1)S(1)} %fusion.11) | copy-start | bytes 7077892

commit v2 on v0

v2 whole, which is shorter than its diff:
```python
import jax
import jax.numpy as jnp
from jax import lax
from jax.sharding import PartitionSpec as P

coef_root = 0.7978845608028654
coef_cube = 0.044715
bf16, f32 = jnp.bfloat16, jnp.float32

N_RING = 4
BOTH = ("ja", "ka")


def gelu_pair(hidden):
    tanh_value = jnp.tanh(coef_root * (hidden + coef_cube * hidden * hidden * hidden))
    activ = 0.5 * hidden * (1.0 + tanh_value)
    derivative = 0.5 * (1.0 + tanh_value) + 0.5 * hidden * (
        1.0 - tanh_value * tanh_value
    ) * coef_root * (1.0 + 3.0 * coef_cube * hidden * hidden)
    return (activ, derivative)


def from_x(v, r):
    return lax.ppermute(v, "ia", [((i + r) % N_RING, i) for i in range(N_RING)])


def to_x(v, r):
    return from_x(v, N_RING - r)


def from_z(v, r):
    return lax.ppermute(
        v, "ja", [(y * 4 + (z + r) % N_RING, y * 4 + z) for y in range(2) for z in range(N_RING)]
    )


def to_z(v, r):
    return from_z(v, N_RING - r)


def swap_y_lo(v):
    return lax.ppermute(v, "ja", [(j, j ^ 4) for j in range(8)])


def swap_y_hi(v):
    return lax.ppermute(v, "ka", [(k, k ^ 2) for k in range(4)])


def swap_core(v):
    return lax.ppermute(v, "ka", [(k, k ^ 1) for k in range(4)])


def exchange_pairs(turn):
    pairs = []
    for y_lo in range(2):
        for z in range(4):
            for y_hi in range(2):
                for core in range(2):
                    half = turn ^ (z // 2)
                    to_ja = y_hi * 4 + 2 * core + half
                    to_ka = (y_hi ^ y_lo) * 2 + ((z % 2) ^ half)
                    pairs.append(((y_lo * 4 + z) * 4 + y_hi * 2 + core, to_ja * 4 + to_ka))
    return pairs


def dot(a, b, dims=(1, 0)):
    return lax.dot_general(
        a, b, (((dims[0],), (dims[1],)), ((), ())), preferred_element_type=f32
    )


def after_done(v, *arrived):
    return lax.optimization_barrier((v, *arrived))[0]


def pick(index, first, second):
    return jnp.where(index == 0, first, second)


def on_device(tokens, weight, grad_out):
    rows, cols = tokens.shape
    half = rows // 2
    units = weight.shape[1]
    x = lax.axis_index("ia")
    z = lax.axis_index("ja") % 4
    z_hi, z_lo = z // 2, z % 2
    y_hi, core = lax.axis_index("ka") // 2, lax.axis_index("ka") % 2

    left, right = grad_out[:, :units], grad_out[:, units:]
    piece0, piece1 = pick(z_hi, left, right), pick(z_hi, right, left)

    other = swap_y_lo(tokens)
    sent0 = lax.ppermute(piece0, BOTH, exchange_pairs(0))
    sent1 = lax.ppermute(after_done(piece1, other), BOTH, exchange_pairs(1))
    tok_a = jnp.concatenate([tokens[:half], other[:half]], 0)
    tok_b = jnp.concatenate([tokens[half:], other[half:]], 0)
    b2, b1, b3 = (from_z(tok_b, r) for r in (2, 1, 3))
    a2, a1, a3 = (from_x(tok_a, r) for r in (2, 1, 3))
    a0 = jnp.concatenate([tok_a, a1, a2, a3], 1)
    b0 = jnp.concatenate([tok_b, b2, b1, b3], 0)
    n = 2 * half

    held = after_done(weight, a0, b0)
    w = [lax.dynamic_slice_in_dim(held, ((x + r) % N_RING) * cols, cols, 0) for r in range(4)]
    turned = jnp.concatenate(w, 0)
    w = [turned[r * cols : (r + 1) * cols] for r in range(4)]

    a0, b0 = after_done(a0, sent0), after_done(b0, sent0)
    a1, a3 = from_z(a0, 1), from_z(a0, 3)
    b1, b3 = from_x(b0, 1), from_x(b0, 3)
    a2 = jnp.concatenate([from_z(a1[:half], 1), from_z(a3[half:], 3)], 0)
    b2_first, b2_second = from_x(b1[: 2 * n], 1), from_x(b3[2 * n :], 3)

    def middle(of_core, go):
        first, second = of_core
        got = swap_core(pick(core, second, first).astype(bf16))
        summed = (pick(core, first, second) + got.astype(f32)).reshape(-1, 2, half, units)
        got = swap_y_hi(pick(y_hi, summed[:, 1], summed[:, 0]).astype(bf16))
        hidden = pick(y_hi, summed[:, 0], summed[:, 1]) + got.astype(f32)
        activ, derivative = gelu_pair(hidden)
        grad = (go.reshape(hidden.shape).astype(f32) * derivative).astype(bf16)
        return activ.astype(bf16), grad

    def regroup(grad):
        there = swap_y_hi(grad)
        grad = jnp.stack([pick(y_hi, grad, there), pick(y_hi, there, grad)], 1)
        there = swap_core(grad)
        return (
            pick(core, grad, there).reshape(-1, units),
            pick(core, there, grad).reshape(-1, units),
        )

    k0 = z_lo ^ z_hi ^ (core & z_lo)
    go0, go1 = pick(k0, sent0, sent1), pick(k0, sent1, sent0)

    act_e, gr_e = middle((dot(a0, turned), dot(a1, turned)), go0[:half])
    act_l, gr_l = middle((dot(a2, turned), dot(a3, turned)), go1[:half])
    early = dot(b0, w[0]) + dot(b1, w[1]) + dot(b3, w[3])
    act_b, gr_b = middle(
        (early[: 2 * n] + dot(b2_first, w[2]), early[2 * n :] + dot(b2_second, w[2])),
        jnp.stack([go0[half:], go1[half:]]),
    )

    g2, g3 = regroup(gr_l)
    gb0, gb1 = regroup(gr_b)
    g0, g1 = regroup(gr_e)

    d2 = dot(g2, turned, (1, 1)).astype(bf16)
    c2_first, c2_second = dot(gb0, w[2], (1, 1)).astype(bf16), dot(gb1, w[2], (1, 1)).astype(bf16)
    up_a, down_a = to_z(d2[:half], 1), to_z(d2[half:], 3)
    up_b, down_b = to_x(c2_first, 1), to_x(c2_second, 3)
    up_a, down_a, up_b, down_b = lax.optimization_barrier((up_a, down_a, up_b, down_b))

    held0 = jnp.concatenate([act_e[0], act_b[0]], 0)
    held1 = jnp.concatenate([act_l[0], act_b[1]], 0)

    def give_back(turn, *arrived):
        piece = after_done(pick(k0 ^ turn, held0, held1), *arrived)
        return lax.ppermute(piece, BOTH, [(t, s) for s, t in exchange_pairs(turn)])

    back0 = give_back(0, up_a, up_b)

    def before(v, extra):
        return jnp.pad(v, ((0, extra), (0, 0))).astype(f32)

    def after(v, extra):
        return jnp.pad(v, ((extra, 0), (0, 0))).astype(f32)

    gb = jnp.concatenate([gb0, gb1], 0)
    d1 = (dot(g1, turned, (1, 1)) + before(up_a, half)).astype(bf16)
    d3 = (dot(g3, turned, (1, 1)) + after(down_a, half)).astype(bf16)
    c1 = (dot(gb, w[1], (1, 1)) + before(up_b, 2 * n)).astype(bf16)
    c3 = (dot(gb, w[3], (1, 1)) + after(down_b, 2 * n)).astype(bf16)
    d1, d3, c1, c3 = to_z(d1, 1), to_z(d3, 3), to_x(c1, 1), to_x(c3, 3)
    back1 = give_back(1, d1, c1)
    part_a = dot(g0, turned, (1, 1)) + d1.astype(f32) + d3.astype(f32)
    part_b = dot(gb, w[0], (1, 1)) + c1.astype(f32) + c3.astype(f32)

    part_a = after_done(part_a, back0)

    def split_sum(parts, send):
        got = {r: send(parts[r].astype(bf16), r) for r in (2, 1, 3)}
        return parts[0] + got[1].astype(f32) + got[2].astype(f32) + got[3].astype(f32)

    part_a = split_sum([part_a[:, r * cols : (r + 1) * cols] for r in range(4)], to_x)
    part_b = split_sum([part_b[i * n : (i + 1) * n] for i in (0, 2, 1, 3)], to_z)
    got = swap_y_lo(jnp.concatenate([part_a[half:], part_b[half:]], 0).astype(bf16))
    grad_input = jnp.concatenate([part_a[:half], part_b[:half]], 0) + got.astype(f32)

    activated = jnp.concatenate([pick(z_hi, back0, back1), pick(z_hi, back1, back0)], 1)

    ga = after_done(jnp.concatenate([g0, g1, g2, g3], 0), up_a, up_b)
    gb = after_done(gb, up_a, up_b)
    all_a = jnp.concatenate([a0, a1, a2, a3], 0)
    b2 = jnp.concatenate([b2_first, b2_second], 0)
    grad_weight = jnp.zeros_like(weight)
    for r, b in enumerate((b0, b1, b2, b3)):
        block = dot(all_a[:, r * cols : (r + 1) * cols], ga, (0, 0)) + dot(b, gb, (0, 0))
        grad_weight = lax.dynamic_update_slice_in_dim(
            grad_weight, block.astype(bf16), ((x + r) % N_RING) * cols, 0
        )
    return (activated, grad_input.astype(bf16), grad_weight)


def solution(mesh):
    placed = (P("ja", ("ka", "ia")), P("ka", ("ia", "ja")), P("ja", ("ia", "ka")))
    return jax.shard_map(
        on_device,
        mesh=mesh,
        in_specs=placed,
        out_specs=(P("ja", ("ia", "ka")), P("ja", ("ka", "ia")), P("ka", ("ia", "ja"))),
        check_vma=False,
    )
```

time: 526 us -> 176 us (0.33)
  waiting for transfers between devices: 449 us -> 70.7 us
  starting transfers between devices: 0.38 us -> 78.8 us
  matrix products: 34.5 us -> 18.2 us
  blocking collectives: 13.5 us -> 0 us
  between operations: 13.8 us -> 1.47 us
  local copies, waits for them, and re-layouts: 7.26 us -> 1.89 us
    reduce_scatter x2 -> x0, waiting for transfers between devices: 230 us -> none  [the longest x1 189 us: on_device(): lax.psum_scatter(weight_term, 'ja', scatter_dimension=1, tiled=True)]
    all_gather x2 -> x0, waiting for transfers between devices: 206 us -> none  [the longest x1 178 us: on_device(): weight_block = lax.all_gather(weight, 'ja', axis=1, tiled=True)]
    ppermute x0 -> x46, starting transfers between devices: none -> 78.8 us  [the longest x14 27.4 us: from_x(): return lax.ppermute(v, 'ia', [((i + r) % N_RING, i) for i in range(N_RING)])]
    ppermute x0 -> x46, waiting for transfers between devices: none -> 70.7 us  [the longest x6 27.8 us: swap_y_hi(): return lax.ppermute(v, 'ka', [(k, k ^ 2) for k in range(4)])]
    dot_general x3 -> x26, matrix products: 34.5 us -> 18.2 us  [dot(): lax.dot_general(a, b, (((dims[0],), (dims[1],)), ((), ())), preferred_ele...]
    unnamed x6 -> x0, waiting for transfers between devices: 14 us -> none
    all_gather x1 -> x0, blocking collectives: 13.5 us -> none  [on_device(): full_rows = lax.all_gather(tokens, 'ia', axis=1, tiled=True)]
    unnamed x9 -> x12, local copies, waits for them, and re-layouts: 7.26 us -> 0.19 us
  transfers between devices with their start and end apart: 5 -> 46, of which waited for: 5 -> 20; matrix products, arithmetic and copies ran while one was open for 2% -> 12% of each run, Pallas kernels for 0% -> 0%
where the time goes in v2:
time: 176 us
  starting transfers between devices  78.8 us (45%)
  waiting for transfers between devices  70.7 us (40%)
  matrix products  18.2 us (10%)
  other arithmetic  4.53 us (3%)
  local copies, waits for them, and re-layouts  1.89 us (1%)
    ppermute x6, waiting for transfers between devices, swap_y_hi(): return lax.ppermute(v, 'ka', [(k, k ^ 2) for k in range(4)])  27.8 us
    ppermute x14, starting transfers between devices, from_x(): return lax.ppermute(v, 'ia', [((i + r) % N_RING, i) for i in range(N_RING)])  27.4 us
    ppermute x14, starting transfers between devices, from_z(): lax.ppermute(v, 'ja', [(y * 4 + (z + r) % N_RING, y * 4 + z) for y in ran...  20.8 us
    dot_general x26, matrix products, dot(): lax.dot_general(a, b, (((dims[0],), (dims[1],)), ((), ())), preferred_ele...  18.2 us
    ppermute x14, waiting for transfers between devices, from_x(): return lax.ppermute(v, 'ia', [((i + r) % N_RING, i) for i in range(N_RING)])  15.9 us
    ppermute x14, waiting for transfers between devices, from_z(): lax.ppermute(v, 'ja', [(y * 4 + (z + r) % N_RING, y * 4 + z) for y in ran...  15.1 us
    ppermute x6, starting transfers between devices, swap_y_hi(): return lax.ppermute(v, 'ka', [(k, k ^ 2) for k in range(4)])  11.3 us
    ppermute x2, starting transfers between devices, give_back(): return lax.ppermute(piece, BOTH, [(t, s) for s, t in exchange_pairs(turn)])  9.6 us
  transfers between devices with their start and end apart: 46, of which 20 were waited for; matrix products, arithmetic and copies ran while one was open for 12% of the time, Pallas kernels for 0%

profile of v2, /device:TPU:40, one launch (start us, length us, event | category | flops | bytes accessed | tf_op | source)
XLA Modules:
  0.0 175.7 jit_solution(14462534105643473362)
XLA Ops:
  2.1 4.4 %collective-permute-done = bf16[192,384]{1,0:T(8,128)(2,1)S(1)} collective-permute-done((bf16[192,384]{1,0:T(8,128)(2,1)}, bf16[192,384]{1,0:T(8,128)(2,1)S(1)}, u32[]{:S(2)}, u32[]{:S(2)}) %collective-permute-start) | collective-permute-done | bytes 147488 | tf_op jit(solution)/shard_map/ppermute | solution.py:42
  6.6 3.1 %collective-permute-start.5 = (bf16[192,384]{1,0:T(8,128)(2,1)S(1)}, bf16[192,384]{1,0:T(8,128)(2,1)S(1)}, u32[]{:S(2)}, u32[]{:S(2)}) collective-permute-start(bf16[192,384]{1,0:T(8,128)(2,1)S(1)} %pad_maximum_fusion.11), channel_id=1, source_target_pairs={{8,0},{12,4},{0,8},{4,12},{24,16},{28,20},{16,24},{20,28},{9,1},{1... | collective-permute-start | bytes 442376 | tf_op jit(solution)/shard_map/ppermute | solution.py:32
  9.7 2.2 %collective-permute-start.4 = (bf16[192,768]{1,0:T(8,128)(2,1)S(1)}, bf16[192,768]{1,0:T(8,128)(2,1)S(1)}, u32[]{:S(2)}, u32[]{:S(2)}) collective-permute-start(bf16[192,768]{1,0:T(8,128)(2,1)S(1)} %get-tuple-element.62), channel_id=1, source_target_pairs={{0,0},{1,8},{2,18},{3,26},{4,1},{5,9},{6,19},{7,27},{8,5},{9,13},{... | collective-permute-start | bytes 884744 | tf_op jit(solution)/shard_map/ppermute | solution.py:93
  12.0 2.3 %collective-permute-start.6 = (bf16[192,384]{1,0:T(8,128)(2,1)S(1)}, bf16[192,384]{1,0:T(8,128)(2,1)S(1)}, u32[]{:S(2)}, u32[]{:S(2)}) collective-permute-start(bf16[192,384]{1,0:T(8,128)(2,1)S(1)} %pad_maximum_fusion.11), channel_id=1, source_target_pairs={{4,0},{8,4},{12,8},{0,12},{20,16},{24,20},{28,24},{16,28},{5,1},{9... | collective-permute-start | bytes 442376 | tf_op jit(solution)/shard_map/ppermute | solution.py:32
  14.4 1.6 collective-permute-start.3
  15.9 2.7 %collective-permute-start.2 = (bf16[192,384]{1,0:T(8,128)(2,1)S(1)}, bf16[192,384]{1,0:T(8,128)(2,1)S(1)}, u32[]{:S(2)}, u32[]{:S(2)}) collective-permute-start(bf16[192,384]{1,0:T(8,128)(2,1)S(1)} %pad_maximum_fusion.10), channel_id=1, source_target_pairs={{64,0},{96,32},{0,64},{32,96},{65,1},{97,33},{1,65},{33,97},{66,2}... | collective-permute-start | bytes 442376 | tf_op jit(solution)/shard_map/ppermute | solution.py:24
  18.7 1.7 collective-permute-done.6
  20.4 2.8 %collective-permute-start.1 = (bf16[192,384]{1,0:T(8,128)(2,1)S(1)}, bf16[192,384]{1,0:T(8,128)(2,1)S(1)}, u32[]{:S(2)}, u32[]{:S(2)}) collective-permute-start(bf16[192,384]{1,0:T(8,128)(2,1)S(1)} %pad_maximum_fusion.10), channel_id=1, source_target_pairs={{32,0},{64,32},{96,64},{0,96},{33,1},{65,33},{97,65},{1,97},{34,2}... | collective-permute-start | bytes 442376 | tf_op jit(solution)/shard_map/ppermute | solution.py:24
  23.2 5.9 %collective-permute-start.22 = (bf16[192,768]{1,0:T(8,128)(2,1)S(1)}, bf16[192,768]{1,0:T(8,128)(2,1)S(1)}, u32[]{:S(2)}, u32[]{:S(2)}) collective-permute-start(bf16[192,768]{1,0:T(8,128)(2,1)S(1)} %get-tuple-element.19), channel_id=1, source_target_pairs={{0,5},{1,13},{2,23},{3,31},{4,4},{5,12},{6,22},{7,30},{8,0},{9,8},... | collective-permute-start | bytes 884744 | tf_op jit(solution)/shard_map/ppermute | solution.py:94
  30.0 1.2 collective-permute-start.12
  31.7 1.7 collective-permute-start.8
  35.2 2.4 %collective-permute-done.22 = bf16[192,768]{1,0:T(8,128)(2,1)S(1)} collective-permute-done((bf16[192,768]{1,0:T(8,128)(2,1)S(1)}, bf16[192,768]{1,0:T(8,128)(2,1)S(1)}, u32[]{:S(2)}, u32[]{:S(2)}) %collective-permute-start.22) | collective-permute-done | bytes 294944 | tf_op jit(solution)/shard_map/ppermute | solution.py:94
  37.7 7.6 %collective-permute-done.12 = bf16[768,384]{1,0:T(8,128)(2,1)S(1)} collective-permute-done((bf16[768,384]{1,0:T(8,128)(2,1)S(1)}, bf16[768,384]{1,0:T(8,128)(2,1)S(1)}, u32[]{:S(2)}, u32[]{:S(2)}) %collective-permute-start.12) | collective-permute-done | bytes 589856 | tf_op jit(solution)/shard_map/ppermute | solution.py:24
  45.5 3.3 %collective-permute-start.13 = (bf16[384,384]{1,0:T(8,128)(2,1)S(1)}, bf16[384,384]{1,0:T(8,128)(2,1)S(1)}, u32[]{:S(2)}, u32[]{:S(2)}) collective-permute-start(bf16[384,384]{1,0:T(8,128)(2,1)S(1)} %slice.187), channel_id=1, source_target_pairs={{32,0},{64,32},{96,64},{0,96},{33,1},{65,33},{97,65},{1,97},{34,2}... | collective-permute-start | bytes 884744 | tf_op jit(solution)/shard_map/ppermute | solution.py:24
  48.8 1.7 collective-permute-start.19
  50.5 1.8 %collective-permute-start.17 = (bf16[96,1536]{1,0:T(8,128)(2,1)S(1)}, bf16[96,1536]{1,0:T(8,128)(2,1)S(1)}, u32[]{:S(2)}, u32[]{:S(2)}) collective-permute-start(bf16[96,1536]{1,0:T(8,128)(2,1)S(1)} %slice.193), channel_id=1, source_target_pairs={{4,0},{8,4},{12,8},{0,12},{20,16},{24,20},{28,24},{16,28},{5,1},{9... | collective-permute-start | bytes 884744 | tf_op jit(solution)/shard_map/ppermute | solution.py:32
  56.1 2.5 %collective-permute-done.19 = bf16[96,1536]{1,0:T(8,128)(2,1)S(1)} collective-permute-done((bf16[96,1536]{1,0:T(8,128)(2,1)S(1)}, bf16[96,1536]{1,0:T(8,128)(2,1)S(1)}, u32[]{:S(2)}, u32[]{:S(2)}) %collective-permute-start.19) | collective-permute-done | bytes 294944 | tf_op jit(solution)/shard_map/ppermute | solution.py:32
  60.1 2.2 %collective-permute-start.10 = (bf16[1,96,768]{2,1,0:T(8,128)(2,1)S(1)}, bf16[1,96,768]{2,1,0:T(8,128)(2,1)S(1)}, u32[]{:S(2)}, u32[]{:S(2)}) collective-permute-start(bf16[1,96,768]{2,1,0:T(8,128)(2,1)S(1)} %fusion.51), channel_id=1, source_target_pairs={{0,2},{1,3},{2,0},{3,1},{4,6},{5,7},{6,4},{7,5},{8,10},{9,11},{10,... | collective-permute-start | bytes 442376 | tf_op jit(solution)/shard_map/ppermute | solution.py:46
  62.4 5.8 %collective-permute-done.10 = bf16[1,96,768]{2,1,0:T(8,128)(2,1)S(1)} collective-permute-done((bf16[1,96,768]{2,1,0:T(8,128)(2,1)S(1)}, bf16[1,96,768]{2,1,0:T(8,128)(2,1)S(1)}, u32[]{:S(2)}, u32[]{:S(2)}) %collective-permute-start.10) | collective-permute-done | bytes 147488 | tf_op jit(solution)/shard_map/ppermute | solution.py:46
  68.4 2.0 %collective-permute-start.32 = (bf16[1,96,768]{2,1,0:T(8,128)(2,1)S(1)}, bf16[1,96,768]{2,1,0:T(8,128)(2,1)S(1)}, u32[]{:S(2)}, u32[]{:S(2)}) collective-permute-start(bf16[1,96,768]{2,1,0:T(8,128)(2,1)S(1)} %get-tuple-element.39), channel_id=1, source_target_pairs={{0,2},{1,3},{2,0},{3,1},{4,6},{5,7},{6,4},{7,5},{8,10},{9,11},{10,... | collective-permute-start | bytes 442376 | tf_op jit(solution)/shard_map/ppermute | solution.py:46
  70.5 1.7 collective-permute-start.21
  72.2 4.5 %collective-permute-done.32 = bf16[1,96,768]{2,1,0:T(8,128)(2,1)S(1)} collective-permute-done((bf16[1,96,768]{2,1,0:T(8,128)(2,1)S(1)}, bf16[1,96,768]{2,1,0:T(8,128)(2,1)S(1)}, u32[]{:S(2)}, u32[]{:S(2)}) %collective-permute-start.32) | collective-permute-done | bytes 147488 | tf_op jit(solution)/shard_map/ppermute | solution.py:46
  76.9 1.7 collective-permute-done.21
  78.9 2.0 %collective-permute-start.23 = (bf16[1,96,768]{2,1,0:T(8,128)(2,1)S(1)}, bf16[1,96,768]{2,1,0:T(8,128)(2,1)S(1)}, u32[]{:S(2)}, u32[]{:S(2)}) collective-permute-start(bf16[1,96,768]{2,1,0:T(8,128)(2,1)S(1)} %get-tuple-element.37), channel_id=1, source_target_pairs={{0,2},{1,3},{2,0},{3,1},{4,6},{5,7},{6,4},{7,5},{8,10},{9,11},{10,... | collective-permute-start | bytes 442376 | tf_op jit(solution)/shard_map/ppermute | solution.py:46
  81.3 1.7 collective-permute-start.16
  83.1 4.0 %collective-permute-done.23 = bf16[1,96,768]{2,1,0:T(8,128)(2,1)S(1)} collective-permute-done((bf16[1,96,768]{2,1,0:T(8,128)(2,1)S(1)}, bf16[1,96,768]{2,1,0:T(8,128)(2,1)S(1)}, u32[]{:S(2)}, u32[]{:S(2)}) %collective-permute-start.23) | collective-permute-done | bytes 147488 | tf_op jit(solution)/shard_map/ppermute | solution.py:46
  87.3 4.6 %collective-permute-done.16 = bf16[2,96,768]{2,1,0:T(8,128)(2,1)S(1)} collective-permute-done((bf16[2,96,768]{2,1,0:T(8,128)(2,1)S(1)}, bf16[2,96,768]{2,1,0:T(8,128)(2,1)S(1)}, u32[]{:S(2)}, u32[]{:S(2)}) %collective-permute-start.16) | collective-permute-done | bytes 294944 | tf_op jit(solution)/shard_map/ppermute | solution.py:46
  92.4 1.8 collective-permute-start.27
  94.3 7.2 %collective-permute-done.27 = bf16[2,96,768]{2,1,0:T(8,128)(2,1)S(1)} collective-permute-done((bf16[2,96,768]{2,1,0:T(8,128)(2,1)S(1)}, bf16[2,96,768]{2,1,0:T(8,128)(2,1)S(1)}, u32[]{:S(2)}, u32[]{:S(2)}) %collective-permute-start.27) | collective-permute-done | bytes 294944 | tf_op jit(solution)/shard_map/ppermute | solution.py:46
  102.6 2.5 %collective-permute-start.25 = (bf16[96,1536]{1,0:T(8,128)(2,1)S(1)}, bf16[96,1536]{1,0:T(8,128)(2,1)S(1)}, u32[]{:S(2)}, u32[]{:S(2)}) collective-permute-start(bf16[96,1536]{1,0:T(8,128)(2,1)S(1)} %get-tuple-element.58), channel_id=1, source_target_pairs={{12,0},{0,4},{4,8},{8,12},{28,16},{16,20},{20,24},{24,28},{13,1},{... | collective-permute-start | bytes 884744 | tf_op jit(solution)/shard_map/ppermute | solution.py:32
  106.9 3.3 %collective-permute-start.30 = (bf16[384,384]{1,0:T(8,128)(2,1)S(1)}, bf16[384,384]{1,0:T(8,128)(2,1)S(1)}, u32[]{:S(2)}, u32[]{:S(2)}) collective-permute-start(bf16[384,384]{1,0:T(8,128)(2,1)S(1)} %convolution_convert_fusion.1), channel_id=1, source_target_pairs={{32,0},{64,32},{96,64},{0,96},{33,1},{65,33},{97,65},{1,97},{34,2}... | collective-permute-start | bytes 884744 | tf_op jit(solution)/shard_map/ppermute | solution.py:24
  110.5 2.9 %collective-permute-done.25 = bf16[96,1536]{1,0:T(8,128)(2,1)S(1)} collective-permute-done((bf16[96,1536]{1,0:T(8,128)(2,1)S(1)}, bf16[96,1536]{1,0:T(8,128)(2,1)S(1)}, u32[]{:S(2)}, u32[]{:S(2)}) %collective-permute-start.25) | collective-permute-done | bytes 294944 | tf_op jit(solution)/shard_map/ppermute | solution.py:32
  113.3 2.2 %collective-permute-done.26 = bf16[96,1536]{1,0:T(8,128)(2,1)S(1)} collective-permute-done((bf16[96,1536]{1,0:T(8,128)(2,1)S(1)}, bf16[96,1536]{1,0:T(8,128)(2,1)S(1)}, u32[]{:S(2)}, u32[]{:S(2)}) %collective-permute-start.26) | collective-permute-done | bytes 294944 | tf_op jit(solution)/shard_map/ppermute | solution.py:32
  115.5 1.2 collective-permute-done.29
  118.5 6.3 %collective-permute-start.31 = (bf16[192,768]{1,0:T(8,128)(2,1)S(1)}, bf16[192,768]{1,0:T(8,128)(2,1)S(1)}, u32[]{:S(2)}, u32[]{:S(2)}) collective-permute-start(bf16[192,768]{1,0:T(8,128)(2,1)S(1)} %get-tuple-element.22), channel_id=1, source_target_pairs={{0,0},{8,1},{18,2},{26,3},{1,4},{9,5},{19,6},{27,7},{5,8},{13,9},{... | collective-permute-start | bytes 884744 | tf_op jit(solution)/shard_map/ppermute | solution.py:159
  126.0 3.4 %collective-permute-start.41 = (bf16[768,384]{1,0:T(8,128)(2,1)S(1)}, bf16[768,384]{1,0:T(8,128)(2,1)S(1)}, u32[]{:S(2)}, u32[]{:S(2)}) collective-permute-start(bf16[768,384]{1,0:T(8,128)(2,1)S(1)} %fusion.5), channel_id=1, source_target_pairs={{32,0},{64,32},{96,64},{0,96},{33,1},{65,33},{97,65},{1,97},{34,2}... | collective-permute-start | bytes 1769480 | tf_op jit(solution)/shard_map/ppermute | solution.py:24
  130.3 2.2 %collective-permute-start.37 = (bf16[192,1536]{1,0:T(8,128)(2,1)S(1)}, bf16[192,1536]{1,0:T(8,128)(2,1)S(1)}, u32[]{:S(2)}, u32[]{:S(2)}) collective-permute-start(bf16[192,1536]{1,0:T(8,128)(2,1)S(1)} %fusion.2), channel_id=1, source_target_pairs={{4,0},{8,4},{12,8},{0,12},{20,16},{24,20},{28,24},{16,28},{5,1},{9... | collective-permute-start | bytes 1769480 | tf_op jit(solution)/shard_map/ppermute | solution.py:32
  137.4 2.6 %collective-permute-done.34 = bf16[192,1536]{1,0:T(8,128)(2,1)S(1)} collective-permute-done((bf16[192,1536]{1,0:T(8,128)(2,1)S(1)}, bf16[192,1536]{1,0:T(8,128)(2,1)S(1)}, u32[]{:S(2)}, u32[]{:S(2)}) %collective-permute-start.34) | collective-permute-done | bytes 589856 | tf_op jit(solution)/shard_map/ppermute | solution.py:32
  140.9 3.3 %collective-permute-start.36 = (bf16[192,768]{1,0:T(8,128)(2,1)S(1)}, bf16[192,768]{1,0:T(8,128)(2,1)S(1)}, u32[]{:S(2)}, u32[]{:S(2)}) collective-permute-start(bf16[192,768]{1,0:T(8,128)(2,1)S(1)} %get-tuple-element.23), channel_id=1, source_target_pairs={{5,0},{13,1},{23,2},{31,3},{4,4},{12,5},{22,6},{30,7},{0,8},{8,9},... | collective-permute-start | bytes 884744 | tf_op jit(solution)/shard_map/ppermute | solution.py:159
  145.1 1.9 %collective-permute-start.44 = (bf16[192,384]{1,0:T(8,128)(2,1)S(1)}, bf16[192,384]{1,0:T(8,128)(2,1)S(1)}, u32[]{:S(2)}, u32[]{:S(2)}) collective-permute-start(bf16[192,384]{1,0:T(8,128)(2,1)S(1)} %get-tuple-element.49), channel_id=1, source_target_pairs={{4,0},{8,4},{12,8},{0,12},{20,16},{24,20},{28,24},{16,28},{5,1},{9... | collective-permute-start | bytes 442376 | tf_op jit(solution)/shard_map/ppermute | solution.py:32
  147.1 2.5 %collective-permute-start.42 = (bf16[192,384]{1,0:T(8,128)(2,1)S(1)}, bf16[192,384]{1,0:T(8,128)(2,1)S(1)}, u32[]{:S(2)}, u32[]{:S(2)}) collective-permute-start(bf16[192,384]{1,0:T(8,128)(2,1)S(1)} %get-tuple-element.48), channel_id=1, source_target_pairs={{12,0},{0,4},{4,8},{8,12},{28,16},{16,20},{20,24},{24,28},{13,1},{... | collective-permute-start | bytes 442376 | tf_op jit(solution)/shard_map/ppermute | solution.py:32
  150.7 3.6 %collective-permute-start.40 = (bf16[192,384]{1,0:T(8,128)(2,1)S(1)}, bf16[192,384]{1,0:T(8,128)(2,1)S(1)}, u32[]{:S(2)}, u32[]{:S(2)}) collective-permute-start(bf16[192,384]{1,0:T(8,128)(2,1)S(1)} %get-tuple-element.42), channel_id=1, source_target_pairs={{32,0},{64,32},{96,64},{0,96},{33,1},{65,33},{97,65},{1,97},{34,2}... | collective-permute-start | bytes 442376 | tf_op jit(solution)/shard_map/ppermute | solution.py:24
  154.2 3.3 %collective-permute-done.44 = bf16[192,384]{1,0:T(8,128)(2,1)S(1)} collective-permute-done((bf16[192,384]{1,0:T(8,128)(2,1)S(1)}, bf16[192,384]{1,0:T(8,128)(2,1)S(1)}, u32[]{:S(2)}, u32[]{:S(2)}) %collective-permute-start.44) | collective-permute-done | bytes 147488 | tf_op jit(solution)/shard_map/ppermute | solution.py:32
  157.5 2.0 %collective-permute-start.39 = (bf16[192,384]{1,0:T(8,128)(2,1)S(1)}, bf16[192,384]{1,0:T(8,128)(2,1)S(1)}, u32[]{:S(2)}, u32[]{:S(2)}) collective-permute-start(bf16[192,384]{1,0:T(8,128)(2,1)S(1)} %get-tuple-element.43), channel_id=1, source_target_pairs={{64,0},{96,32},{0,64},{32,96},{65,1},{97,33},{1,65},{33,97},{66,2}... | collective-permute-start | bytes 442376 | tf_op jit(solution)/shard_map/ppermute | solution.py:24
  159.5 2.2 %collective-permute-start.38 = (bf16[192,384]{1,0:T(8,128)(2,1)S(1)}, bf16[192,384]{1,0:T(8,128)(2,1)S(1)}, u32[]{:S(2)}, u32[]{:S(2)}) collective-permute-start(bf16[192,384]{1,0:T(8,128)(2,1)S(1)} %get-tuple-element.41), channel_id=1, source_target_pairs={{96,0},{0,32},{32,64},{64,96},{97,1},{1,33},{33,65},{65,97},{98,2}... | collective-permute-start | bytes 442376 | tf_op jit(solution)/shard_map/ppermute | solution.py:24
  161.9 3.8 %collective-permute-done.39 = bf16[192,384]{1,0:T(8,128)(2,1)S(1)} collective-permute-done((bf16[192,384]{1,0:T(8,128)(2,1)S(1)}, bf16[192,384]{1,0:T(8,128)(2,1)S(1)}, u32[]{:S(2)}, u32[]{:S(2)}) %collective-permute-start.39) | collective-permute-done | bytes 147488 | tf_op jit(solution)/shard_map/ppermute | solution.py:24
  165.7 2.4 %collective-permute-done.38 = bf16[192,384]{1,0:T(8,128)(2,1)S(1)} collective-permute-done((bf16[192,384]{1,0:T(8,128)(2,1)S(1)}, bf16[192,384]{1,0:T(8,128)(2,1)S(1)}, u32[]{:S(2)}, u32[]{:S(2)}) %collective-permute-start.38) | collective-permute-done | bytes 147488 | tf_op jit(solution)/shard_map/ppermute | solution.py:24
  169.0 5.0 %collective-permute-done.45 = bf16[192,384]{1,0:T(8,128)(2,1)S(1)} collective-permute-done((bf16[192,384]{1,0:T(8,128)(2,1)S(1)}, bf16[192,384]{1,0:T(8,128)(2,1)S(1)}, u32[]{:S(2)}, u32[]{:S(2)}) %collective-permute-start.45) | collective-permute-done | bytes 147488 | tf_op jit(solution)/shard_map/ppermute | solution.py:42
  (135 shorter events, 29.7 us)
Async XLA Ops:
  0.6 9.0 %copy-start.2 = (bf16[192,1536]{1,0:T(8,128)(2,1)S(1)}, bf16[192,1536]{1,0:T(8,128)(2,1)}, u32[]{:S(2)}) copy-start(bf16[192,1536]{1,0:T(8,128)(2,1)} %param.5) | copy-start | bytes 1769476
  0.6 5.9 %collective-permute-start = (bf16[192,384]{1,0:T(8,128)(2,1)}, bf16[192,384]{1,0:T(8,128)(2,1)S(1)}, u32[]{:S(2)}, u32[]{:S(2)}) collective-permute-start(bf16[192,384]{1,0:T(8,128)(2,1)} %param.3), channel_id=1, source_target_pairs={{0,16},{4,20},{8,24},{12,28},{16,0},{20,4},{24,8},{28,12},{1,17},{... | collective-permute-start | bytes 442376 | tf_op jit(solution)/shard_map/ppermute | solution.py:42
  6.6 9.4 %collective-permute-start.5 = (bf16[192,384]{1,0:T(8,128)(2,1)S(1)}, bf16[192,384]{1,0:T(8,128)(2,1)S(1)}, u32[]{:S(2)}, u32[]{:S(2)}) collective-permute-start(bf16[192,384]{1,0:T(8,128)(2,1)S(1)} %pad_maximum_fusion.11), channel_id=1, source_target_pairs={{8,0},{12,4},{0,8},{4,12},{24,16},{28,20},{16,24},{20,28},{9,1},{1... | collective-permute-start | bytes 442376 | tf_op jit(solution)/shard_map/ppermute | solution.py:32
  9.7 19.4 %collective-permute-start.4 = (bf16[192,768]{1,0:T(8,128)(2,1)S(1)}, bf16[192,768]{1,0:T(8,128)(2,1)S(1)}, u32[]{:S(2)}, u32[]{:S(2)}) collective-permute-start(bf16[192,768]{1,0:T(8,128)(2,1)S(1)} %get-tuple-element.62), channel_id=1, source_target_pairs={{0,0},{1,8},{2,18},{3,26},{4,1},{5,9},{6,19},{7,27},{8,5},{9,13},{... | collective-permute-start | bytes 884744 | tf_op jit(solution)/shard_map/ppermute | solution.py:93
  12.0 8.4 %collective-permute-start.6 = (bf16[192,384]{1,0:T(8,128)(2,1)S(1)}, bf16[192,384]{1,0:T(8,128)(2,1)S(1)}, u32[]{:S(2)}, u32[]{:S(2)}) collective-permute-start(bf16[192,384]{1,0:T(8,128)(2,1)S(1)} %pad_maximum_fusion.11), channel_id=1, source_target_pairs={{4,0},{8,4},{12,8},{0,12},{20,16},{24,20},{28,24},{16,28},{5,1},{9... | collective-permute-start | bytes 442376 | tf_op jit(solution)/shard_map/ppermute | solution.py:32
  14.3 8.8 %collective-permute-start.7 = (bf16[192,384]{1,0:T(8,128)(2,1)S(1)}, bf16[192,384]{1,0:T(8,128)(2,1)S(1)}, u32[]{:S(2)}, u32[]{:S(2)}) collective-permute-start(bf16[192,384]{1,0:T(8,128)(2,1)S(1)} %pad_maximum_fusion.11), channel_id=1, source_target_pairs={{12,0},{0,4},{4,8},{8,12},{28,16},{16,20},{20,24},{24,28},{13,1},{... | collective-permute-start | bytes 442376 | tf_op jit(solution)/shard_map/ppermute | solution.py:32
  14.4 19.0 %copy-start.1 = (bf16[1536,768]{1,0:T(8,128)(2,1)S(1)}, bf16[1536,768]{1,0:T(8,128)(2,1)}, u32[]{:S(2)}) copy-start(bf16[1536,768]{1,0:T(8,128)(2,1)} %param.4) | copy-start | bytes 7077892
  14.4 15.6 %collective-permute-start.3 = (bf16[192,384]{1,0:T(8,128)(2,1)S(1)}, bf16[192,384]{1,0:T(8,128)(2,1)S(1)}, u32[]{:S(2)}, u32[]{:S(2)}) collective-permute-start(bf16[192,384]{1,0:T(8,128)(2,1)S(1)} %pad_maximum_fusion.10), channel_id=1, source_target_pairs={{96,0},{0,32},{32,64},{64,96},{97,1},{1,33},{33,65},{65,97},{98,2}... | collective-permute-start | bytes 442376 | tf_op jit(solution)/shard_map/ppermute | solution.py:24
  15.9 15.3 %collective-permute-start.2 = (bf16[192,384]{1,0:T(8,128)(2,1)S(1)}, bf16[192,384]{1,0:T(8,128)(2,1)S(1)}, u32[]{:S(2)}, u32[]{:S(2)}) collective-permute-start(bf16[192,384]{1,0:T(8,128)(2,1)S(1)} %pad_maximum_fusion.10), channel_id=1, source_target_pairs={{64,0},{96,32},{0,64},{32,96},{65,1},{97,33},{1,65},{33,97},{66,2}... | collective-permute-start | bytes 442376 | tf_op jit(solution)/shard_map/ppermute | solution.py:24
  20.4 10.9 %collective-permute-start.1 = (bf16[192,384]{1,0:T(8,128)(2,1)S(1)}, bf16[192,384]{1,0:T(8,128)(2,1)S(1)}, u32[]{:S(2)}, u32[]{:S(2)}) collective-permute-start(bf16[192,384]{1,0:T(8,128)(2,1)S(1)} %pad_maximum_fusion.10), channel_id=1, source_target_pairs={{32,0},{64,32},{96,64},{0,96},{33,1},{65,33},{97,65},{1,97},{34,2}... | collective-permute-start | bytes 442376 | tf_op jit(solution)/shard_map/ppermute | solution.py:24
  23.2 14.4 %collective-permute-start.22 = (bf16[192,768]{1,0:T(8,128)(2,1)S(1)}, bf16[192,768]{1,0:T(8,128)(2,1)S(1)}, u32[]{:S(2)}, u32[]{:S(2)}) collective-permute-start(bf16[192,768]{1,0:T(8,128)(2,1)S(1)} %get-tuple-element.19), channel_id=1, source_target_pairs={{0,5},{1,13},{2,23},{3,31},{4,4},{5,12},{6,22},{7,30},{8,0},{9,8},... | collective-permute-start | bytes 884744 | tf_op jit(solution)/shard_map/ppermute | solution.py:94
  29.1 16.3 %collective-permute-start.11 = (bf16[768,384]{1,0:T(8,128)(2,1)S(1)}, bf16[768,384]{1,0:T(8,128)(2,1)S(1)}, u32[]{:S(2)}, u32[]{:S(2)}) collective-permute-start(bf16[768,384]{1,0:T(8,128)(2,1)S(1)} %constant_dynamic-update-slice_fusion), channel_id=1, source_target_pairs={{32,0},{64,32},{96,64},{0,96},{33,1},{65,33},{97,65},{1,97},{34,2}... | collective-permute-start | bytes 1769480 | tf_op jit(solution)/shard_map/ppermute | solution.py:24
  30.0 15.3 %collective-permute-start.12 = (bf16[768,384]{1,0:T(8,128)(2,1)S(1)}, bf16[768,384]{1,0:T(8,128)(2,1)S(1)}, u32[]{:S(2)}, u32[]{:S(2)}) collective-permute-start(bf16[768,384]{1,0:T(8,128)(2,1)S(1)} %constant_dynamic-update-slice_fusion), channel_id=1, source_target_pairs={{96,0},{0,32},{32,64},{64,96},{97,1},{1,33},{33,65},{65,97},{98,2}... | collective-permute-start | bytes 1769480 | tf_op jit(solution)/shard_map/ppermute | solution.py:24
  31.3 17.5 %collective-permute-start.18 = (bf16[192,1536]{1,0:T(8,128)(2,1)S(1)}, bf16[192,1536]{1,0:T(8,128)(2,1)S(1)}, u32[]{:S(2)}, u32[]{:S(2)}) collective-permute-start(bf16[192,1536]{1,0:T(8,128)(2,1)S(1)} %pad_maximum_fusion.3), channel_id=1, source_target_pairs={{12,0},{0,4},{4,8},{8,12},{28,16},{16,20},{20,24},{24,28},{13,1},{... | collective-permute-start | bytes 1769480 | tf_op jit(solution)/shard_map/ppermute | solution.py:32
  31.7 18.8 %collective-permute-start.8 = (bf16[192,1536]{1,0:T(8,128)(2,1)S(1)}, bf16[192,1536]{1,0:T(8,128)(2,1)S(1)}, u32[]{:S(2)}, u32[]{:S(2)}) collective-permute-start(bf16[192,1536]{1,0:T(8,128)(2,1)S(1)} %pad_maximum_fusion.3), channel_id=1, source_target_pairs={{4,0},{8,4},{12,8},{0,12},{20,16},{24,20},{28,24},{16,28},{5,1},{9... | collective-permute-start | bytes 1769480 | tf_op jit(solution)/shard_map/ppermute | solution.py:32
  45.4 9.2 %collective-permute-start.14 = (bf16[384,384]{1,0:T(8,128)(2,1)S(1)}, bf16[384,384]{1,0:T(8,128)(2,1)S(1)}, u32[]{:S(2)}, u32[]{:S(2)}) collective-permute-start(bf16[384,384]{1,0:T(8,128)(2,1)S(1)} %slice.189), channel_id=1, source_target_pairs={{96,0},{0,32},{32,64},{64,96},{97,1},{1,33},{33,65},{65,97},{98,2}... | collective-permute-start | bytes 884744 | tf_op jit(solution)/shard_map/ppermute | solution.py:24
  45.5 9.6 %collective-permute-start.13 = (bf16[384,384]{1,0:T(8,128)(2,1)S(1)}, bf16[384,384]{1,0:T(8,128)(2,1)S(1)}, u32[]{:S(2)}, u32[]{:S(2)}) collective-permute-start(bf16[384,384]{1,0:T(8,128)(2,1)S(1)} %slice.187), channel_id=1, source_target_pairs={{32,0},{64,32},{96,64},{0,96},{33,1},{65,33},{97,65},{1,97},{34,2}... | collective-permute-start | bytes 884744 | tf_op jit(solution)/shard_map/ppermute | solution.py:24
  48.8 9.8 %collective-permute-start.19 = (bf16[96,1536]{1,0:T(8,128)(2,1)S(1)}, bf16[96,1536]{1,0:T(8,128)(2,1)S(1)}, u32[]{:S(2)}, u32[]{:S(2)}) collective-permute-start(bf16[96,1536]{1,0:T(8,128)(2,1)S(1)} %slice.194), channel_id=1, source_target_pairs={{12,0},{0,4},{4,8},{8,12},{28,16},{16,20},{20,24},{24,28},{13,1},{... | collective-permute-start | bytes 884744 | tf_op jit(solution)/shard_map/ppermute | solution.py:32
  50.5 8.2 %collective-permute-start.17 = (bf16[96,1536]{1,0:T(8,128)(2,1)S(1)}, bf16[96,1536]{1,0:T(8,128)(2,1)S(1)}, u32[]{:S(2)}, u32[]{:S(2)}) collective-permute-start(bf16[96,1536]{1,0:T(8,128)(2,1)S(1)} %slice.193), channel_id=1, source_target_pairs={{4,0},{8,4},{12,8},{0,12},{20,16},{24,20},{28,24},{16,28},{5,1},{9... | collective-permute-start | bytes 884744 | tf_op jit(solution)/shard_map/ppermute | solution.py:32
  52.9 7.1 %collective-permute-start.9 = (bf16[192,768]{1,0:T(8,128)(2,1)S(1)}, bf16[192,768]{1,0:T(8,128)(2,1)S(1)}, u32[]{:S(2)}, u32[]{:S(2)}) collective-permute-start(bf16[192,768]{1,0:T(8,128)(2,1)S(1)} %get-tuple-element.79), channel_id=1, source_target_pairs={{0,1},{1,0},{2,3},{3,2},{4,5},{5,4},{6,7},{7,6},{8,9},{9,8},{10,11... | collective-permute-start | bytes 884744 | tf_op jit(solution)/shard_map/ppermute | solution.py:50
  55.6 25.3 %collective-permute-start.15 = (bf16[384,768]{1,0:T(8,128)(2,1)S(1)}, bf16[384,768]{1,0:T(8,128)(2,1)S(1)}, u32[]{:S(2)}, u32[]{:S(2)}) collective-permute-start(bf16[384,768]{1,0:T(8,128)(2,1)S(1)} %get-tuple-element.75), channel_id=1, source_target_pairs={{0,1},{1,0},{2,3},{3,2},{4,5},{5,4},{6,7},{7,6},{8,9},{9,8},{10,11... | collective-permute-start | bytes 1769480 | tf_op jit(solution)/shard_map/ppermute | solution.py:50
  59.9 10.5 %collective-permute-start.20 = (bf16[192,768]{1,0:T(8,128)(2,1)S(1)}, bf16[192,768]{1,0:T(8,128)(2,1)S(1)}, u32[]{:S(2)}, u32[]{:S(2)}) collective-permute-start(bf16[192,768]{1,0:T(8,128)(2,1)S(1)} %get-tuple-element.77), channel_id=1, source_target_pairs={{0,1},{1,0},{2,3},{3,2},{4,5},{5,4},{6,7},{7,6},{8,9},{9,8},{10,11... | collective-permute-start | bytes 884744 | tf_op jit(solution)/shard_map/ppermute | solution.py:50
  60.1 8.0 %collective-permute-start.10 = (bf16[1,96,768]{2,1,0:T(8,128)(2,1)S(1)}, bf16[1,96,768]{2,1,0:T(8,128)(2,1)S(1)}, u32[]{:S(2)}, u32[]{:S(2)}) collective-permute-start(bf16[1,96,768]{2,1,0:T(8,128)(2,1)S(1)} %fusion.51), channel_id=1, source_target_pairs={{0,2},{1,3},{2,0},{3,1},{4,6},{5,7},{6,4},{7,5},{8,10},{9,11},{10,... | collective-permute-start | bytes 442376 | tf_op jit(solution)/shard_map/ppermute | solution.py:46
  68.4 8.3 %collective-permute-start.32 = (bf16[1,96,768]{2,1,0:T(8,128)(2,1)S(1)}, bf16[1,96,768]{2,1,0:T(8,128)(2,1)S(1)}, u32[]{:S(2)}, u32[]{:S(2)}) collective-permute-start(bf16[1,96,768]{2,1,0:T(8,128)(2,1)S(1)} %get-tuple-element.39), channel_id=1, source_target_pairs={{0,2},{1,3},{2,0},{3,1},{4,6},{5,7},{6,4},{7,5},{8,10},{9,11},{10,... | collective-permute-start | bytes 442376 | tf_op jit(solution)/shard_map/ppermute | solution.py:46
  70.5 8.1 %collective-permute-start.21 = (bf16[1,96,768]{2,1,0:T(8,128)(2,1)S(1)}, bf16[1,96,768]{2,1,0:T(8,128)(2,1)S(1)}, u32[]{:S(2)}, u32[]{:S(2)}) collective-permute-start(bf16[1,96,768]{2,1,0:T(8,128)(2,1)S(1)} %fusion.52), channel_id=1, source_target_pairs={{0,2},{1,3},{2,0},{3,1},{4,6},{5,7},{6,4},{7,5},{8,10},{9,11},{10,... | collective-permute-start | bytes 442376 | tf_op jit(solution)/shard_map/ppermute | solution.py:46
  76.8 6.2 %collective-permute-start.33 = (bf16[1,2,96,768]{3,2,1,0:T(8,128)(2,1)S(1)}, bf16[1,2,96,768]{3,2,1,0:T(8,128)(2,1)S(1)}, u32[]{:S(2)}, u32[]{:S(2)}) collective-permute-start(bf16[1,2,96,768]{3,2,1,0:T(8,128)(2,1)S(1)} %pad_maximum_fusion.9), channel_id=1, source_target_pairs={{0,1},{1,0},{2,3},{3,2},{4,5},{5,4},{6,7},{7,6},{8,9},{9,8},{10,11... | collective-permute-start | bytes 884744 | tf_op jit(solution)/shard_map/ppermute | solution.py:50
  78.9 8.3 %collective-permute-start.23 = (bf16[1,96,768]{2,1,0:T(8,128)(2,1)S(1)}, bf16[1,96,768]{2,1,0:T(8,128)(2,1)S(1)}, u32[]{:S(2)}, u32[]{:S(2)}) collective-permute-start(bf16[1,96,768]{2,1,0:T(8,128)(2,1)S(1)} %get-tuple-element.37), channel_id=1, source_target_pairs={{0,2},{1,3},{2,0},{3,1},{4,6},{5,7},{6,4},{7,5},{8,10},{9,11},{10,... | collective-permute-start | bytes 442376 | tf_op jit(solution)/shard_map/ppermute | solution.py:46
  81.3 10.6 %collective-permute-start.16 = (bf16[2,96,768]{2,1,0:T(8,128)(2,1)S(1)}, bf16[2,96,768]{2,1,0:T(8,128)(2,1)S(1)}, u32[]{:S(2)}, u32[]{:S(2)}) collective-permute-start(bf16[2,96,768]{2,1,0:T(8,128)(2,1)S(1)} %fusion.47), channel_id=1, source_target_pairs={{0,2},{1,3},{2,0},{3,1},{4,6},{5,7},{6,4},{7,5},{8,10},{9,11},{10,... | collective-permute-start | bytes 884744 | tf_op jit(solution)/shard_map/ppermute | solution.py:46
  87.2 7.0 %collective-permute-start.24 = (bf16[1,2,96,768]{3,2,1,0:T(8,128)(2,1)S(1)}, bf16[1,2,96,768]{3,2,1,0:T(8,128)(2,1)S(1)}, u32[]{:S(2)}, u32[]{:S(2)}) collective-permute-start(bf16[1,2,96,768]{3,2,1,0:T(8,128)(2,1)S(1)} %pad_maximum_fusion.8), channel_id=1, source_target_pairs={{0,1},{1,0},{2,3},{3,2},{4,5},{5,4},{6,7},{7,6},{8,9},{9,8},{10,11... | collective-permute-start | bytes 884744 | tf_op jit(solution)/shard_map/ppermute | solution.py:50
  92.4 9.1 %collective-permute-start.27 = (bf16[2,96,768]{2,1,0:T(8,128)(2,1)S(1)}, bf16[2,96,768]{2,1,0:T(8,128)(2,1)S(1)}, u32[]{:S(2)}, u32[]{:S(2)}) collective-permute-start(bf16[2,96,768]{2,1,0:T(8,128)(2,1)S(1)} %get-tuple-element.33), channel_id=1, source_target_pairs={{0,2},{1,3},{2,0},{3,1},{4,6},{5,7},{6,4},{7,5},{8,10},{9,11},{10,... | collective-permute-start | bytes 884744 | tf_op jit(solution)/shard_map/ppermute | solution.py:46
  101.6 4.2 %collective-permute-start.28 = (bf16[2,2,96,768]{3,2,1,0:T(8,128)(2,1)S(1)}, bf16[2,2,96,768]{3,2,1,0:T(8,128)(2,1)S(1)}, u32[]{:S(2)}, u32[]{:S(2)}) collective-permute-start(bf16[2,2,96,768]{3,2,1,0:T(8,128)(2,1)S(1)} %pad_maximum_fusion.4), channel_id=1, source_target_pairs={{0,1},{1,0},{2,3},{3,2},{4,5},{5,4},{6,7},{7,6},{8,9},{9,8},{10,11... | collective-permute-start | bytes 1769480 | tf_op jit(solution)/shard_map/ppermute | solution.py:50
  102.6 10.7 %collective-permute-start.25 = (bf16[96,1536]{1,0:T(8,128)(2,1)S(1)}, bf16[96,1536]{1,0:T(8,128)(2,1)S(1)}, u32[]{:S(2)}, u32[]{:S(2)}) collective-permute-start(bf16[96,1536]{1,0:T(8,128)(2,1)S(1)} %get-tuple-element.58), channel_id=1, source_target_pairs={{12,0},{0,4},{4,8},{8,12},{28,16},{16,20},{20,24},{24,28},{13,1},{... | collective-permute-start | bytes 884744 | tf_op jit(solution)/shard_map/ppermute | solution.py:32
  105.2 10.3 %collective-permute-start.26 = (bf16[96,1536]{1,0:T(8,128)(2,1)S(1)}, bf16[96,1536]{1,0:T(8,128)(2,1)S(1)}, u32[]{:S(2)}, u32[]{:S(2)}) collective-permute-start(bf16[96,1536]{1,0:T(8,128)(2,1)S(1)} %get-tuple-element.57), channel_id=1, source_target_pairs={{4,0},{8,4},{12,8},{0,12},{20,16},{24,20},{28,24},{16,28},{5,1},{9... | collective-permute-start | bytes 884744 | tf_op jit(solution)/shard_map/ppermute | solution.py:32
  106.3 10.4 %collective-permute-start.29 = (bf16[384,384]{1,0:T(8,128)(2,1)S(1)}, bf16[384,384]{1,0:T(8,128)(2,1)S(1)}, u32[]{:S(2)}, u32[]{:S(2)}) collective-permute-start(bf16[384,384]{1,0:T(8,128)(2,1)S(1)} %convolution_convert_fusion.2), channel_id=1, source_target_pairs={{96,0},{0,32},{32,64},{64,96},{97,1},{1,33},{33,65},{65,97},{98,2}... | collective-permute-start | bytes 884744 | tf_op jit(solution)/shard_map/ppermute | solution.py:24
  106.9 9.8 %collective-permute-start.30 = (bf16[384,384]{1,0:T(8,128)(2,1)S(1)}, bf16[384,384]{1,0:T(8,128)(2,1)S(1)}, u32[]{:S(2)}, u32[]{:S(2)}) collective-permute-start(bf16[384,384]{1,0:T(8,128)(2,1)S(1)} %convolution_convert_fusion.1), channel_id=1, source_target_pairs={{32,0},{64,32},{96,64},{0,96},{33,1},{65,33},{97,65},{1,97},{34,2}... | collective-permute-start | bytes 884744 | tf_op jit(solution)/shard_map/ppermute | solution.py:24
  118.5 32.0 %collective-permute-start.31 = (bf16[192,768]{1,0:T(8,128)(2,1)S(1)}, bf16[192,768]{1,0:T(8,128)(2,1)S(1)}, u32[]{:S(2)}, u32[]{:S(2)}) collective-permute-start(bf16[192,768]{1,0:T(8,128)(2,1)S(1)} %get-tuple-element.22), channel_id=1, source_target_pairs={{0,0},{8,1},{18,2},{26,3},{1,4},{9,5},{19,6},{27,7},{5,8},{13,9},{... | collective-permute-start | bytes 884744 | tf_op jit(solution)/shard_map/ppermute | solution.py:159
  124.8 15.3 %collective-permute-start.34 = (bf16[192,1536]{1,0:T(8,128)(2,1)S(1)}, bf16[192,1536]{1,0:T(8,128)(2,1)S(1)}, u32[]{:S(2)}, u32[]{:S(2)}) collective-permute-start(bf16[192,1536]{1,0:T(8,128)(2,1)S(1)} %fusion.1), channel_id=1, source_target_pairs={{12,0},{0,4},{4,8},{8,12},{28,16},{16,20},{20,24},{24,28},{13,1},{... | collective-permute-start | bytes 1769480 | tf_op jit(solution)/shard_map/ppermute | solution.py:32
  124.9 16.0 %collective-permute-start.35 = (bf16[768,384]{1,0:T(8,128)(2,1)S(1)}, bf16[768,384]{1,0:T(8,128)(2,1)S(1)}, u32[]{:S(2)}, u32[]{:S(2)}) collective-permute-start(bf16[768,384]{1,0:T(8,128)(2,1)S(1)} %fusion.4), channel_id=1, source_target_pairs={{96,0},{0,32},{32,64},{64,96},{97,1},{1,33},{33,65},{65,97},{98,2}... | collective-permute-start | bytes 1769480 | tf_op jit(solution)/shard_map/ppermute | solution.py:24
  126.0 18.2 %collective-permute-start.41 = (bf16[768,384]{1,0:T(8,128)(2,1)S(1)}, bf16[768,384]{1,0:T(8,128)(2,1)S(1)}, u32[]{:S(2)}, u32[]{:S(2)}) collective-permute-start(bf16[768,384]{1,0:T(8,128)(2,1)S(1)} %fusion.5), channel_id=1, source_target_pairs={{32,0},{64,32},{96,64},{0,96},{33,1},{65,33},{97,65},{1,97},{34,2}... | collective-permute-start | bytes 1769480 | tf_op jit(solution)/shard_map/ppermute | solution.py:24
  130.3 16.8 %collective-permute-start.37 = (bf16[192,1536]{1,0:T(8,128)(2,1)S(1)}, bf16[192,1536]{1,0:T(8,128)(2,1)S(1)}, u32[]{:S(2)}, u32[]{:S(2)}) collective-permute-start(bf16[192,1536]{1,0:T(8,128)(2,1)S(1)} %fusion.2), channel_id=1, source_target_pairs={{4,0},{8,4},{12,8},{0,12},{20,16},{24,20},{28,24},{16,28},{5,1},{9... | collective-permute-start | bytes 1769480 | tf_op jit(solution)/shard_map/ppermute | solution.py:32
  140.9 33.8 %collective-permute-start.36 = (bf16[192,768]{1,0:T(8,128)(2,1)S(1)}, bf16[192,768]{1,0:T(8,128)(2,1)S(1)}, u32[]{:S(2)}, u32[]{:S(2)}) collective-permute-start(bf16[192,768]{1,0:T(8,128)(2,1)S(1)} %get-tuple-element.23), channel_id=1, source_target_pairs={{5,0},{13,1},{23,2},{31,3},{4,4},{12,5},{22,6},{30,7},{0,8},{8,9},... | collective-permute-start | bytes 884744 | tf_op jit(solution)/shard_map/ppermute | solution.py:159
  145.1 12.4 %collective-permute-start.44 = (bf16[192,384]{1,0:T(8,128)(2,1)S(1)}, bf16[192,384]{1,0:T(8,128)(2,1)S(1)}, u32[]{:S(2)}, u32[]{:S(2)}) collective-permute-start(bf16[192,384]{1,0:T(8,128)(2,1)S(1)} %get-tuple-element.49), channel_id=1, source_target_pairs={{4,0},{8,4},{12,8},{0,12},{20,16},{24,20},{28,24},{16,28},{5,1},{9... | collective-permute-start | bytes 442376 | tf_op jit(solution)/shard_map/ppermute | solution.py:32
  146.9 12.6 %collective-permute-start.43 = (bf16[192,384]{1,0:T(8,128)(2,1)S(1)}, bf16[192,384]{1,0:T(8,128)(2,1)S(1)}, u32[]{:S(2)}, u32[]{:S(2)}) collective-permute-start(bf16[192,384]{1,0:T(8,128)(2,1)S(1)} %get-tuple-element.50), channel_id=1, source_target_pairs={{8,0},{12,4},{0,8},{4,12},{24,16},{28,20},{16,24},{20,28},{9,1},{1... | collective-permute-start | bytes 442376 | tf_op jit(solution)/shard_map/ppermute | solution.py:32
  147.1 14.7 %collective-permute-start.42 = (bf16[192,384]{1,0:T(8,128)(2,1)S(1)}, bf16[192,384]{1,0:T(8,128)(2,1)S(1)}, u32[]{:S(2)}, u32[]{:S(2)}) collective-permute-start(bf16[192,384]{1,0:T(8,128)(2,1)S(1)} %get-tuple-element.48), channel_id=1, source_target_pairs={{12,0},{0,4},{4,8},{8,12},{28,16},{16,20},{20,24},{24,28},{13,1},{... | collective-permute-start | bytes 442376 | tf_op jit(solution)/shard_map/ppermute | solution.py:32
  150.7 11.2 %collective-permute-start.40 = (bf16[192,384]{1,0:T(8,128)(2,1)S(1)}, bf16[192,384]{1,0:T(8,128)(2,1)S(1)}, u32[]{:S(2)}, u32[]{:S(2)}) collective-permute-start(bf16[192,384]{1,0:T(8,128)(2,1)S(1)} %get-tuple-element.42), channel_id=1, source_target_pairs={{32,0},{64,32},{96,64},{0,96},{33,1},{65,33},{97,65},{1,97},{34,2}... | collective-permute-start | bytes 442376 | tf_op jit(solution)/shard_map/ppermute | solution.py:24
  157.5 8.2 %collective-permute-start.39 = (bf16[192,384]{1,0:T(8,128)(2,1)S(1)}, bf16[192,384]{1,0:T(8,128)(2,1)S(1)}, u32[]{:S(2)}, u32[]{:S(2)}) collective-permute-start(bf16[192,384]{1,0:T(8,128)(2,1)S(1)} %get-tuple-element.43), channel_id=1, source_target_pairs={{64,0},{96,32},{0,64},{32,96},{65,1},{97,33},{1,65},{33,97},{66,2}... | collective-permute-start | bytes 442376 | tf_op jit(solution)/shard_map/ppermute | solution.py:24
  159.5 8.6 %collective-permute-start.38 = (bf16[192,384]{1,0:T(8,128)(2,1)S(1)}, bf16[192,384]{1,0:T(8,128)(2,1)S(1)}, u32[]{:S(2)}, u32[]{:S(2)}) collective-permute-start(bf16[192,384]{1,0:T(8,128)(2,1)S(1)} %get-tuple-element.41), channel_id=1, source_target_pairs={{96,0},{0,32},{32,64},{64,96},{97,1},{1,33},{33,65},{65,97},{98,2}... | collective-permute-start | bytes 442376 | tf_op jit(solution)/shard_map/ppermute | solution.py:24
  168.2 5.8 %collective-permute-start.45 = (bf16[192,384]{1,0:T(8,128)(2,1)S(1)}, bf16[192,384]{1,0:T(8,128)(2,1)S(1)}, u32[]{:S(2)}, u32[]{:S(2)}) collective-permute-start(bf16[192,384]{1,0:T(8,128)(2,1)S(1)} %pad_maximum_fusion.12), channel_id=1, source_target_pairs={{0,16},{4,20},{8,24},{12,28},{16,0},{20,4},{24,8},{28,12},{1,17},{... | collective-permute-start | bytes 442376 | tf_op jit(solution)/shard_map/ppermute | solution.py:42
  (1 other events, 5.8 us)

commit v3 on v2

v3 whole, which is shorter than its diff:
```python
import jax
import jax.numpy as jnp
from jax import lax
from jax.sharding import PartitionSpec as P

coef_root = 0.7978845608028654
coef_cube = 0.044715
bf16, f32 = jnp.bfloat16, jnp.float32

N_RING = 4
BOTH = ("ja", "ka")


def gelu_pair(hidden):
    tanh_value = jnp.tanh(coef_root * (hidden + coef_cube * hidden * hidden * hidden))
    activ = 0.5 * hidden * (1.0 + tanh_value)
    derivative = 0.5 * (1.0 + tanh_value) + 0.5 * hidden * (
        1.0 - tanh_value * tanh_value
    ) * coef_root * (1.0 + 3.0 * coef_cube * hidden * hidden)
    return (activ, derivative)


def from_x(v, r):
    return lax.ppermute(v, "ia", [((i + r) % N_RING, i) for i in range(N_RING)])


def to_x(v, r):
    return from_x(v, N_RING - r)


def from_z(v, r):
    return lax.ppermute(
        v, "ja", [(y * 4 + (z + r) % N_RING, y * 4 + z) for y in range(2) for z in range(N_RING)]
    )


def to_z(v, r):
    return from_z(v, N_RING - r)


def swap_y_lo(v):
    return lax.ppermute(v, "ja", [(j, j ^ 4) for j in range(8)])


def swap_y_hi(v):
    return lax.ppermute(v, "ka", [(k, k ^ 2) for k in range(4)])


def swap_core(v):
    return lax.ppermute(v, "ka", [(k, k ^ 1) for k in range(4)])


def exchange_pairs(turn):
    pairs = []
    for y_lo in range(2):
        for z in range(4):
            for y_hi in range(2):
                for core in range(2):
                    half = turn ^ (z // 2)
                    to_ja = y_hi * 4 + 2 * core + half
                    to_ka = (y_hi ^ y_lo ^ core) * 2 + ((z % 2) ^ half)
                    pairs.append(((y_lo * 4 + z) * 4 + y_hi * 2 + core, to_ja * 4 + to_ka))
    return pairs


def dot(a, b, dims=(1, 0)):
    return lax.dot_general(
        a, b, (((dims[0],), (dims[1],)), ((), ())), preferred_element_type=f32
    )


def after_done(v, *arrived):
    return lax.optimization_barrier((v, *arrived))[0]


def together(*arrays):
    return lax.optimization_barrier(arrays)


def pick(index, first, second):
    return jnp.where(index == 0, first, second)


def on_device(tokens, weight, grad_out):
    rows, cols = tokens.shape
    half = rows // 2
    units = weight.shape[1]
    x = lax.axis_index("ia")
    z = lax.axis_index("ja") % 4
    z_hi, z_lo = z // 2, z % 2
    y_hi, core = lax.axis_index("ka") // 2, lax.axis_index("ka") % 2
    y_rows = y_hi ^ z_hi

    left, right = grad_out[:, :units], grad_out[:, units:]
    piece0, piece1 = pick(z_hi, left, right), pick(z_hi, right, left)

    other = swap_y_lo(tokens)
    tok_a = jnp.concatenate([tokens[:half], other[:half]], 0)
    tok_b = jnp.concatenate([tokens[half:], other[half:]], 0)
    b2, b1, b3 = (from_z(tok_b, r) for r in (2, 1, 3))
    a2, a1, a3 = (from_x(tok_a, r) for r in (2, 1, 3))
    a1, a2, a3, b1, b2, b3 = together(a1, a2, a3, b1, b2, b3)
    a0 = jnp.concatenate([tok_a, a1, a2, a3], 1)
    b0 = jnp.concatenate([tok_b, b2, b1, b3], 0)
    n = 2 * half

    held = after_done(weight, a0, b0)
    w = [lax.dynamic_slice_in_dim(held, ((x + r) % N_RING) * cols, cols, 0) for r in range(4)]
    turned = jnp.concatenate(w, 0)
    w = [turned[r * cols : (r + 1) * cols] for r in range(4)]

    sent0 = lax.ppermute(after_done(piece0, a0, b0), BOTH, exchange_pairs(0))
    a1, a3 = from_z(a0, 1), from_z(a0, 3)
    b1, b3 = from_x(b0, 1), from_x(b0, 3)
    a1, a3, b1, b3, sent0 = together(a1, a3, b1, b3, sent0)
    a2_first, a2_second = from_z(a1[:half], 1), from_z(a3[half:], 3)
    b2_first, b2_second = from_x(b1[: 2 * n], 1), from_x(b3[2 * n :], 3)
    early = dot(b0, w[0]) + dot(b1, w[1]) + dot(b3, w[3])
    sent1 = lax.ppermute(after_done(piece1, early), BOTH, exchange_pairs(1))
    a2_first, a2_second, b2_first, b2_second, sent1 = together(
        a2_first, a2_second, b2_first, b2_second, sent1
    )
    a2 = jnp.concatenate([a2_first, a2_second], 0)

    def over_core(first, second):
        got = swap_core(pick(core, second, first).astype(bf16))
        return (pick(core, first, second) + got.astype(f32)).reshape(-1, 2, half, units)

    def over_y(summed, *arrived):
        away = after_done(pick(y_rows, summed[:, 1], summed[:, 0]).astype(bf16), *arrived)
        return pick(y_rows, summed[:, 0], summed[:, 1]) + swap_y_hi(away).astype(f32)

    def gelu(hidden, go):
        activ, derivative = gelu_pair(hidden)
        grad = (go.reshape(hidden.shape).astype(f32) * derivative).astype(bf16)
        return activ.astype(bf16), grad

    def back_core(grad, there):
        grad = jnp.concatenate(
            [v[i] for i in range(grad.shape[0]) for v in (pick(y_rows, grad, there), pick(y_rows, there, grad))], 0
        )
        there = swap_core(grad)
        return pick(core, grad, there), pick(core, there, grad)

    k0 = z_lo ^ z_hi ^ (core & z_lo)
    go0, go1 = pick(k0, sent0, sent1), pick(k0, sent1, sent0)

    first, second = [dot(a0, turned), dot(a2, turned)], [dot(a1, turned), dot(a3, turned)]
    summed_a = over_core(jnp.concatenate(first, 0), jnp.concatenate(second, 0))
    summed_b = over_core(
        early[: 2 * n] + dot(b2_first, w[2]), early[2 * n :] + dot(b2_second, w[2])
    )
    hidden_a, hidden_b = over_y(summed_a), over_y(summed_b)
    act_a, gr_a = gelu(hidden_a, jnp.concatenate([go0[:half], go1[:half]], 0))
    act_b, gr_b = gelu(hidden_b, jnp.concatenate([go0[half:], go1[half:]], 0))
    there_a, there_b = swap_y_hi(gr_a), swap_y_hi(gr_b)

    first, second = back_core(gr_a, there_a)
    g0, g2, g1, g3 = first[:n], first[n:], second[:n], second[n:]
    gb0, gb1 = back_core(gr_b, there_b)

    d2 = dot(g2, turned, (1, 1)).astype(bf16)
    c2_first, c2_second = dot(gb0, w[2], (1, 1)).astype(bf16), dot(gb1, w[2], (1, 1)).astype(bf16)
    up_a, down_a = to_z(d2[:half], 1), to_z(d2[half:], 3)
    up_b, down_b = to_x(c2_first, 1), to_x(c2_second, 3)

    def before(v, extra):
        return jnp.pad(v, ((0, extra), (0, 0))).astype(f32)

    def after(v, extra):
        return jnp.pad(v, ((extra, 0), (0, 0))).astype(f32)

    gb = jnp.concatenate(together(gb0, gb1, d2, c2_first, c2_second)[:2], 0)
    held0 = jnp.concatenate([act_a[0], act_b[0]], 0)
    held1 = jnp.concatenate([act_a[1], act_b[1]], 0)

    def give_back(turn, *arrived):
        piece = after_done(pick(k0 ^ turn, held0, held1), *arrived)
        return lax.ppermute(piece, BOTH, [(t, s) for s, t in exchange_pairs(turn)])

    back0 = give_back(0, d2, c2_first, c2_second)
    up_a, down_a, up_b, down_b, back0 = together(up_a, down_a, up_b, down_b, back0)
    d1 = (dot(g1, turned, (1, 1)) + before(up_a, half)).astype(bf16)
    d3 = (dot(g3, turned, (1, 1)) + after(down_a, half)).astype(bf16)
    c1 = (dot(gb, w[1], (1, 1)) + before(up_b, 2 * n)).astype(bf16)
    c3 = (dot(gb, w[3], (1, 1)) + after(down_b, 2 * n)).astype(bf16)
    added = (d1, d3, c1, c3)
    d1, d3, c1, c3 = to_z(d1, 1), to_z(d3, 3), to_x(c1, 1), to_x(c3, 3)
    d1, d3, c1, c3 = together(d1, d3, c1, c3)
    part_a = dot(g0, turned, (1, 1)) + d1.astype(f32) + d3.astype(f32)
    part_b = dot(gb, w[0], (1, 1)) + c1.astype(f32) + c3.astype(f32)

    ga = after_done(jnp.concatenate([g0, g1, g2, g3], 0), *added)
    gb = after_done(gb, d1, c1)
    all_a = jnp.concatenate([a0, a1, a2, a3], 0)
    b2 = jnp.concatenate([b2_first, b2_second], 0)
    blocks = []
    for r, b in enumerate((b0, b1, b2, b3)):
        block = dot(all_a[:, r * cols : (r + 1) * cols], ga, (0, 0)) + dot(b, gb, (0, 0))
        blocks.append(block.astype(bf16))

    back1 = give_back(1, *added)
    grad_weight = jnp.zeros_like(weight)
    for r in range(4):
        grad_weight = lax.dynamic_update_slice_in_dim(
            grad_weight, blocks[r], ((x + r) % N_RING) * cols, 0
        )

    part_a, part_b, back1 = together(part_a, part_b, back1)

    def split_sum(parts, send):
        got = {r: send(parts[r].astype(bf16), r) for r in (2, 1, 3)}
        return parts[0] + got[1].astype(f32) + got[2].astype(f32) + got[3].astype(f32)

    part_a = split_sum([part_a[:, r * cols : (r + 1) * cols] for r in range(4)], to_x)
    part_b = split_sum([part_b[i * n : (i + 1) * n] for i in (0, 2, 1, 3)], to_z)
    got = swap_y_lo(jnp.concatenate([part_a[half:], part_b[half:]], 0).astype(bf16))
    grad_input = jnp.concatenate([part_a[:half], part_b[:half]], 0) + got.astype(f32)

    activated = jnp.concatenate([pick(z_hi, back0, back1), pick(z_hi, back1, back0)], 1)

    return (activated, grad_input.astype(bf16), grad_weight)


def solution(mesh):
    placed = (P("ja", ("ka", "ia")), P("ka", ("ia", "ja")), P("ja", ("ia", "ka")))
    return jax.shard_map(
        on_device,
        mesh=mesh,
        in_specs=placed,
        out_specs=(P("ja", ("ia", "ka")), P("ja", ("ka", "ia")), P("ka", ("ia", "ja"))),
        check_vma=False,
    )
```

time: 176 us -> 164 us (0.932)
  starting transfers between devices: 78.8 us -> 64.2 us
    ppermute x2, waiting for transfers between devices: 2.45 us -> 14.8 us  [the longest x1 10.3 us: on_device(): sent0 = lax.ppermute(after_done(piece0, a0, b0), BOTH, exchange_pairs(0))]
    ppermute x6 -> x4, starting transfers between devices: 11.3 us -> 2.89 us  [swap_y_hi(): return lax.ppermute(v, 'ka', [(k, k ^ 2) for k in range(4)])]
    ppermute x14, starting transfers between devices: 27.4 us -> 19.4 us  [from_x(): return lax.ppermute(v, 'ia', [((i + r) % N_RING, i) for i in range(N_RING)])]
    ppermute x14, waiting for transfers between devices: 15.1 us -> 10.5 us  [from_z(): lax.ppermute(v, 'ja', [(y * 4 + (z + r) % N_RING, y * 4 + z) for y in ran...]
    ppermute x14, starting transfers between devices: 20.8 us -> 25 us  [from_z(): lax.ppermute(v, 'ja', [(y * 4 + (z + r) % N_RING, y * 4 + z) for y in ran...]
    ppermute x6 -> x4, waiting for transfers between devices: 27.8 us -> 23.8 us  [swap_y_hi(): return lax.ppermute(v, 'ka', [(k, k ^ 2) for k in range(4)])]
    ppermute x14, waiting for transfers between devices: 15.9 us -> 12.7 us  [from_x(): return lax.ppermute(v, 'ia', [((i + r) % N_RING, i) for i in range(N_RING)])]
    ppermute x2, waiting for transfers between devices: 9.38 us -> 7.43 us  [swap_y_lo(): return lax.ppermute(v, 'ja', [(j, j ^ 4) for j in range(8)])]
  transfers between devices with their start and end apart: 46 -> 42, of which waited for: 20 -> 24; matrix products, arithmetic and copies ran while one was open for 12% -> 13% of each run, Pallas kernels for 0% -> 0%
where the time goes in v3:
time: 164 us; the launch traced here: 162 us
  waiting for transfers between devices  71.1 us (43%)
  starting transfers between devices  64.2 us (39%)
  matrix products  18.2 us (11%)
  other arithmetic  5.2 us (3%)
  local copies, waits for them, and re-layouts  2.17 us (1%)
    ppermute x14, starting transfers between devices, from_z(): lax.ppermute(v, 'ja', [(y * 4 + (z + r) % N_RING, y * 4 + z) for y in ran...  25 us
    ppermute x4, waiting for transfers between devices, swap_y_hi(): return lax.ppermute(v, 'ka', [(k, k ^ 2) for k in range(4)])  23.8 us
    ppermute x14, starting transfers between devices, from_x(): return lax.ppermute(v, 'ia', [((i + r) % N_RING, i) for i in range(N_RING)])  19.4 us
    dot_general x26, matrix products, dot(): lax.dot_general(a, b, (((dims[0],), (dims[1],)), ((), ())), preferred_ele...  18.2 us
    ppermute x14, waiting for transfers between devices, from_x(): return lax.ppermute(v, 'ia', [((i + r) % N_RING, i) for i in range(N_RING)])  12.7 us
    ppermute x14, waiting for transfers between devices, from_z(): lax.ppermute(v, 'ja', [(y * 4 + (z + r) % N_RING, y * 4 + z) for y in ran...  10.5 us
    ppermute x1, waiting for transfers between devices, on_device(): sent0 = lax.ppermute(after_done(piece0, a0, b0), BOTH, exchange_pairs(0))  10.3 us
    ppermute x2, starting transfers between devices, give_back(): return lax.ppermute(piece, BOTH, [(t, s) for s, t in exchange_pairs(turn)])  7.87 us
  transfers between devices with their start and end apart: 42, of which 24 were waited for; matrix products, arithmetic and copies ran while one was open for 13% of the time, Pallas kernels for 0%

profile of v3, /device:TPU:40, one launch (start us, length us, event | category | flops | bytes accessed | tf_op | source)
XLA Modules:
  0.0 162.2 jit_solution(13532816645904923599)
XLA Ops:
  1.2 1.0 constant_dynamic-update-slice_fusion.4
  2.1 4.4 %collective-permute-done = bf16[192,384]{1,0:T(8,128)(2,1)S(1)} collective-permute-done((bf16[192,384]{1,0:T(8,128)(2,1)}, bf16[192,384]{1,0:T(8,128)(2,1)S(1)}, u32[]{:S(2)}, u32[]{:S(2)}) %collective-permute-start) | collective-permute-done | bytes 147488 | tf_op jit(solution)/shard_map/ppermute | solution.py:42
  6.6 2.8 %collective-permute-start.1 = (bf16[192,384]{1,0:T(8,128)(2,1)S(1)}, bf16[192,384]{1,0:T(8,128)(2,1)S(1)}, u32[]{:S(2)}, u32[]{:S(2)}) collective-permute-start(bf16[192,384]{1,0:T(8,128)(2,1)S(1)} %pad_maximum_fusion.17), channel_id=1, source_target_pairs={{32,0},{64,32},{96,64},{0,96},{33,1},{65,33},{97,65},{1,97},{34,2}... | collective-permute-start | bytes 442376 | tf_op jit(solution)/shard_map/ppermute | solution.py:24
  10.2 0.9 collective-permute-start.3
  11.3 3.3 %collective-permute-start.5 = (bf16[192,384]{1,0:T(8,128)(2,1)S(1)}, bf16[192,384]{1,0:T(8,128)(2,1)S(1)}, u32[]{:S(2)}, u32[]{:S(2)}) collective-permute-start(bf16[192,384]{1,0:T(8,128)(2,1)S(1)} %pad_maximum_fusion.18), channel_id=1, source_target_pairs={{8,0},{12,4},{0,8},{4,12},{24,16},{28,20},{16,24},{20,28},{9,1},{1... | collective-permute-start | bytes 442376 | tf_op jit(solution)/shard_map/ppermute | solution.py:32
  14.8 2.0 %collective-permute-start.6 = (bf16[192,384]{1,0:T(8,128)(2,1)S(1)}, bf16[192,384]{1,0:T(8,128)(2,1)S(1)}, u32[]{:S(2)}, u32[]{:S(2)}) collective-permute-start(bf16[192,384]{1,0:T(8,128)(2,1)S(1)} %pad_maximum_fusion.18), channel_id=1, source_target_pairs={{12,0},{0,4},{4,8},{8,12},{28,16},{16,20},{20,24},{24,28},{13,1},{... | collective-permute-start | bytes 442376 | tf_op jit(solution)/shard_map/ppermute | solution.py:32
  17.0 1.5 collective-permute-done.3
  18.5 1.1 collective-permute-done.5
  20.4 3.4 %collective-permute-start.7 = (bf16[192,1536]{1,0:T(8,128)(2,1)S(1)}, bf16[192,1536]{1,0:T(8,128)(2,1)S(1)}, u32[]{:S(2)}, u32[]{:S(2)}) collective-permute-start(bf16[192,1536]{1,0:T(8,128)(2,1)S(1)} %get-tuple-element.114), channel_id=1, source_target_pairs={{4,0},{8,4},{12,8},{0,12},{20,16},{24,20},{28,24},{16,28},{5,1},{9... | collective-permute-start | bytes 1769480 | tf_op jit(solution)/shard_map/ppermute | solution.py:32
  23.9 2.5 %collective-permute-start.9 = (bf16[768,384]{1,0:T(8,128)(2,1)S(1)}, bf16[768,384]{1,0:T(8,128)(2,1)S(1)}, u32[]{:S(2)}, u32[]{:S(2)}) collective-permute-start(bf16[768,384]{1,0:T(8,128)(2,1)S(1)} %constant_dynamic-update-slice_fusion), channel_id=1, source_target_pairs={{32,0},{64,32},{96,64},{0,96},{33,1},{65,33},{97,65},{1,97},{34,2}... | collective-permute-start | bytes 1769480 | tf_op jit(solution)/shard_map/ppermute | solution.py:24
  26.4 1.9 %collective-permute-start.11 = (bf16[192,768]{1,0:T(8,128)(2,1)S(1)}, bf16[192,768]{1,0:T(8,128)(2,1)S(1)}, u32[]{:S(2)}, u32[]{:S(2)}) collective-permute-start(bf16[192,768]{1,0:T(8,128)(2,1)S(1)} %get-tuple-element.46), channel_id=1, source_target_pairs={{0,0},{1,10},{2,18},{3,24},{4,1},{5,11},{6,19},{7,25},{8,5},{9,15}... | collective-permute-start | bytes 884744 | tf_op jit(solution)/shard_map/ppermute | solution.py:112
  30.1 10.3 %collective-permute-done.11 = bf16[192,768]{1,0:T(8,128)(2,1)S(1)} collective-permute-done((bf16[192,768]{1,0:T(8,128)(2,1)S(1)}, bf16[192,768]{1,0:T(8,128)(2,1)S(1)}, u32[]{:S(2)}, u32[]{:S(2)}) %collective-permute-start.11) | collective-permute-done | bytes 294944 | tf_op jit(solution)/shard_map/ppermute | solution.py:112
  42.1 2.1 %collective-permute-start.13 = (bf16[96,1536]{1,0:T(8,128)(2,1)S(1)}, bf16[96,1536]{1,0:T(8,128)(2,1)S(1)}, u32[]{:S(2)}, u32[]{:S(2)}) collective-permute-start(bf16[96,1536]{1,0:T(8,128)(2,1)S(1)} %slice.181), channel_id=1, source_target_pairs={{12,0},{0,4},{4,8},{8,12},{28,16},{16,20},{20,24},{24,28},{13,1},{... | collective-permute-start | bytes 884744 | tf_op jit(solution)/shard_map/ppermute | solution.py:32
  44.2 3.2 %collective-permute-start.14 = (bf16[384,384]{1,0:T(8,128)(2,1)S(1)}, bf16[384,384]{1,0:T(8,128)(2,1)S(1)}, u32[]{:S(2)}, u32[]{:S(2)}) collective-permute-start(bf16[384,384]{1,0:T(8,128)(2,1)S(1)} %slice.182), channel_id=1, source_target_pairs={{32,0},{64,32},{96,64},{0,96},{33,1},{65,33},{97,65},{1,97},{34,2}... | collective-permute-start | bytes 884744 | tf_op jit(solution)/shard_map/ppermute | solution.py:24
  48.3 4.3 %collective-permute-start.16 = (bf16[192,768]{1,0:T(8,128)(2,1)S(1)}, bf16[192,768]{1,0:T(8,128)(2,1)S(1)}, u32[]{:S(2)}, u32[]{:S(2)}) collective-permute-start(bf16[192,768]{1,0:T(8,128)(2,1)S(1)} %get-tuple-element.53), channel_id=1, source_target_pairs={{0,5},{1,15},{2,23},{3,29},{4,4},{5,14},{6,22},{7,28},{8,0},{9,10}... | collective-permute-start | bytes 884744 | tf_op jit(solution)/shard_map/ppermute | solution.py:119
  53.3 2.1 %collective-permute-done.15 = bf16[384,384]{1,0:T(8,128)(2,1)S(1)} collective-permute-done((bf16[384,384]{1,0:T(8,128)(2,1)S(1)}, bf16[384,384]{1,0:T(8,128)(2,1)S(1)}, u32[]{:S(2)}, u32[]{:S(2)}) %collective-permute-start.15) | collective-permute-done | bytes 294944 | tf_op jit(solution)/shard_map/ppermute | solution.py:24
  55.4 4.6 %collective-permute-done.16 = bf16[192,768]{1,0:T(8,128)(2,1)S(1)} collective-permute-done((bf16[192,768]{1,0:T(8,128)(2,1)S(1)}, bf16[192,768]{1,0:T(8,128)(2,1)S(1)}, u32[]{:S(2)}, u32[]{:S(2)}) %collective-permute-start.16) | collective-permute-done | bytes 294944 | tf_op jit(solution)/shard_map/ppermute | solution.py:119
  63.3 1.0 collective-permute-done.23
  64.7 2.6 %collective-permute-start.24 = (bf16[2,96,768]{2,1,0:T(8,128)(2,1)S(1)}, bf16[2,96,768]{2,1,0:T(8,128)(2,1)S(1)}, u32[]{:S(2)}, u32[]{:S(2)}) collective-permute-start(bf16[2,96,768]{2,1,0:T(8,128)(2,1)S(1)} %fusion.42), channel_id=1, source_target_pairs={{0,2},{1,3},{2,0},{3,1},{4,6},{5,7},{6,4},{7,5},{8,10},{9,11},{10,... | collective-permute-start | bytes 884744 | tf_op jit(solution)/shard_map/ppermute | solution.py:46
  67.4 7.3 %collective-permute-done.18 = bf16[2,96,768]{2,1,0:T(8,128)(2,1)S(1)} collective-permute-done((bf16[2,96,768]{2,1,0:T(8,128)(2,1)S(1)}, bf16[2,96,768]{2,1,0:T(8,128)(2,1)S(1)}, u32[]{:S(2)}, u32[]{:S(2)}) %collective-permute-start.18) | collective-permute-done | bytes 294944 | tf_op jit(solution)/shard_map/ppermute | solution.py:46
  75.2 5.7 %collective-permute-done.24 = bf16[2,96,768]{2,1,0:T(8,128)(2,1)S(1)} collective-permute-done((bf16[2,96,768]{2,1,0:T(8,128)(2,1)S(1)}, bf16[2,96,768]{2,1,0:T(8,128)(2,1)S(1)}, u32[]{:S(2)}, u32[]{:S(2)}) %collective-permute-start.24) | collective-permute-done | bytes 294944 | tf_op jit(solution)/shard_map/ppermute | solution.py:46
  81.7 5.6 %collective-permute-done.19 = bf16[2,96,768]{2,1,0:T(8,128)(2,1)S(1)} collective-permute-done((bf16[2,96,768]{2,1,0:T(8,128)(2,1)S(1)}, bf16[2,96,768]{2,1,0:T(8,128)(2,1)S(1)}, u32[]{:S(2)}, u32[]{:S(2)}) %collective-permute-start.19) | collective-permute-done | bytes 294944 | tf_op jit(solution)/shard_map/ppermute | solution.py:46
  87.5 5.3 %collective-permute-done.25 = bf16[2,96,768]{2,1,0:T(8,128)(2,1)S(1)} collective-permute-done((bf16[2,96,768]{2,1,0:T(8,128)(2,1)S(1)}, bf16[2,96,768]{2,1,0:T(8,128)(2,1)S(1)}, u32[]{:S(2)}, u32[]{:S(2)}) %collective-permute-start.25) | collective-permute-done | bytes 294944 | tf_op jit(solution)/shard_map/ppermute | solution.py:46
  93.3 0.9 convolution_convert_fusion
  96.3 3.3 %collective-permute-start.28 = (bf16[384,384]{1,0:T(8,128)(2,1)S(1)}, bf16[384,384]{1,0:T(8,128)(2,1)S(1)}, u32[]{:S(2)}, u32[]{:S(2)}) collective-permute-start(bf16[384,384]{1,0:T(8,128)(2,1)S(1)} %convolution_convert_fusion.1), channel_id=1, source_target_pairs={{32,0},{64,32},{96,64},{0,96},{33,1},{65,33},{97,65},{1,97},{34,2}... | collective-permute-start | bytes 884744 | tf_op jit(solution)/shard_map/ppermute | solution.py:24
  99.7 1.5 collective-permute-start.21
  101.2 1.7 %collective-permute-start.22 = (bf16[96,1536]{1,0:T(8,128)(2,1)S(1)}, bf16[96,1536]{1,0:T(8,128)(2,1)S(1)}, u32[]{:S(2)}, u32[]{:S(2)}) collective-permute-start(bf16[96,1536]{1,0:T(8,128)(2,1)S(1)} %get-tuple-element.105), channel_id=1, source_target_pairs={{4,0},{8,4},{12,8},{0,12},{20,16},{24,20},{28,24},{16,28},{5,1},{9... | collective-permute-start | bytes 884744 | tf_op jit(solution)/shard_map/ppermute | solution.py:32
  102.9 5.1 %collective-permute-start.29 = (bf16[192,768]{1,0:T(8,128)(2,1)S(1)}, bf16[192,768]{1,0:T(8,128)(2,1)S(1)}, u32[]{:S(2)}, u32[]{:S(2)}) collective-permute-start(bf16[192,768]{1,0:T(8,128)(2,1)S(1)} %get-tuple-element.59), channel_id=1, source_target_pairs={{0,0},{10,1},{18,2},{24,3},{1,4},{11,5},{19,6},{25,7},{5,8},{15,9}... | collective-permute-start | bytes 884744 | tf_op jit(solution)/shard_map/ppermute | solution.py:179
  109.0 2.3 %collective-permute-done.21 = bf16[96,1536]{1,0:T(8,128)(2,1)S(1)} collective-permute-done((bf16[96,1536]{1,0:T(8,128)(2,1)S(1)}, bf16[96,1536]{1,0:T(8,128)(2,1)S(1)}, u32[]{:S(2)}, u32[]{:S(2)}) %collective-permute-start.21) | collective-permute-done | bytes 294944 | tf_op jit(solution)/shard_map/ppermute | solution.py:32
  111.3 3.4 %collective-permute-done.22 = bf16[96,1536]{1,0:T(8,128)(2,1)S(1)} collective-permute-done((bf16[96,1536]{1,0:T(8,128)(2,1)S(1)}, bf16[96,1536]{1,0:T(8,128)(2,1)S(1)}, u32[]{:S(2)}, u32[]{:S(2)}) %collective-permute-start.22) | collective-permute-done | bytes 294944 | tf_op jit(solution)/shard_map/ppermute | solution.py:32
  114.8 0.9 fusion.1
  115.7 1.8 %collective-permute-start.30 = (bf16[192,1536]{1,0:T(8,128)(2,1)S(1)}, bf16[192,1536]{1,0:T(8,128)(2,1)S(1)}, u32[]{:S(2)}, u32[]{:S(2)}) collective-permute-start(bf16[192,1536]{1,0:T(8,128)(2,1)S(1)} %fusion.1), channel_id=1, source_target_pairs={{12,0},{0,4},{4,8},{8,12},{28,16},{16,20},{20,24},{24,28},{13,1},{... | collective-permute-start | bytes 1769480 | tf_op jit(solution)/shard_map/ppermute | solution.py:32
  117.5 0.9 fusion.2
  120.5 3.5 %collective-permute-start.33 = (bf16[768,384]{1,0:T(8,128)(2,1)S(1)}, bf16[768,384]{1,0:T(8,128)(2,1)S(1)}, u32[]{:S(2)}, u32[]{:S(2)}) collective-permute-start(bf16[768,384]{1,0:T(8,128)(2,1)S(1)} %add_convert_fusion), channel_id=1, source_target_pairs={{32,0},{64,32},{96,64},{0,96},{33,1},{65,33},{97,65},{1,97},{34,2}... | collective-permute-start | bytes 1769480 | tf_op jit(solution)/shard_map/ppermute | solution.py:24
  125.3 2.8 %collective-permute-start.34 = (bf16[192,768]{1,0:T(8,128)(2,1)S(1)}, bf16[192,768]{1,0:T(8,128)(2,1)S(1)}, u32[]{:S(2)}, u32[]{:S(2)}) collective-permute-start(bf16[192,768]{1,0:T(8,128)(2,1)S(1)} %get-tuple-element.71), channel_id=1, source_target_pairs={{5,0},{15,1},{23,2},{29,3},{4,4},{14,5},{22,6},{28,7},{0,8},{10,9}... | collective-permute-start | bytes 884744 | tf_op jit(solution)/shard_map/ppermute | solution.py:179
  129.5 0.9 collective-permute-done.30
  130.4 2.0 %collective-permute-done.31 = bf16[192,1536]{1,0:T(8,128)(2,1)S(1)} collective-permute-done((bf16[192,1536]{1,0:T(8,128)(2,1)S(1)}, bf16[192,1536]{1,0:T(8,128)(2,1)S(1)}, u32[]{:S(2)}, u32[]{:S(2)}) %collective-permute-start.31) | collective-permute-done | bytes 589856 | tf_op jit(solution)/shard_map/ppermute | solution.py:32
  132.4 2.6 %collective-permute-done.32 = bf16[768,384]{1,0:T(8,128)(2,1)S(1)} collective-permute-done((bf16[768,384]{1,0:T(8,128)(2,1)S(1)}, bf16[768,384]{1,0:T(8,128)(2,1)S(1)}, u32[]{:S(2)}, u32[]{:S(2)}) %collective-permute-start.32) | collective-permute-done | bytes 589856 | tf_op jit(solution)/shard_map/ppermute | solution.py:24
  135.3 0.9 fusion
  136.6 3.7 %collective-permute-start.40 = (bf16[192,384]{1,0:T(8,128)(2,1)S(1)}, bf16[192,384]{1,0:T(8,128)(2,1)S(1)}, u32[]{:S(2)}, u32[]{:S(2)}) collective-permute-start(bf16[192,384]{1,0:T(8,128)(2,1)S(1)} %get-tuple-element.97), channel_id=1, source_target_pairs={{4,0},{8,4},{12,8},{0,12},{20,16},{24,20},{28,24},{16,28},{5,1},{9... | collective-permute-start | bytes 442376 | tf_op jit(solution)/shard_map/ppermute | solution.py:32
  140.3 3.0 %collective-permute-start.39 = (bf16[192,384]{1,0:T(8,128)(2,1)S(1)}, bf16[192,384]{1,0:T(8,128)(2,1)S(1)}, u32[]{:S(2)}, u32[]{:S(2)}) collective-permute-start(bf16[192,384]{1,0:T(8,128)(2,1)S(1)} %get-tuple-element.98), channel_id=1, source_target_pairs={{8,0},{12,4},{0,8},{4,12},{24,16},{28,20},{16,24},{20,28},{9,1},{1... | collective-permute-start | bytes 442376 | tf_op jit(solution)/shard_map/ppermute | solution.py:32
  143.4 1.7 %collective-permute-start.38 = (bf16[192,384]{1,0:T(8,128)(2,1)S(1)}, bf16[192,384]{1,0:T(8,128)(2,1)S(1)}, u32[]{:S(2)}, u32[]{:S(2)}) collective-permute-start(bf16[192,384]{1,0:T(8,128)(2,1)S(1)} %get-tuple-element.96), channel_id=1, source_target_pairs={{12,0},{0,4},{4,8},{8,12},{28,16},{16,20},{20,24},{24,28},{13,1},{... | collective-permute-start | bytes 442376 | tf_op jit(solution)/shard_map/ppermute | solution.py:32
  145.2 0.9 collective-permute-start.37
  149.2 1.2 collective-permute-start.35
  150.5 3.5 %collective-permute-done.36 = bf16[192,384]{1,0:T(8,128)(2,1)S(1)} collective-permute-done((bf16[192,384]{1,0:T(8,128)(2,1)S(1)}, bf16[192,384]{1,0:T(8,128)(2,1)S(1)}, u32[]{:S(2)}, u32[]{:S(2)}) %collective-permute-start.36) | collective-permute-done | bytes 147488 | tf_op jit(solution)/shard_map/ppermute | solution.py:24
  154.0 2.2 %collective-permute-done.35 = bf16[192,384]{1,0:T(8,128)(2,1)S(1)} collective-permute-done((bf16[192,384]{1,0:T(8,128)(2,1)S(1)}, bf16[192,384]{1,0:T(8,128)(2,1)S(1)}, u32[]{:S(2)}, u32[]{:S(2)}) %collective-permute-start.35) | collective-permute-done | bytes 147488 | tf_op jit(solution)/shard_map/ppermute | solution.py:24
  156.3 1.3 collective-permute-start.41
  158.5 3.1 %collective-permute-done.41 = bf16[192,384]{1,0:T(8,128)(2,1)S(1)} collective-permute-done((bf16[192,384]{1,0:T(8,128)(2,1)S(1)}, bf16[192,384]{1,0:T(8,128)(2,1)S(1)}, u32[]{:S(2)}, u32[]{:S(2)}) %collective-permute-start.41) | collective-permute-done | bytes 147488 | tf_op jit(solution)/shard_map/ppermute | solution.py:42
  (133 shorter events, 27.0 us)
Async XLA Ops:
  0.6 16.2 %copy-start.2 = (bf16[192,1536]{1,0:T(8,128)(2,1)S(1)}, bf16[192,1536]{1,0:T(8,128)(2,1)}, u32[]{:S(2)}) copy-start(bf16[192,1536]{1,0:T(8,128)(2,1)} %param.5) | copy-start | bytes 1769476
  0.6 5.9 %collective-permute-start = (bf16[192,384]{1,0:T(8,128)(2,1)}, bf16[192,384]{1,0:T(8,128)(2,1)S(1)}, u32[]{:S(2)}, u32[]{:S(2)}) collective-permute-start(bf16[192,384]{1,0:T(8,128)(2,1)} %param.3), channel_id=1, source_target_pairs={{0,16},{4,20},{8,24},{12,28},{16,0},{20,4},{24,8},{28,12},{1,17},{... | collective-permute-start | bytes 442376 | tf_op jit(solution)/shard_map/ppermute | solution.py:42
  6.6 8.3 %collective-permute-start.1 = (bf16[192,384]{1,0:T(8,128)(2,1)S(1)}, bf16[192,384]{1,0:T(8,128)(2,1)S(1)}, u32[]{:S(2)}, u32[]{:S(2)}) collective-permute-start(bf16[192,384]{1,0:T(8,128)(2,1)S(1)} %pad_maximum_fusion.17), channel_id=1, source_target_pairs={{32,0},{64,32},{96,64},{0,96},{33,1},{65,33},{97,65},{1,97},{34,2}... | collective-permute-start | bytes 442376 | tf_op jit(solution)/shard_map/ppermute | solution.py:24
  9.4 7.6 %collective-permute-start.2 = (bf16[192,384]{1,0:T(8,128)(2,1)S(1)}, bf16[192,384]{1,0:T(8,128)(2,1)S(1)}, u32[]{:S(2)}, u32[]{:S(2)}) collective-permute-start(bf16[192,384]{1,0:T(8,128)(2,1)S(1)} %pad_maximum_fusion.17), channel_id=1, source_target_pairs={{64,0},{96,32},{0,64},{32,96},{65,1},{97,33},{1,65},{33,97},{66,2}... | collective-permute-start | bytes 442376 | tf_op jit(solution)/shard_map/ppermute | solution.py:24
  10.2 8.3 %collective-permute-start.3 = (bf16[192,384]{1,0:T(8,128)(2,1)S(1)}, bf16[192,384]{1,0:T(8,128)(2,1)S(1)}, u32[]{:S(2)}, u32[]{:S(2)}) collective-permute-start(bf16[192,384]{1,0:T(8,128)(2,1)S(1)} %pad_maximum_fusion.17), channel_id=1, source_target_pairs={{96,0},{0,32},{32,64},{64,96},{97,1},{1,33},{33,65},{65,97},{98,2}... | collective-permute-start | bytes 442376 | tf_op jit(solution)/shard_map/ppermute | solution.py:24
  11.1 7.4 %collective-permute-start.4 = (bf16[192,384]{1,0:T(8,128)(2,1)S(1)}, bf16[192,384]{1,0:T(8,128)(2,1)S(1)}, u32[]{:S(2)}, u32[]{:S(2)}) collective-permute-start(bf16[192,384]{1,0:T(8,128)(2,1)S(1)} %pad_maximum_fusion.18), channel_id=1, source_target_pairs={{4,0},{8,4},{12,8},{0,12},{20,16},{24,20},{28,24},{16,28},{5,1},{9... | collective-permute-start | bytes 442376 | tf_op jit(solution)/shard_map/ppermute | solution.py:32
  11.3 8.3 %collective-permute-start.5 = (bf16[192,384]{1,0:T(8,128)(2,1)S(1)}, bf16[192,384]{1,0:T(8,128)(2,1)S(1)}, u32[]{:S(2)}, u32[]{:S(2)}) collective-permute-start(bf16[192,384]{1,0:T(8,128)(2,1)S(1)} %pad_maximum_fusion.18), channel_id=1, source_target_pairs={{8,0},{12,4},{0,8},{4,12},{24,16},{28,20},{16,24},{20,28},{9,1},{1... | collective-permute-start | bytes 442376 | tf_op jit(solution)/shard_map/ppermute | solution.py:32
  14.8 5.5 %collective-permute-start.6 = (bf16[192,384]{1,0:T(8,128)(2,1)S(1)}, bf16[192,384]{1,0:T(8,128)(2,1)S(1)}, u32[]{:S(2)}, u32[]{:S(2)}) collective-permute-start(bf16[192,384]{1,0:T(8,128)(2,1)S(1)} %pad_maximum_fusion.18), channel_id=1, source_target_pairs={{12,0},{0,4},{4,8},{8,12},{28,16},{16,20},{20,24},{24,28},{13,1},{... | collective-permute-start | bytes 442376 | tf_op jit(solution)/shard_map/ppermute | solution.py:32
  16.8 11.5 %copy-start.1 = (bf16[1536,768]{1,0:T(8,128)(2,1)S(1)}, bf16[1536,768]{1,0:T(8,128)(2,1)}, u32[]{:S(2)}) copy-start(bf16[1536,768]{1,0:T(8,128)(2,1)} %param.4) | copy-start | bytes 7077892
  20.4 20.0 %collective-permute-start.7 = (bf16[192,1536]{1,0:T(8,128)(2,1)S(1)}, bf16[192,1536]{1,0:T(8,128)(2,1)S(1)}, u32[]{:S(2)}, u32[]{:S(2)}) collective-permute-start(bf16[192,1536]{1,0:T(8,128)(2,1)S(1)} %get-tuple-element.114), channel_id=1, source_target_pairs={{4,0},{8,4},{12,8},{0,12},{20,16},{24,20},{28,24},{16,28},{5,1},{9... | collective-permute-start | bytes 1769480 | tf_op jit(solution)/shard_map/ppermute | solution.py:32
  23.8 16.6 %collective-permute-start.8 = (bf16[192,1536]{1,0:T(8,128)(2,1)S(1)}, bf16[192,1536]{1,0:T(8,128)(2,1)S(1)}, u32[]{:S(2)}, u32[]{:S(2)}) collective-permute-start(bf16[192,1536]{1,0:T(8,128)(2,1)S(1)} %get-tuple-element.114), channel_id=1, source_target_pairs={{12,0},{0,4},{4,8},{8,12},{28,16},{16,20},{20,24},{24,28},{13,1},{... | collective-permute-start | bytes 1769480 | tf_op jit(solution)/shard_map/ppermute | solution.py:32
  23.9 16.5 %collective-permute-start.9 = (bf16[768,384]{1,0:T(8,128)(2,1)S(1)}, bf16[768,384]{1,0:T(8,128)(2,1)S(1)}, u32[]{:S(2)}, u32[]{:S(2)}) collective-permute-start(bf16[768,384]{1,0:T(8,128)(2,1)S(1)} %constant_dynamic-update-slice_fusion), channel_id=1, source_target_pairs={{32,0},{64,32},{96,64},{0,96},{33,1},{65,33},{97,65},{1,97},{34,2}... | collective-permute-start | bytes 1769480 | tf_op jit(solution)/shard_map/ppermute | solution.py:24
  26.4 14.0 %collective-permute-start.10 = (bf16[768,384]{1,0:T(8,128)(2,1)S(1)}, bf16[768,384]{1,0:T(8,128)(2,1)S(1)}, u32[]{:S(2)}, u32[]{:S(2)}) collective-permute-start(bf16[768,384]{1,0:T(8,128)(2,1)S(1)} %constant_dynamic-update-slice_fusion), channel_id=1, source_target_pairs={{96,0},{0,32},{32,64},{64,96},{97,1},{1,33},{33,65},{65,97},{98,2}... | collective-permute-start | bytes 1769480 | tf_op jit(solution)/shard_map/ppermute | solution.py:24
  26.4 14.0 %collective-permute-start.11 = (bf16[192,768]{1,0:T(8,128)(2,1)S(1)}, bf16[192,768]{1,0:T(8,128)(2,1)S(1)}, u32[]{:S(2)}, u32[]{:S(2)}) collective-permute-start(bf16[192,768]{1,0:T(8,128)(2,1)S(1)} %get-tuple-element.46), channel_id=1, source_target_pairs={{0,0},{1,10},{2,18},{3,24},{4,1},{5,11},{6,19},{7,25},{8,5},{9,15}... | collective-permute-start | bytes 884744 | tf_op jit(solution)/shard_map/ppermute | solution.py:112
  41.9 11.4 %collective-permute-start.12 = (bf16[96,1536]{1,0:T(8,128)(2,1)S(1)}, bf16[96,1536]{1,0:T(8,128)(2,1)S(1)}, u32[]{:S(2)}, u32[]{:S(2)}) collective-permute-start(bf16[96,1536]{1,0:T(8,128)(2,1)S(1)} %slice.180), channel_id=1, source_target_pairs={{4,0},{8,4},{12,8},{0,12},{20,16},{24,20},{28,24},{16,28},{5,1},{9... | collective-permute-start | bytes 884744 | tf_op jit(solution)/shard_map/ppermute | solution.py:32
  42.1 11.2 %collective-permute-start.13 = (bf16[96,1536]{1,0:T(8,128)(2,1)S(1)}, bf16[96,1536]{1,0:T(8,128)(2,1)S(1)}, u32[]{:S(2)}, u32[]{:S(2)}) collective-permute-start(bf16[96,1536]{1,0:T(8,128)(2,1)S(1)} %slice.181), channel_id=1, source_target_pairs={{12,0},{0,4},{4,8},{8,12},{28,16},{16,20},{20,24},{24,28},{13,1},{... | collective-permute-start | bytes 884744 | tf_op jit(solution)/shard_map/ppermute | solution.py:32
  44.2 9.1 %collective-permute-start.14 = (bf16[384,384]{1,0:T(8,128)(2,1)S(1)}, bf16[384,384]{1,0:T(8,128)(2,1)S(1)}, u32[]{:S(2)}, u32[]{:S(2)}) collective-permute-start(bf16[384,384]{1,0:T(8,128)(2,1)S(1)} %slice.182), channel_id=1, source_target_pairs={{32,0},{64,32},{96,64},{0,96},{33,1},{65,33},{97,65},{1,97},{34,2}... | collective-permute-start | bytes 884744 | tf_op jit(solution)/shard_map/ppermute | solution.py:24
  47.4 8.0 %collective-permute-start.15 = (bf16[384,384]{1,0:T(8,128)(2,1)S(1)}, bf16[384,384]{1,0:T(8,128)(2,1)S(1)}, u32[]{:S(2)}, u32[]{:S(2)}) collective-permute-start(bf16[384,384]{1,0:T(8,128)(2,1)S(1)} %slice.183), channel_id=1, source_target_pairs={{96,0},{0,32},{32,64},{64,96},{97,1},{1,33},{33,65},{65,97},{98,2}... | collective-permute-start | bytes 884744 | tf_op jit(solution)/shard_map/ppermute | solution.py:24
  48.3 11.7 %collective-permute-start.16 = (bf16[192,768]{1,0:T(8,128)(2,1)S(1)}, bf16[192,768]{1,0:T(8,128)(2,1)S(1)}, u32[]{:S(2)}, u32[]{:S(2)}) collective-permute-start(bf16[192,768]{1,0:T(8,128)(2,1)S(1)} %get-tuple-element.53), channel_id=1, source_target_pairs={{0,5},{1,15},{2,23},{3,29},{4,4},{5,14},{6,22},{7,28},{8,0},{9,10}... | collective-permute-start | bytes 884744 | tf_op jit(solution)/shard_map/ppermute | solution.py:119
  60.8 2.1 %collective-permute-start.17 = (bf16[384,768]{1,0:T(8,128)(2,1)S(1)}, bf16[384,768]{1,0:T(8,128)(2,1)S(1)}, u32[]{:S(2)}, u32[]{:S(2)}) collective-permute-start(bf16[384,768]{1,0:T(8,128)(2,1)S(1)} %select_convert_fusion.1), channel_id=1, source_target_pairs={{0,1},{1,0},{2,3},{3,2},{4,5},{5,4},{6,7},{7,6},{8,9},{9,8},{10,11... | collective-permute-start | bytes 1769480 | tf_op jit(solution)/shard_map/ppermute | solution.py:50
  61.9 2.4 %collective-permute-start.23 = (bf16[384,768]{1,0:T(8,128)(2,1)S(1)}, bf16[384,768]{1,0:T(8,128)(2,1)S(1)}, u32[]{:S(2)}, u32[]{:S(2)}) collective-permute-start(bf16[384,768]{1,0:T(8,128)(2,1)S(1)} %get-tuple-element.137), channel_id=1, source_target_pairs={{0,1},{1,0},{2,3},{3,2},{4,5},{5,4},{6,7},{7,6},{8,9},{9,8},{10,11... | collective-permute-start | bytes 1769480 | tf_op jit(solution)/shard_map/ppermute | solution.py:50
  63.2 11.4 %collective-permute-start.18 = (bf16[2,96,768]{2,1,0:T(8,128)(2,1)S(1)}, bf16[2,96,768]{2,1,0:T(8,128)(2,1)S(1)}, u32[]{:S(2)}, u32[]{:S(2)}) collective-permute-start(bf16[2,96,768]{2,1,0:T(8,128)(2,1)S(1)} %fusion.41), channel_id=1, source_target_pairs={{0,2},{1,3},{2,0},{3,1},{4,6},{5,7},{6,4},{7,5},{8,10},{9,11},{10,... | collective-permute-start | bytes 884744 | tf_op jit(solution)/shard_map/ppermute | solution.py:46
  64.7 16.2 %collective-permute-start.24 = (bf16[2,96,768]{2,1,0:T(8,128)(2,1)S(1)}, bf16[2,96,768]{2,1,0:T(8,128)(2,1)S(1)}, u32[]{:S(2)}, u32[]{:S(2)}) collective-permute-start(bf16[2,96,768]{2,1,0:T(8,128)(2,1)S(1)} %fusion.42), channel_id=1, source_target_pairs={{0,2},{1,3},{2,0},{3,1},{4,6},{5,7},{6,4},{7,5},{8,10},{9,11},{10,... | collective-permute-start | bytes 884744 | tf_op jit(solution)/shard_map/ppermute | solution.py:46
  75.1 12.1 %collective-permute-start.19 = (bf16[2,96,768]{2,1,0:T(8,128)(2,1)S(1)}, bf16[2,96,768]{2,1,0:T(8,128)(2,1)S(1)}, u32[]{:S(2)}, u32[]{:S(2)}) collective-permute-start(bf16[2,96,768]{2,1,0:T(8,128)(2,1)S(1)} %get-tuple-element.82), channel_id=1, source_target_pairs={{0,2},{1,3},{2,0},{3,1},{4,6},{5,7},{6,4},{7,5},{8,10},{9,11},{10,... | collective-permute-start | bytes 884744 | tf_op jit(solution)/shard_map/ppermute | solution.py:46
  81.5 11.3 %collective-permute-start.25 = (bf16[2,96,768]{2,1,0:T(8,128)(2,1)S(1)}, bf16[2,96,768]{2,1,0:T(8,128)(2,1)S(1)}, u32[]{:S(2)}, u32[]{:S(2)}) collective-permute-start(bf16[2,96,768]{2,1,0:T(8,128)(2,1)S(1)} %get-tuple-element.84), channel_id=1, source_target_pairs={{0,2},{1,3},{2,0},{3,1},{4,6},{5,7},{6,4},{7,5},{8,10},{9,11},{10,... | collective-permute-start | bytes 884744 | tf_op jit(solution)/shard_map/ppermute | solution.py:46
  87.4 5.6 %collective-permute-start.20 = (bf16[384,768]{1,0:T(8,128)(2,1)S(1)}, bf16[384,768]{1,0:T(8,128)(2,1)S(1)}, u32[]{:S(2)}, u32[]{:S(2)}) collective-permute-start(bf16[384,768]{1,0:T(8,128)(2,1)S(1)} %pad_maximum_fusion.10), channel_id=1, source_target_pairs={{0,1},{1,0},{2,3},{3,2},{4,5},{5,4},{6,7},{7,6},{8,9},{9,8},{10,11... | collective-permute-start | bytes 1769480 | tf_op jit(solution)/shard_map/ppermute | solution.py:50
  93.0 2.1 %collective-permute-start.26 = (bf16[384,768]{1,0:T(8,128)(2,1)S(1)}, bf16[384,768]{1,0:T(8,128)(2,1)S(1)}, u32[]{:S(2)}, u32[]{:S(2)}) collective-permute-start(bf16[384,768]{1,0:T(8,128)(2,1)S(1)} %pad_maximum_fusion.11), channel_id=1, source_target_pairs={{0,1},{1,0},{2,3},{3,2},{4,5},{5,4},{6,7},{7,6},{8,9},{9,8},{10,11... | collective-permute-start | bytes 1769480 | tf_op jit(solution)/shard_map/ppermute | solution.py:50
  95.8 19.0 %collective-permute-start.27 = (bf16[384,384]{1,0:T(8,128)(2,1)S(1)}, bf16[384,384]{1,0:T(8,128)(2,1)S(1)}, u32[]{:S(2)}, u32[]{:S(2)}) collective-permute-start(bf16[384,384]{1,0:T(8,128)(2,1)S(1)} %convolution_convert_fusion.2), channel_id=1, source_target_pairs={{96,0},{0,32},{32,64},{64,96},{97,1},{1,33},{33,65},{65,97},{98,2}... | collective-permute-start | bytes 884744 | tf_op jit(solution)/shard_map/ppermute | solution.py:24
  96.3 18.4 %collective-permute-start.28 = (bf16[384,384]{1,0:T(8,128)(2,1)S(1)}, bf16[384,384]{1,0:T(8,128)(2,1)S(1)}, u32[]{:S(2)}, u32[]{:S(2)}) collective-permute-start(bf16[384,384]{1,0:T(8,128)(2,1)S(1)} %convolution_convert_fusion.1), channel_id=1, source_target_pairs={{32,0},{64,32},{96,64},{0,96},{33,1},{65,33},{97,65},{1,97},{34,2}... | collective-permute-start | bytes 884744 | tf_op jit(solution)/shard_map/ppermute | solution.py:24
  99.7 11.6 %collective-permute-start.21 = (bf16[96,1536]{1,0:T(8,128)(2,1)S(1)}, bf16[96,1536]{1,0:T(8,128)(2,1)S(1)}, u32[]{:S(2)}, u32[]{:S(2)}) collective-permute-start(bf16[96,1536]{1,0:T(8,128)(2,1)S(1)} %get-tuple-element.106), channel_id=1, source_target_pairs={{12,0},{0,4},{4,8},{8,12},{28,16},{16,20},{20,24},{24,28},{13,1},{... | collective-permute-start | bytes 884744 | tf_op jit(solution)/shard_map/ppermute | solution.py:32
  101.2 13.6 %collective-permute-start.22 = (bf16[96,1536]{1,0:T(8,128)(2,1)S(1)}, bf16[96,1536]{1,0:T(8,128)(2,1)S(1)}, u32[]{:S(2)}, u32[]{:S(2)}) collective-permute-start(bf16[96,1536]{1,0:T(8,128)(2,1)S(1)} %get-tuple-element.105), channel_id=1, source_target_pairs={{4,0},{8,4},{12,8},{0,12},{20,16},{24,20},{28,24},{16,28},{5,1},{9... | collective-permute-start | bytes 884744 | tf_op jit(solution)/shard_map/ppermute | solution.py:32
  102.9 11.9 %collective-permute-start.29 = (bf16[192,768]{1,0:T(8,128)(2,1)S(1)}, bf16[192,768]{1,0:T(8,128)(2,1)S(1)}, u32[]{:S(2)}, u32[]{:S(2)}) collective-permute-start(bf16[192,768]{1,0:T(8,128)(2,1)S(1)} %get-tuple-element.59), channel_id=1, source_target_pairs={{0,0},{10,1},{18,2},{24,3},{1,4},{11,5},{19,6},{25,7},{5,8},{15,9}... | collective-permute-start | bytes 884744 | tf_op jit(solution)/shard_map/ppermute | solution.py:179
  115.7 14.7 %collective-permute-start.30 = (bf16[192,1536]{1,0:T(8,128)(2,1)S(1)}, bf16[192,1536]{1,0:T(8,128)(2,1)S(1)}, u32[]{:S(2)}, u32[]{:S(2)}) collective-permute-start(bf16[192,1536]{1,0:T(8,128)(2,1)S(1)} %fusion.1), channel_id=1, source_target_pairs={{12,0},{0,4},{4,8},{8,12},{28,16},{16,20},{20,24},{24,28},{13,1},{... | collective-permute-start | bytes 1769480 | tf_op jit(solution)/shard_map/ppermute | solution.py:32
  118.4 13.9 %collective-permute-start.31 = (bf16[192,1536]{1,0:T(8,128)(2,1)S(1)}, bf16[192,1536]{1,0:T(8,128)(2,1)S(1)}, u32[]{:S(2)}, u32[]{:S(2)}) collective-permute-start(bf16[192,1536]{1,0:T(8,128)(2,1)S(1)} %fusion.2), channel_id=1, source_target_pairs={{4,0},{8,4},{12,8},{0,12},{20,16},{24,20},{28,24},{16,28},{5,1},{9... | collective-permute-start | bytes 1769480 | tf_op jit(solution)/shard_map/ppermute | solution.py:32
  119.6 15.4 %collective-permute-start.32 = (bf16[768,384]{1,0:T(8,128)(2,1)S(1)}, bf16[768,384]{1,0:T(8,128)(2,1)S(1)}, u32[]{:S(2)}, u32[]{:S(2)}) collective-permute-start(bf16[768,384]{1,0:T(8,128)(2,1)S(1)} %add_convert_fusion.1), channel_id=1, source_target_pairs={{96,0},{0,32},{32,64},{64,96},{97,1},{1,33},{33,65},{65,97},{98,2}... | collective-permute-start | bytes 1769480 | tf_op jit(solution)/shard_map/ppermute | solution.py:24
  120.5 14.8 %collective-permute-start.33 = (bf16[768,384]{1,0:T(8,128)(2,1)S(1)}, bf16[768,384]{1,0:T(8,128)(2,1)S(1)}, u32[]{:S(2)}, u32[]{:S(2)}) collective-permute-start(bf16[768,384]{1,0:T(8,128)(2,1)S(1)} %add_convert_fusion), channel_id=1, source_target_pairs={{32,0},{64,32},{96,64},{0,96},{33,1},{65,33},{97,65},{1,97},{34,2}... | collective-permute-start | bytes 1769480 | tf_op jit(solution)/shard_map/ppermute | solution.py:24
  125.3 11.1 %collective-permute-start.34 = (bf16[192,768]{1,0:T(8,128)(2,1)S(1)}, bf16[192,768]{1,0:T(8,128)(2,1)S(1)}, u32[]{:S(2)}, u32[]{:S(2)}) collective-permute-start(bf16[192,768]{1,0:T(8,128)(2,1)S(1)} %get-tuple-element.71), channel_id=1, source_target_pairs={{5,0},{15,1},{23,2},{29,3},{4,4},{14,5},{22,6},{28,7},{0,8},{10,9}... | collective-permute-start | bytes 884744 | tf_op jit(solution)/shard_map/ppermute | solution.py:179
  136.6 12.6 %collective-permute-start.40 = (bf16[192,384]{1,0:T(8,128)(2,1)S(1)}, bf16[192,384]{1,0:T(8,128)(2,1)S(1)}, u32[]{:S(2)}, u32[]{:S(2)}) collective-permute-start(bf16[192,384]{1,0:T(8,128)(2,1)S(1)} %get-tuple-element.97), channel_id=1, source_target_pairs={{4,0},{8,4},{12,8},{0,12},{20,16},{24,20},{28,24},{16,28},{5,1},{9... | collective-permute-start | bytes 442376 | tf_op jit(solution)/shard_map/ppermute | solution.py:32
  140.3 10.1 %collective-permute-start.39 = (bf16[192,384]{1,0:T(8,128)(2,1)S(1)}, bf16[192,384]{1,0:T(8,128)(2,1)S(1)}, u32[]{:S(2)}, u32[]{:S(2)}) collective-permute-start(bf16[192,384]{1,0:T(8,128)(2,1)S(1)} %get-tuple-element.98), channel_id=1, source_target_pairs={{8,0},{12,4},{0,8},{4,12},{24,16},{28,20},{16,24},{20,28},{9,1},{1... | collective-permute-start | bytes 442376 | tf_op jit(solution)/shard_map/ppermute | solution.py:32
  143.4 7.1 %collective-permute-start.38 = (bf16[192,384]{1,0:T(8,128)(2,1)S(1)}, bf16[192,384]{1,0:T(8,128)(2,1)S(1)}, u32[]{:S(2)}, u32[]{:S(2)}) collective-permute-start(bf16[192,384]{1,0:T(8,128)(2,1)S(1)} %get-tuple-element.96), channel_id=1, source_target_pairs={{12,0},{0,4},{4,8},{8,12},{28,16},{16,20},{20,24},{24,28},{13,1},{... | collective-permute-start | bytes 442376 | tf_op jit(solution)/shard_map/ppermute | solution.py:32
  145.2 5.3 %collective-permute-start.37 = (bf16[192,384]{1,0:T(8,128)(2,1)S(1)}, bf16[192,384]{1,0:T(8,128)(2,1)S(1)}, u32[]{:S(2)}, u32[]{:S(2)}) collective-permute-start(bf16[192,384]{1,0:T(8,128)(2,1)S(1)} %get-tuple-element.94), channel_id=1, source_target_pairs={{32,0},{64,32},{96,64},{0,96},{33,1},{65,33},{97,65},{1,97},{34,2}... | collective-permute-start | bytes 442376 | tf_op jit(solution)/shard_map/ppermute | solution.py:24
  146.1 7.9 %collective-permute-start.36 = (bf16[192,384]{1,0:T(8,128)(2,1)S(1)}, bf16[192,384]{1,0:T(8,128)(2,1)S(1)}, u32[]{:S(2)}, u32[]{:S(2)}) collective-permute-start(bf16[192,384]{1,0:T(8,128)(2,1)S(1)} %get-tuple-element.95), channel_id=1, source_target_pairs={{64,0},{96,32},{0,64},{32,96},{65,1},{97,33},{1,65},{33,97},{66,2}... | collective-permute-start | bytes 442376 | tf_op jit(solution)/shard_map/ppermute | solution.py:24
  149.1 1.4 copy-start
  149.2 7.0 %collective-permute-start.35 = (bf16[192,384]{1,0:T(8,128)(2,1)S(1)}, bf16[192,384]{1,0:T(8,128)(2,1)S(1)}, u32[]{:S(2)}, u32[]{:S(2)}) collective-permute-start(bf16[192,384]{1,0:T(8,128)(2,1)S(1)} %get-tuple-element.93), channel_id=1, source_target_pairs={{96,0},{0,32},{32,64},{64,96},{97,1},{1,33},{33,65},{65,97},{98,2}... | collective-permute-start | bytes 442376 | tf_op jit(solution)/shard_map/ppermute | solution.py:24
  156.3 5.2 %collective-permute-start.41 = (bf16[192,384]{1,0:T(8,128)(2,1)S(1)}, bf16[192,384]{1,0:T(8,128)(2,1)S(1)}, u32[]{:S(2)}, u32[]{:S(2)}) collective-permute-start(bf16[192,384]{1,0:T(8,128)(2,1)S(1)} %pad_maximum_fusion.19), channel_id=1, source_target_pairs={{0,16},{4,20},{8,24},{12,28},{16,0},{20,4},{24,8},{28,12},{1,17},{... | collective-permute-start | bytes 442376 | tf_op jit(solution)/shard_map/ppermute | solution.py:42

commit v4 on v3

--- a/solution.py
+++ b/solution.py
@@ -99,7 +99,6 @@
     tok_b = jnp.concatenate([tokens[half:], other[half:]], 0)
     b2, b1, b3 = (from_z(tok_b, r) for r in (2, 1, 3))
     a2, a1, a3 = (from_x(tok_a, r) for r in (2, 1, 3))
-    a1, a2, a3, b1, b2, b3 = together(a1, a2, a3, b1, b2, b3)
     a0 = jnp.concatenate([tok_a, a1, a2, a3], 1)
     b0 = jnp.concatenate([tok_b, b2, b1, b3], 0)
     n = 2 * half
@@ -116,10 +115,8 @@
     a2_first, a2_second = from_z(a1[:half], 1), from_z(a3[half:], 3)
     b2_first, b2_second = from_x(b1[: 2 * n], 1), from_x(b3[2 * n :], 3)
     early = dot(b0, w[0]) + dot(b1, w[1]) + dot(b3, w[3])
-    sent1 = lax.ppermute(after_done(piece1, early), BOTH, exchange_pairs(1))
-    a2_first, a2_second, b2_first, b2_second, sent1 = together(
-        a2_first, a2_second, b2_first, b2_second, sent1
-    )
+    at_1 = dot(a1, turned)
+    sent1 = lax.ppermute(after_done(piece1, early, at_1), BOTH, exchange_pairs(1))
     a2 = jnp.concatenate([a2_first, a2_second], 0)
 
     def over_core(first, second):
@@ -142,15 +139,15 @@
         there = swap_core(grad)
         return pick(core, grad, there), pick(core, there, grad)
 
-    k0 = z_lo ^ z_hi ^ (core & z_lo)
-    go0, go1 = pick(k0, sent0, sent1), pick(k0, sent1, sent0)
-
-    first, second = [dot(a0, turned), dot(a2, turned)], [dot(a1, turned), dot(a3, turned)]
+    first, second = [dot(a0, turned), dot(a2, turned)], [at_1, dot(a3, turned)]
     summed_a = over_core(jnp.concatenate(first, 0), jnp.concatenate(second, 0))
     summed_b = over_core(
         early[: 2 * n] + dot(b2_first, w[2]), early[2 * n :] + dot(b2_second, w[2])
     )
+    summed_a, sent1 = together(summed_a, sent1)
     hidden_a, hidden_b = over_y(summed_a), over_y(summed_b)
+    k0 = z_lo ^ z_hi ^ (core & z_lo)
+    go0, go1 = pick(k0, sent0, sent1), pick(k0, sent1, sent0)
     act_a, gr_a = gelu(hidden_a, jnp.concatenate([go0[:half], go1[:half]], 0))
     act_b, gr_b = gelu(hidden_b, jnp.concatenate([go0[half:], go1[half:]], 0))
     there_a, there_b = swap_y_hi(gr_a), swap_y_hi(gr_b)

time: 164 us -> 160 us (0.976)
  starting transfers between devices: 64.2 us -> 60.9 us
    ppermute x14, waiting for transfers between devices: 10.5 us -> 16.6 us  [from_z(): lax.ppermute(v, 'ja', [(y * 4 + (z + r) % N_RING, y * 4 + z) for y in ran...]
    ppermute x14, starting transfers between devices: 25 us -> 19 us  [from_z(): lax.ppermute(v, 'ja', [(y * 4 + (z + r) % N_RING, y * 4 + z) for y in ran...]
    ppermute x1, waiting for transfers between devices: 4.57 us -> 0.01 us  [on_device(): lax.ppermute(after_done(piece1, early, at_1), BOTH, exchange_pairs(1))]
    ppermute x4, starting transfers between devices: 2.89 us -> 5.31 us  [swap_y_hi(): return lax.ppermute(v, 'ka', [(k, k ^ 2) for k in range(4)])]
where the time goes in v4:
time: 160 us; the launch traced here: 158 us
  waiting for transfers between devices  70 us (44%)
  starting transfers between devices  60.9 us (38%)
  matrix products  18.2 us (11%)
  other arithmetic  5.03 us (3%)
  local copies, waits for them, and re-layouts  2.35 us (1%)
    ppermute x4, waiting for transfers between devices, swap_y_hi(): return lax.ppermute(v, 'ka', [(k, k ^ 2) for k in range(4)])  22.3 us
    ppermute x14, starting transfers between devices, from_x(): return lax.ppermute(v, 'ia', [((i + r) % N_RING, i) for i in range(N_RING)])  20.6 us
    ppermute x14, starting transfers between devices, from_z(): lax.ppermute(v, 'ja', [(y * 4 + (z + r) % N_RING, y * 4 + z) for y in ran...  19 us
    dot_general x26, matrix products, dot(): lax.dot_general(a, b, (((dims[0],), (dims[1],)), ((), ())), preferred_ele...  18.2 us
    ppermute x14, waiting for transfers between devices, from_z(): lax.ppermute(v, 'ja', [(y * 4 + (z + r) % N_RING, y * 4 + z) for y in ran...  16.6 us
    ppermute x14, waiting for transfers between devices, from_x(): return lax.ppermute(v, 'ia', [((i + r) % N_RING, i) for i in range(N_RING)])  13.1 us
    ppermute x1, waiting for transfers between devices, on_device(): sent0 = lax.ppermute(after_done(piece0, a0, b0), BOTH, exchange_pairs(0))  9.08 us
    ppermute x2, starting transfers between devices, give_back(): return lax.ppermute(piece, BOTH, [(t, s) for s, t in exchange_pairs(turn)])  7.56 us
  transfers between devices with their start and end apart: 42, of which 24 were waited for; matrix products, arithmetic and copies ran while one was open for 13% of the time, Pallas kernels for 0%

profile of v4, /device:TPU:40, one launch (start us, length us, event | category | flops | bytes accessed | tf_op | source)
XLA Modules:
  0.0 158.0 jit_solution(16764799497688927861)
XLA Ops:
  1.2 1.0 fusion.55
  2.1 4.4 %collective-permute-done = bf16[192,384]{1,0:T(8,128)(2,1)S(1)} collective-permute-done((bf16[192,384]{1,0:T(8,128)(2,1)}, bf16[192,384]{1,0:T(8,128)(2,1)S(1)}, u32[]{:S(2)}, u32[]{:S(2)}) %collective-permute-start) | collective-permute-done | bytes 147488 | tf_op jit(solution)/shard_map/ppermute | solution.py:42
  6.6 1.6 collective-permute-start.3
  8.1 2.7 %collective-permute-start.2 = (bf16[192,384]{1,0:T(8,128)(2,1)S(1)}, bf16[192,384]{1,0:T(8,128)(2,1)S(1)}, u32[]{:S(2)}, u32[]{:S(2)}) collective-permute-start(bf16[192,384]{1,0:T(8,128)(2,1)S(1)} %pad_maximum_fusion.17), channel_id=1, source_target_pairs={{64,0},{96,32},{0,64},{32,96},{65,1},{97,33},{1,65},{33,97},{66,2}... | collective-permute-start | bytes 442376 | tf_op jit(solution)/shard_map/ppermute | solution.py:24
  10.9 1.4 collective-permute-start.1
  12.5 3.1 %collective-permute-start.6 = (bf16[192,384]{1,0:T(8,128)(2,1)S(1)}, bf16[192,384]{1,0:T(8,128)(2,1)S(1)}, u32[]{:S(2)}, u32[]{:S(2)}) collective-permute-start(bf16[192,384]{1,0:T(8,128)(2,1)S(1)} %pad_maximum_fusion.18), channel_id=1, source_target_pairs={{8,0},{12,4},{0,8},{4,12},{24,16},{28,20},{16,24},{20,28},{9,1},{1... | collective-permute-start | bytes 442376 | tf_op jit(solution)/shard_map/ppermute | solution.py:32
  15.5 1.0 collective-permute-start.7
  16.6 1.0 collective-permute-start.8
  17.7 1.1 collective-permute-start.4
  18.8 1.0 collective-permute-start.5
  20.3 2.7 %collective-permute-done.7 = bf16[192,384]{1,0:T(8,128)(2,1)S(1)} collective-permute-done((bf16[192,384]{1,0:T(8,128)(2,1)S(1)}, bf16[192,384]{1,0:T(8,128)(2,1)S(1)}, u32[]{:S(2)}, u32[]{:S(2)}) %collective-permute-start.7) | collective-permute-done | bytes 147488 | tf_op jit(solution)/shard_map/ppermute | solution.py:32
  23.7 2.0 %collective-permute-start.10 = (bf16[768,384]{1,0:T(8,128)(2,1)S(1)}, bf16[768,384]{1,0:T(8,128)(2,1)S(1)}, u32[]{:S(2)}, u32[]{:S(2)}) collective-permute-start(bf16[768,384]{1,0:T(8,128)(2,1)S(1)} %constant_dynamic-update-slice_fusion), channel_id=1, source_target_pairs={{96,0},{0,32},{32,64},{64,96},{97,1},{1,33},{33,65},{65,97},{98,2}... | collective-permute-start | bytes 1769480 | tf_op jit(solution)/shard_map/ppermute | solution.py:24
  25.7 1.9 %collective-permute-start.11 = (bf16[192,768]{1,0:T(8,128)(2,1)S(1)}, bf16[192,768]{1,0:T(8,128)(2,1)S(1)}, u32[]{:S(2)}, u32[]{:S(2)}) collective-permute-start(bf16[192,768]{1,0:T(8,128)(2,1)S(1)} %get-tuple-element.31), channel_id=1, source_target_pairs={{0,0},{1,10},{2,18},{3,24},{4,1},{5,11},{6,19},{7,25},{8,5},{9,15}... | collective-permute-start | bytes 884744 | tf_op jit(solution)/shard_map/ppermute | solution.py:111
  29.4 9.1 %collective-permute-done.11 = bf16[192,768]{1,0:T(8,128)(2,1)S(1)} collective-permute-done((bf16[192,768]{1,0:T(8,128)(2,1)S(1)}, bf16[192,768]{1,0:T(8,128)(2,1)S(1)}, u32[]{:S(2)}, u32[]{:S(2)}) %collective-permute-start.11) | collective-permute-done | bytes 294944 | tf_op jit(solution)/shard_map/ppermute | solution.py:111
  38.5 1.6 %collective-permute-done.4 = bf16[192,1536]{1,0:T(8,128)(2,1)S(1)} collective-permute-done((bf16[192,1536]{1,0:T(8,128)(2,1)S(1)}, bf16[192,1536]{1,0:T(8,128)(2,1)S(1)}, u32[]{:S(2)}, u32[]{:S(2)}) %collective-permute-start.4) | collective-permute-done | bytes 589856 | tf_op jit(solution)/shard_map/ppermute | solution.py:32
  41.6 2.0 %collective-permute-start.13 = (bf16[96,1536]{1,0:T(8,128)(2,1)S(1)}, bf16[96,1536]{1,0:T(8,128)(2,1)S(1)}, u32[]{:S(2)}, u32[]{:S(2)}) collective-permute-start(bf16[96,1536]{1,0:T(8,128)(2,1)S(1)} %slice.181), channel_id=1, source_target_pairs={{12,0},{0,4},{4,8},{8,12},{28,16},{16,20},{20,24},{24,28},{13,1},{... | collective-permute-start | bytes 884744 | tf_op jit(solution)/shard_map/ppermute | solution.py:32
  44.5 3.5 %collective-permute-start.15 = (bf16[192,768]{1,0:T(8,128)(2,1)S(1)}, bf16[192,768]{1,0:T(8,128)(2,1)S(1)}, u32[]{:S(2)}, u32[]{:S(2)}) collective-permute-start(bf16[192,768]{1,0:T(8,128)(2,1)S(1)} %get-tuple-element.38), channel_id=1, source_target_pairs={{0,5},{1,15},{2,23},{3,29},{4,4},{5,14},{6,22},{7,28},{8,0},{9,10}... | collective-permute-start | bytes 884744 | tf_op jit(solution)/shard_map/ppermute | solution.py:119
  48.0 1.2 collective-permute-start.21
  49.1 0.9 collective-permute-start.22
  51.7 5.1 %collective-permute-done.21 = bf16[384,384]{1,0:T(8,128)(2,1)S(1)} collective-permute-done((bf16[384,384]{1,0:T(8,128)(2,1)S(1)}, bf16[384,384]{1,0:T(8,128)(2,1)S(1)}, u32[]{:S(2)}, u32[]{:S(2)}) %collective-permute-start.21) | collective-permute-done | bytes 294944 | tf_op jit(solution)/shard_map/ppermute | solution.py:24
  59.3 1.1 collective-permute-start.16
  61.1 2.1 %collective-permute-start.24 = (bf16[2,96,768]{2,1,0:T(8,128)(2,1)S(1)}, bf16[2,96,768]{2,1,0:T(8,128)(2,1)S(1)}, u32[]{:S(2)}, u32[]{:S(2)}) collective-permute-start(bf16[2,96,768]{2,1,0:T(8,128)(2,1)S(1)} %fusion.39), channel_id=1, source_target_pairs={{0,2},{1,3},{2,0},{3,1},{4,6},{5,7},{6,4},{7,5},{8,10},{9,11},{10,... | collective-permute-start | bytes 884744 | tf_op jit(solution)/shard_map/ppermute | solution.py:46
  63.4 7.3 %collective-permute-done.16 = bf16[2,96,768]{2,1,0:T(8,128)(2,1)S(1)} collective-permute-done((bf16[2,96,768]{2,1,0:T(8,128)(2,1)S(1)}, bf16[2,96,768]{2,1,0:T(8,128)(2,1)S(1)}, u32[]{:S(2)}, u32[]{:S(2)}) %collective-permute-start.16) | collective-permute-done | bytes 294944 | tf_op jit(solution)/shard_map/ppermute | solution.py:46
  71.2 1.1 collective-permute-start.17
  72.2 4.8 %collective-permute-done.24 = bf16[2,96,768]{2,1,0:T(8,128)(2,1)S(1)} collective-permute-done((bf16[2,96,768]{2,1,0:T(8,128)(2,1)S(1)}, bf16[2,96,768]{2,1,0:T(8,128)(2,1)S(1)}, u32[]{:S(2)}, u32[]{:S(2)}) %collective-permute-start.24) | collective-permute-done | bytes 294944 | tf_op jit(solution)/shard_map/ppermute | solution.py:46
  77.5 1.1 collective-permute-start.25
  78.7 4.6 %collective-permute-done.17 = bf16[2,96,768]{2,1,0:T(8,128)(2,1)S(1)} collective-permute-done((bf16[2,96,768]{2,1,0:T(8,128)(2,1)S(1)}, bf16[2,96,768]{2,1,0:T(8,128)(2,1)S(1)}, u32[]{:S(2)}, u32[]{:S(2)}) %collective-permute-start.17) | collective-permute-done | bytes 294944 | tf_op jit(solution)/shard_map/ppermute | solution.py:46
  83.5 5.7 %collective-permute-done.25 = bf16[2,96,768]{2,1,0:T(8,128)(2,1)S(1)} collective-permute-done((bf16[2,96,768]{2,1,0:T(8,128)(2,1)S(1)}, bf16[2,96,768]{2,1,0:T(8,128)(2,1)S(1)}, u32[]{:S(2)}, u32[]{:S(2)}) %collective-permute-start.25) | collective-permute-done | bytes 294944 | tf_op jit(solution)/shard_map/ppermute | solution.py:46
  93.2 2.8 %collective-permute-start.28 = (bf16[384,384]{1,0:T(8,128)(2,1)S(1)}, bf16[384,384]{1,0:T(8,128)(2,1)S(1)}, u32[]{:S(2)}, u32[]{:S(2)}) collective-permute-start(bf16[384,384]{1,0:T(8,128)(2,1)S(1)} %convolution_convert_fusion.1), channel_id=1, source_target_pairs={{32,0},{64,32},{96,64},{0,96},{33,1},{65,33},{97,65},{1,97},{34,2}... | collective-permute-start | bytes 884744 | tf_op jit(solution)/shard_map/ppermute | solution.py:24
  96.0 1.1 collective-permute-start.19
  97.1 1.0 collective-permute-start.20
  98.1 2.8 %collective-permute-start.29 = (bf16[192,768]{1,0:T(8,128)(2,1)S(1)}, bf16[192,768]{1,0:T(8,128)(2,1)S(1)}, u32[]{:S(2)}, u32[]{:S(2)}) collective-permute-start(bf16[192,768]{1,0:T(8,128)(2,1)S(1)} %get-tuple-element.41), channel_id=1, source_target_pairs={{0,0},{10,1},{18,2},{24,3},{1,4},{11,5},{19,6},{25,7},{5,8},{15,9}... | collective-permute-start | bytes 884744 | tf_op jit(solution)/shard_map/ppermute | solution.py:176
  101.1 4.2 %collective-permute-done.19 = bf16[96,1536]{1,0:T(8,128)(2,1)S(1)} collective-permute-done((bf16[96,1536]{1,0:T(8,128)(2,1)S(1)}, bf16[96,1536]{1,0:T(8,128)(2,1)S(1)}, u32[]{:S(2)}, u32[]{:S(2)}) %collective-permute-start.19) | collective-permute-done | bytes 294944 | tf_op jit(solution)/shard_map/ppermute | solution.py:32
  105.3 3.2 %collective-permute-done.20 = bf16[96,1536]{1,0:T(8,128)(2,1)S(1)} collective-permute-done((bf16[96,1536]{1,0:T(8,128)(2,1)S(1)}, bf16[96,1536]{1,0:T(8,128)(2,1)S(1)}, u32[]{:S(2)}, u32[]{:S(2)}) %collective-permute-start.20) | collective-permute-done | bytes 294944 | tf_op jit(solution)/shard_map/ppermute | solution.py:32
  110.3 1.9 %collective-permute-start.30 = (bf16[192,1536]{1,0:T(8,128)(2,1)S(1)}, bf16[192,1536]{1,0:T(8,128)(2,1)S(1)}, u32[]{:S(2)}, u32[]{:S(2)}) collective-permute-start(bf16[192,1536]{1,0:T(8,128)(2,1)S(1)} %fusion.1), channel_id=1, source_target_pairs={{12,0},{0,4},{4,8},{8,12},{28,16},{16,20},{20,24},{24,28},{13,1},{... | collective-permute-start | bytes 1769480 | tf_op jit(solution)/shard_map/ppermute | solution.py:32
  115.1 3.3 %collective-permute-start.33 = (bf16[768,384]{1,0:T(8,128)(2,1)S(1)}, bf16[768,384]{1,0:T(8,128)(2,1)S(1)}, u32[]{:S(2)}, u32[]{:S(2)}) collective-permute-start(bf16[768,384]{1,0:T(8,128)(2,1)S(1)} %add_convert_fusion), channel_id=1, source_target_pairs={{32,0},{64,32},{96,64},{0,96},{33,1},{65,33},{97,65},{1,97},{34,2}... | collective-permute-start | bytes 1769480 | tf_op jit(solution)/shard_map/ppermute | solution.py:24
  119.3 4.7 %collective-permute-start.34 = (bf16[192,768]{1,0:T(8,128)(2,1)S(1)}, bf16[192,768]{1,0:T(8,128)(2,1)S(1)}, u32[]{:S(2)}, u32[]{:S(2)}) collective-permute-start(bf16[192,768]{1,0:T(8,128)(2,1)S(1)} %get-tuple-element.53), channel_id=1, source_target_pairs={{5,0},{15,1},{23,2},{29,3},{4,4},{14,5},{22,6},{28,7},{0,8},{10,9}... | collective-permute-start | bytes 884744 | tf_op jit(solution)/shard_map/ppermute | solution.py:176
  124.0 1.2 collective-permute-done.30
  125.2 2.7 %collective-permute-done.31 = bf16[192,1536]{1,0:T(8,128)(2,1)S(1)} collective-permute-done((bf16[192,1536]{1,0:T(8,128)(2,1)S(1)}, bf16[192,1536]{1,0:T(8,128)(2,1)S(1)}, u32[]{:S(2)}, u32[]{:S(2)}) %collective-permute-start.31) | collective-permute-done | bytes 589856 | tf_op jit(solution)/shard_map/ppermute | solution.py:32
  127.9 1.8 %collective-permute-done.32 = bf16[768,384]{1,0:T(8,128)(2,1)S(1)} collective-permute-done((bf16[768,384]{1,0:T(8,128)(2,1)S(1)}, bf16[768,384]{1,0:T(8,128)(2,1)S(1)}, u32[]{:S(2)}, u32[]{:S(2)}) %collective-permute-start.32) | collective-permute-done | bytes 589856 | tf_op jit(solution)/shard_map/ppermute | solution.py:24
  133.2 3.0 %collective-permute-start.40 = (bf16[192,384]{1,0:T(8,128)(2,1)S(1)}, bf16[192,384]{1,0:T(8,128)(2,1)S(1)}, u32[]{:S(2)}, u32[]{:S(2)}) collective-permute-start(bf16[192,384]{1,0:T(8,128)(2,1)S(1)} %get-tuple-element.79), channel_id=1, source_target_pairs={{4,0},{8,4},{12,8},{0,12},{20,16},{24,20},{28,24},{16,28},{5,1},{9... | collective-permute-start | bytes 442376 | tf_op jit(solution)/shard_map/ppermute | solution.py:32
  137.0 1.7 %collective-permute-start.38 = (bf16[192,384]{1,0:T(8,128)(2,1)S(1)}, bf16[192,384]{1,0:T(8,128)(2,1)S(1)}, u32[]{:S(2)}, u32[]{:S(2)}) collective-permute-start(bf16[192,384]{1,0:T(8,128)(2,1)S(1)} %get-tuple-element.78), channel_id=1, source_target_pairs={{12,0},{0,4},{4,8},{8,12},{28,16},{16,20},{20,24},{24,28},{13,1},{... | collective-permute-start | bytes 442376 | tf_op jit(solution)/shard_map/ppermute | solution.py:32
  138.9 3.0 %collective-permute-start.37 = (bf16[192,384]{1,0:T(8,128)(2,1)S(1)}, bf16[192,384]{1,0:T(8,128)(2,1)S(1)}, u32[]{:S(2)}, u32[]{:S(2)}) collective-permute-start(bf16[192,384]{1,0:T(8,128)(2,1)S(1)} %get-tuple-element.76), channel_id=1, source_target_pairs={{32,0},{64,32},{96,64},{0,96},{33,1},{65,33},{97,65},{1,97},{34,2}... | collective-permute-start | bytes 442376 | tf_op jit(solution)/shard_map/ppermute | solution.py:24
  145.5 1.0 collective-permute-start.35
  146.8 3.2 %collective-permute-done.36 = bf16[192,384]{1,0:T(8,128)(2,1)S(1)} collective-permute-done((bf16[192,384]{1,0:T(8,128)(2,1)S(1)}, bf16[192,384]{1,0:T(8,128)(2,1)S(1)}, u32[]{:S(2)}, u32[]{:S(2)}) %collective-permute-start.36) | collective-permute-done | bytes 147488 | tf_op jit(solution)/shard_map/ppermute | solution.py:24
  150.0 1.9 %collective-permute-done.35 = bf16[192,384]{1,0:T(8,128)(2,1)S(1)} collective-permute-done((bf16[192,384]{1,0:T(8,128)(2,1)S(1)}, bf16[192,384]{1,0:T(8,128)(2,1)S(1)}, u32[]{:S(2)}, u32[]{:S(2)}) %collective-permute-start.35) | collective-permute-done | bytes 147488 | tf_op jit(solution)/shard_map/ppermute | solution.py:24
  152.0 2.0 %collective-permute-start.41 = (bf16[192,384]{1,0:T(8,128)(2,1)S(1)}, bf16[192,384]{1,0:T(8,128)(2,1)S(1)}, u32[]{:S(2)}, u32[]{:S(2)}) collective-permute-start(bf16[192,384]{1,0:T(8,128)(2,1)S(1)} %pad_maximum_fusion.19), channel_id=1, source_target_pairs={{0,16},{4,20},{8,24},{12,28},{16,0},{20,4},{24,8},{28,12},{1,17},{... | collective-permute-start | bytes 442376 | tf_op jit(solution)/shard_map/ppermute | solution.py:42
  154.9 2.4 %collective-permute-done.41 = bf16[192,384]{1,0:T(8,128)(2,1)S(1)} collective-permute-done((bf16[192,384]{1,0:T(8,128)(2,1)S(1)}, bf16[192,384]{1,0:T(8,128)(2,1)S(1)}, u32[]{:S(2)}, u32[]{:S(2)}) %collective-permute-start.41) | collective-permute-done | bytes 147488 | tf_op jit(solution)/shard_map/ppermute | solution.py:42
  (133 shorter events, 31.8 us)
Async XLA Ops:
  0.6 11.7 %copy-start.2 = (bf16[192,1536]{1,0:T(8,128)(2,1)S(1)}, bf16[192,1536]{1,0:T(8,128)(2,1)}, u32[]{:S(2)}) copy-start(bf16[192,1536]{1,0:T(8,128)(2,1)} %param.5) | copy-start | bytes 1769476
  0.6 5.9 %collective-permute-start = (bf16[192,384]{1,0:T(8,128)(2,1)}, bf16[192,384]{1,0:T(8,128)(2,1)S(1)}, u32[]{:S(2)}, u32[]{:S(2)}) collective-permute-start(bf16[192,384]{1,0:T(8,128)(2,1)} %param.3), channel_id=1, source_target_pairs={{0,16},{4,20},{8,24},{12,28},{16,0},{20,4},{24,8},{28,12},{1,17},{... | collective-permute-start | bytes 442376 | tf_op jit(solution)/shard_map/ppermute | solution.py:42
  6.6 10.0 %collective-permute-start.3 = (bf16[192,384]{1,0:T(8,128)(2,1)S(1)}, bf16[192,384]{1,0:T(8,128)(2,1)S(1)}, u32[]{:S(2)}, u32[]{:S(2)}) collective-permute-start(bf16[192,384]{1,0:T(8,128)(2,1)S(1)} %pad_maximum_fusion.17), channel_id=1, source_target_pairs={{96,0},{0,32},{32,64},{64,96},{97,1},{1,33},{33,65},{65,97},{98,2}... | collective-permute-start | bytes 442376 | tf_op jit(solution)/shard_map/ppermute | solution.py:24
  8.1 9.4 %collective-permute-start.2 = (bf16[192,384]{1,0:T(8,128)(2,1)S(1)}, bf16[192,384]{1,0:T(8,128)(2,1)S(1)}, u32[]{:S(2)}, u32[]{:S(2)}) collective-permute-start(bf16[192,384]{1,0:T(8,128)(2,1)S(1)} %pad_maximum_fusion.17), channel_id=1, source_target_pairs={{64,0},{96,32},{0,64},{32,96},{65,1},{97,33},{1,65},{33,97},{66,2}... | collective-permute-start | bytes 442376 | tf_op jit(solution)/shard_map/ppermute | solution.py:24
  10.9 6.7 %collective-permute-start.1 = (bf16[192,384]{1,0:T(8,128)(2,1)S(1)}, bf16[192,384]{1,0:T(8,128)(2,1)S(1)}, u32[]{:S(2)}, u32[]{:S(2)}) collective-permute-start(bf16[192,384]{1,0:T(8,128)(2,1)S(1)} %pad_maximum_fusion.17), channel_id=1, source_target_pairs={{32,0},{64,32},{96,64},{0,96},{33,1},{65,33},{97,65},{1,97},{34,2}... | collective-permute-start | bytes 442376 | tf_op jit(solution)/shard_map/ppermute | solution.py:24
  12.5 15.1 %copy-start.1 = (bf16[1536,768]{1,0:T(8,128)(2,1)S(1)}, bf16[1536,768]{1,0:T(8,128)(2,1)}, u32[]{:S(2)}) copy-start(bf16[1536,768]{1,0:T(8,128)(2,1)} %param.4) | copy-start | bytes 7077892
  12.5 7.8 %collective-permute-start.6 = (bf16[192,384]{1,0:T(8,128)(2,1)S(1)}, bf16[192,384]{1,0:T(8,128)(2,1)S(1)}, u32[]{:S(2)}, u32[]{:S(2)}) collective-permute-start(bf16[192,384]{1,0:T(8,128)(2,1)S(1)} %pad_maximum_fusion.18), channel_id=1, source_target_pairs={{8,0},{12,4},{0,8},{4,12},{24,16},{28,20},{16,24},{20,28},{9,1},{1... | collective-permute-start | bytes 442376 | tf_op jit(solution)/shard_map/ppermute | solution.py:32
  15.5 7.5 %collective-permute-start.7 = (bf16[192,384]{1,0:T(8,128)(2,1)S(1)}, bf16[192,384]{1,0:T(8,128)(2,1)S(1)}, u32[]{:S(2)}, u32[]{:S(2)}) collective-permute-start(bf16[192,384]{1,0:T(8,128)(2,1)S(1)} %pad_maximum_fusion.18), channel_id=1, source_target_pairs={{4,0},{8,4},{12,8},{0,12},{20,16},{24,20},{28,24},{16,28},{5,1},{9... | collective-permute-start | bytes 442376 | tf_op jit(solution)/shard_map/ppermute | solution.py:32
  16.6 7.0 %collective-permute-start.8 = (bf16[192,384]{1,0:T(8,128)(2,1)S(1)}, bf16[192,384]{1,0:T(8,128)(2,1)S(1)}, u32[]{:S(2)}, u32[]{:S(2)}) collective-permute-start(bf16[192,384]{1,0:T(8,128)(2,1)S(1)} %pad_maximum_fusion.18), channel_id=1, source_target_pairs={{12,0},{0,4},{4,8},{8,12},{28,16},{16,20},{20,24},{24,28},{13,1},{... | collective-permute-start | bytes 442376 | tf_op jit(solution)/shard_map/ppermute | solution.py:32
  17.7 22.4 %collective-permute-start.4 = (bf16[192,1536]{1,0:T(8,128)(2,1)S(1)}, bf16[192,1536]{1,0:T(8,128)(2,1)S(1)}, u32[]{:S(2)}, u32[]{:S(2)}) collective-permute-start(bf16[192,1536]{1,0:T(8,128)(2,1)S(1)} %get-tuple-element.96), channel_id=1, source_target_pairs={{4,0},{8,4},{12,8},{0,12},{20,16},{24,20},{28,24},{16,28},{5,1},{9... | collective-permute-start | bytes 1769480 | tf_op jit(solution)/shard_map/ppermute | solution.py:32
  18.8 21.3 %collective-permute-start.5 = (bf16[192,1536]{1,0:T(8,128)(2,1)S(1)}, bf16[192,1536]{1,0:T(8,128)(2,1)S(1)}, u32[]{:S(2)}, u32[]{:S(2)}) collective-permute-start(bf16[192,1536]{1,0:T(8,128)(2,1)S(1)} %get-tuple-element.96), channel_id=1, source_target_pairs={{12,0},{0,4},{4,8},{8,12},{28,16},{16,20},{20,24},{24,28},{13,1},{... | collective-permute-start | bytes 1769480 | tf_op jit(solution)/shard_map/ppermute | solution.py:32
  23.6 16.5 %collective-permute-start.9 = (bf16[768,384]{1,0:T(8,128)(2,1)S(1)}, bf16[768,384]{1,0:T(8,128)(2,1)S(1)}, u32[]{:S(2)}, u32[]{:S(2)}) collective-permute-start(bf16[768,384]{1,0:T(8,128)(2,1)S(1)} %constant_dynamic-update-slice_fusion), channel_id=1, source_target_pairs={{32,0},{64,32},{96,64},{0,96},{33,1},{65,33},{97,65},{1,97},{34,2}... | collective-permute-start | bytes 1769480 | tf_op jit(solution)/shard_map/ppermute | solution.py:24
  23.7 16.4 %collective-permute-start.10 = (bf16[768,384]{1,0:T(8,128)(2,1)S(1)}, bf16[768,384]{1,0:T(8,128)(2,1)S(1)}, u32[]{:S(2)}, u32[]{:S(2)}) collective-permute-start(bf16[768,384]{1,0:T(8,128)(2,1)S(1)} %constant_dynamic-update-slice_fusion), channel_id=1, source_target_pairs={{96,0},{0,32},{32,64},{64,96},{97,1},{1,33},{33,65},{65,97},{98,2}... | collective-permute-start | bytes 1769480 | tf_op jit(solution)/shard_map/ppermute | solution.py:24
  25.7 12.8 %collective-permute-start.11 = (bf16[192,768]{1,0:T(8,128)(2,1)S(1)}, bf16[192,768]{1,0:T(8,128)(2,1)S(1)}, u32[]{:S(2)}, u32[]{:S(2)}) collective-permute-start(bf16[192,768]{1,0:T(8,128)(2,1)S(1)} %get-tuple-element.31), channel_id=1, source_target_pairs={{0,0},{1,10},{2,18},{3,24},{4,1},{5,11},{6,19},{7,25},{8,5},{9,15}... | collective-permute-start | bytes 884744 | tf_op jit(solution)/shard_map/ppermute | solution.py:111
  41.6 9.2 %collective-permute-start.13 = (bf16[96,1536]{1,0:T(8,128)(2,1)S(1)}, bf16[96,1536]{1,0:T(8,128)(2,1)S(1)}, u32[]{:S(2)}, u32[]{:S(2)}) collective-permute-start(bf16[96,1536]{1,0:T(8,128)(2,1)S(1)} %slice.181), channel_id=1, source_target_pairs={{12,0},{0,4},{4,8},{8,12},{28,16},{16,20},{20,24},{24,28},{13,1},{... | collective-permute-start | bytes 884744 | tf_op jit(solution)/shard_map/ppermute | solution.py:32
  43.6 7.2 %collective-permute-start.12 = (bf16[96,1536]{1,0:T(8,128)(2,1)S(1)}, bf16[96,1536]{1,0:T(8,128)(2,1)S(1)}, u32[]{:S(2)}, u32[]{:S(2)}) collective-permute-start(bf16[96,1536]{1,0:T(8,128)(2,1)S(1)} %slice.180), channel_id=1, source_target_pairs={{4,0},{8,4},{12,8},{0,12},{20,16},{24,20},{28,24},{16,28},{5,1},{9... | collective-permute-start | bytes 884744 | tf_op jit(solution)/shard_map/ppermute | solution.py:32
  44.5 14.7 %collective-permute-start.15 = (bf16[192,768]{1,0:T(8,128)(2,1)S(1)}, bf16[192,768]{1,0:T(8,128)(2,1)S(1)}, u32[]{:S(2)}, u32[]{:S(2)}) collective-permute-start(bf16[192,768]{1,0:T(8,128)(2,1)S(1)} %get-tuple-element.38), channel_id=1, source_target_pairs={{0,5},{1,15},{2,23},{3,29},{4,4},{5,14},{6,22},{7,28},{8,0},{9,10}... | collective-permute-start | bytes 884744 | tf_op jit(solution)/shard_map/ppermute | solution.py:119
  48.0 8.8 %collective-permute-start.21 = (bf16[384,384]{1,0:T(8,128)(2,1)S(1)}, bf16[384,384]{1,0:T(8,128)(2,1)S(1)}, u32[]{:S(2)}, u32[]{:S(2)}) collective-permute-start(bf16[384,384]{1,0:T(8,128)(2,1)S(1)} %slice.196), channel_id=1, source_target_pairs={{32,0},{64,32},{96,64},{0,96},{33,1},{65,33},{97,65},{1,97},{34,2}... | collective-permute-start | bytes 884744 | tf_op jit(solution)/shard_map/ppermute | solution.py:24
  49.1 9.0 %collective-permute-start.22 = (bf16[384,384]{1,0:T(8,128)(2,1)S(1)}, bf16[384,384]{1,0:T(8,128)(2,1)S(1)}, u32[]{:S(2)}, u32[]{:S(2)}) collective-permute-start(bf16[384,384]{1,0:T(8,128)(2,1)S(1)} %slice.198), channel_id=1, source_target_pairs={{96,0},{0,32},{32,64},{64,96},{97,1},{1,33},{33,65},{65,97},{98,2}... | collective-permute-start | bytes 884744 | tf_op jit(solution)/shard_map/ppermute | solution.py:24
  51.6 7.4 %collective-permute-start.14 = (bf16[384,768]{1,0:T(8,128)(2,1)S(1)}, bf16[384,768]{1,0:T(8,128)(2,1)S(1)}, u32[]{:S(2)}, u32[]{:S(2)}) collective-permute-start(bf16[384,768]{1,0:T(8,128)(2,1)S(1)} %select_convert_fusion.1), channel_id=1, source_target_pairs={{0,1},{1,0},{2,3},{3,2},{4,5},{5,4},{6,7},{7,6},{8,9},{9,8},{10,11... | collective-permute-start | bytes 1769480 | tf_op jit(solution)/shard_map/ppermute | solution.py:50
  58.6 2.3 %collective-permute-start.23 = (bf16[384,768]{1,0:T(8,128)(2,1)S(1)}, bf16[384,768]{1,0:T(8,128)(2,1)S(1)}, u32[]{:S(2)}, u32[]{:S(2)}) collective-permute-start(bf16[384,768]{1,0:T(8,128)(2,1)S(1)} %get-tuple-element.119), channel_id=1, source_target_pairs={{0,1},{1,0},{2,3},{3,2},{4,5},{5,4},{6,7},{7,6},{8,9},{9,8},{10,11... | collective-permute-start | bytes 1769480 | tf_op jit(solution)/shard_map/ppermute | solution.py:50
  59.3 11.4 %collective-permute-start.16 = (bf16[2,96,768]{2,1,0:T(8,128)(2,1)S(1)}, bf16[2,96,768]{2,1,0:T(8,128)(2,1)S(1)}, u32[]{:S(2)}, u32[]{:S(2)}) collective-permute-start(bf16[2,96,768]{2,1,0:T(8,128)(2,1)S(1)} %fusion.38), channel_id=1, source_target_pairs={{0,2},{1,3},{2,0},{3,1},{4,6},{5,7},{6,4},{7,5},{8,10},{9,11},{10,... | collective-permute-start | bytes 884744 | tf_op jit(solution)/shard_map/ppermute | solution.py:46
  61.1 15.9 %collective-permute-start.24 = (bf16[2,96,768]{2,1,0:T(8,128)(2,1)S(1)}, bf16[2,96,768]{2,1,0:T(8,128)(2,1)S(1)}, u32[]{:S(2)}, u32[]{:S(2)}) collective-permute-start(bf16[2,96,768]{2,1,0:T(8,128)(2,1)S(1)} %fusion.39), channel_id=1, source_target_pairs={{0,2},{1,3},{2,0},{3,1},{4,6},{5,7},{6,4},{7,5},{8,10},{9,11},{10,... | collective-permute-start | bytes 884744 | tf_op jit(solution)/shard_map/ppermute | solution.py:46
  71.2 12.1 %collective-permute-start.17 = (bf16[2,96,768]{2,1,0:T(8,128)(2,1)S(1)}, bf16[2,96,768]{2,1,0:T(8,128)(2,1)S(1)}, u32[]{:S(2)}, u32[]{:S(2)}) collective-permute-start(bf16[2,96,768]{2,1,0:T(8,128)(2,1)S(1)} %get-tuple-element.64), channel_id=1, source_target_pairs={{0,2},{1,3},{2,0},{3,1},{4,6},{5,7},{6,4},{7,5},{8,10},{9,11},{10,... | collective-permute-start | bytes 884744 | tf_op jit(solution)/shard_map/ppermute | solution.py:46
  77.5 11.7 %collective-permute-start.25 = (bf16[2,96,768]{2,1,0:T(8,128)(2,1)S(1)}, bf16[2,96,768]{2,1,0:T(8,128)(2,1)S(1)}, u32[]{:S(2)}, u32[]{:S(2)}) collective-permute-start(bf16[2,96,768]{2,1,0:T(8,128)(2,1)S(1)} %get-tuple-element.66), channel_id=1, source_target_pairs={{0,2},{1,3},{2,0},{3,1},{4,6},{5,7},{6,4},{7,5},{8,10},{9,11},{10,... | collective-permute-start | bytes 884744 | tf_op jit(solution)/shard_map/ppermute | solution.py:46
  83.5 6.0 %collective-permute-start.18 = (bf16[384,768]{1,0:T(8,128)(2,1)S(1)}, bf16[384,768]{1,0:T(8,128)(2,1)S(1)}, u32[]{:S(2)}, u32[]{:S(2)}) collective-permute-start(bf16[384,768]{1,0:T(8,128)(2,1)S(1)} %pad_maximum_fusion.10), channel_id=1, source_target_pairs={{0,1},{1,0},{2,3},{3,2},{4,5},{5,4},{6,7},{7,6},{8,9},{9,8},{10,11... | collective-permute-start | bytes 1769480 | tf_op jit(solution)/shard_map/ppermute | solution.py:50
  89.4 2.1 %collective-permute-start.26 = (bf16[384,768]{1,0:T(8,128)(2,1)S(1)}, bf16[384,768]{1,0:T(8,128)(2,1)S(1)}, u32[]{:S(2)}, u32[]{:S(2)}) collective-permute-start(bf16[384,768]{1,0:T(8,128)(2,1)S(1)} %pad_maximum_fusion.11), channel_id=1, source_target_pairs={{0,1},{1,0},{2,3},{3,2},{4,5},{5,4},{6,7},{7,6},{8,9},{9,8},{10,11... | collective-permute-start | bytes 1769480 | tf_op jit(solution)/shard_map/ppermute | solution.py:50
  92.2 16.3 %collective-permute-start.27 = (bf16[384,384]{1,0:T(8,128)(2,1)S(1)}, bf16[384,384]{1,0:T(8,128)(2,1)S(1)}, u32[]{:S(2)}, u32[]{:S(2)}) collective-permute-start(bf16[384,384]{1,0:T(8,128)(2,1)S(1)} %convolution_convert_fusion.2), channel_id=1, source_target_pairs={{96,0},{0,32},{32,64},{64,96},{97,1},{1,33},{33,65},{65,97},{98,2}... | collective-permute-start | bytes 884744 | tf_op jit(solution)/shard_map/ppermute | solution.py:24
  93.2 15.2 %collective-permute-start.28 = (bf16[384,384]{1,0:T(8,128)(2,1)S(1)}, bf16[384,384]{1,0:T(8,128)(2,1)S(1)}, u32[]{:S(2)}, u32[]{:S(2)}) collective-permute-start(bf16[384,384]{1,0:T(8,128)(2,1)S(1)} %convolution_convert_fusion.1), channel_id=1, source_target_pairs={{32,0},{64,32},{96,64},{0,96},{33,1},{65,33},{97,65},{1,97},{34,2}... | collective-permute-start | bytes 884744 | tf_op jit(solution)/shard_map/ppermute | solution.py:24
  96.0 9.2 %collective-permute-start.19 = (bf16[96,1536]{1,0:T(8,128)(2,1)S(1)}, bf16[96,1536]{1,0:T(8,128)(2,1)S(1)}, u32[]{:S(2)}, u32[]{:S(2)}) collective-permute-start(bf16[96,1536]{1,0:T(8,128)(2,1)S(1)} %get-tuple-element.88), channel_id=1, source_target_pairs={{12,0},{0,4},{4,8},{8,12},{28,16},{16,20},{20,24},{24,28},{13,1},{... | collective-permute-start | bytes 884744 | tf_op jit(solution)/shard_map/ppermute | solution.py:32
  97.1 11.3 %collective-permute-start.20 = (bf16[96,1536]{1,0:T(8,128)(2,1)S(1)}, bf16[96,1536]{1,0:T(8,128)(2,1)S(1)}, u32[]{:S(2)}, u32[]{:S(2)}) collective-permute-start(bf16[96,1536]{1,0:T(8,128)(2,1)S(1)} %get-tuple-element.87), channel_id=1, source_target_pairs={{4,0},{8,4},{12,8},{0,12},{20,16},{24,20},{28,24},{16,28},{5,1},{9... | collective-permute-start | bytes 884744 | tf_op jit(solution)/shard_map/ppermute | solution.py:32
  98.1 11.3 %collective-permute-start.29 = (bf16[192,768]{1,0:T(8,128)(2,1)S(1)}, bf16[192,768]{1,0:T(8,128)(2,1)S(1)}, u32[]{:S(2)}, u32[]{:S(2)}) collective-permute-start(bf16[192,768]{1,0:T(8,128)(2,1)S(1)} %get-tuple-element.41), channel_id=1, source_target_pairs={{0,0},{10,1},{18,2},{24,3},{1,4},{11,5},{19,6},{25,7},{5,8},{15,9}... | collective-permute-start | bytes 884744 | tf_op jit(solution)/shard_map/ppermute | solution.py:176
  110.3 14.9 %collective-permute-start.30 = (bf16[192,1536]{1,0:T(8,128)(2,1)S(1)}, bf16[192,1536]{1,0:T(8,128)(2,1)S(1)}, u32[]{:S(2)}, u32[]{:S(2)}) collective-permute-start(bf16[192,1536]{1,0:T(8,128)(2,1)S(1)} %fusion.1), channel_id=1, source_target_pairs={{12,0},{0,4},{4,8},{8,12},{28,16},{16,20},{20,24},{24,28},{13,1},{... | collective-permute-start | bytes 1769480 | tf_op jit(solution)/shard_map/ppermute | solution.py:32
  113.1 14.8 %collective-permute-start.31 = (bf16[192,1536]{1,0:T(8,128)(2,1)S(1)}, bf16[192,1536]{1,0:T(8,128)(2,1)S(1)}, u32[]{:S(2)}, u32[]{:S(2)}) collective-permute-start(bf16[192,1536]{1,0:T(8,128)(2,1)S(1)} %fusion.2), channel_id=1, source_target_pairs={{4,0},{8,4},{12,8},{0,12},{20,16},{24,20},{28,24},{16,28},{5,1},{9... | collective-permute-start | bytes 1769480 | tf_op jit(solution)/shard_map/ppermute | solution.py:32
  114.2 15.5 %collective-permute-start.32 = (bf16[768,384]{1,0:T(8,128)(2,1)S(1)}, bf16[768,384]{1,0:T(8,128)(2,1)S(1)}, u32[]{:S(2)}, u32[]{:S(2)}) collective-permute-start(bf16[768,384]{1,0:T(8,128)(2,1)S(1)} %add_convert_fusion.1), channel_id=1, source_target_pairs={{96,0},{0,32},{32,64},{64,96},{97,1},{1,33},{33,65},{65,97},{98,2}... | collective-permute-start | bytes 1769480 | tf_op jit(solution)/shard_map/ppermute | solution.py:24
  115.1 14.8 %collective-permute-start.33 = (bf16[768,384]{1,0:T(8,128)(2,1)S(1)}, bf16[768,384]{1,0:T(8,128)(2,1)S(1)}, u32[]{:S(2)}, u32[]{:S(2)}) collective-permute-start(bf16[768,384]{1,0:T(8,128)(2,1)S(1)} %add_convert_fusion), channel_id=1, source_target_pairs={{32,0},{64,32},{96,64},{0,96},{33,1},{65,33},{97,65},{1,97},{34,2}... | collective-permute-start | bytes 1769480 | tf_op jit(solution)/shard_map/ppermute | solution.py:24
  119.3 13.8 %collective-permute-start.34 = (bf16[192,768]{1,0:T(8,128)(2,1)S(1)}, bf16[192,768]{1,0:T(8,128)(2,1)S(1)}, u32[]{:S(2)}, u32[]{:S(2)}) collective-permute-start(bf16[192,768]{1,0:T(8,128)(2,1)S(1)} %get-tuple-element.53), channel_id=1, source_target_pairs={{5,0},{15,1},{23,2},{29,3},{4,4},{14,5},{22,6},{28,7},{0,8},{10,9}... | collective-permute-start | bytes 884744 | tf_op jit(solution)/shard_map/ppermute | solution.py:176
  133.2 12.3 %collective-permute-start.40 = (bf16[192,384]{1,0:T(8,128)(2,1)S(1)}, bf16[192,384]{1,0:T(8,128)(2,1)S(1)}, u32[]{:S(2)}, u32[]{:S(2)}) collective-permute-start(bf16[192,384]{1,0:T(8,128)(2,1)S(1)} %get-tuple-element.79), channel_id=1, source_target_pairs={{4,0},{8,4},{12,8},{0,12},{20,16},{24,20},{28,24},{16,28},{5,1},{9... | collective-permute-start | bytes 442376 | tf_op jit(solution)/shard_map/ppermute | solution.py:32
  136.2 10.3 %collective-permute-start.39 = (bf16[192,384]{1,0:T(8,128)(2,1)S(1)}, bf16[192,384]{1,0:T(8,128)(2,1)S(1)}, u32[]{:S(2)}, u32[]{:S(2)}) collective-permute-start(bf16[192,384]{1,0:T(8,128)(2,1)S(1)} %get-tuple-element.80), channel_id=1, source_target_pairs={{8,0},{12,4},{0,8},{4,12},{24,16},{28,20},{16,24},{20,28},{9,1},{1... | collective-permute-start | bytes 442376 | tf_op jit(solution)/shard_map/ppermute | solution.py:32
  137.0 9.5 %collective-permute-start.38 = (bf16[192,384]{1,0:T(8,128)(2,1)S(1)}, bf16[192,384]{1,0:T(8,128)(2,1)S(1)}, u32[]{:S(2)}, u32[]{:S(2)}) collective-permute-start(bf16[192,384]{1,0:T(8,128)(2,1)S(1)} %get-tuple-element.78), channel_id=1, source_target_pairs={{12,0},{0,4},{4,8},{8,12},{28,16},{16,20},{20,24},{24,28},{13,1},{... | collective-permute-start | bytes 442376 | tf_op jit(solution)/shard_map/ppermute | solution.py:32
  138.9 7.9 %collective-permute-start.37 = (bf16[192,384]{1,0:T(8,128)(2,1)S(1)}, bf16[192,384]{1,0:T(8,128)(2,1)S(1)}, u32[]{:S(2)}, u32[]{:S(2)}) collective-permute-start(bf16[192,384]{1,0:T(8,128)(2,1)S(1)} %get-tuple-element.76), channel_id=1, source_target_pairs={{32,0},{64,32},{96,64},{0,96},{33,1},{65,33},{97,65},{1,97},{34,2}... | collective-permute-start | bytes 442376 | tf_op jit(solution)/shard_map/ppermute | solution.py:24
  141.8 8.2 %collective-permute-start.36 = (bf16[192,384]{1,0:T(8,128)(2,1)S(1)}, bf16[192,384]{1,0:T(8,128)(2,1)S(1)}, u32[]{:S(2)}, u32[]{:S(2)}) collective-permute-start(bf16[192,384]{1,0:T(8,128)(2,1)S(1)} %get-tuple-element.77), channel_id=1, source_target_pairs={{64,0},{96,32},{0,64},{32,96},{65,1},{97,33},{1,65},{33,97},{66,2}... | collective-permute-start | bytes 442376 | tf_op jit(solution)/shard_map/ppermute | solution.py:24
  145.4 1.4 copy-start
  145.5 6.4 %collective-permute-start.35 = (bf16[192,384]{1,0:T(8,128)(2,1)S(1)}, bf16[192,384]{1,0:T(8,128)(2,1)S(1)}, u32[]{:S(2)}, u32[]{:S(2)}) collective-permute-start(bf16[192,384]{1,0:T(8,128)(2,1)S(1)} %get-tuple-element.75), channel_id=1, source_target_pairs={{96,0},{0,32},{32,64},{64,96},{97,1},{1,33},{33,65},{65,97},{98,2}... | collective-permute-start | bytes 442376 | tf_op jit(solution)/shard_map/ppermute | solution.py:24
  152.0 5.2 %collective-permute-start.41 = (bf16[192,384]{1,0:T(8,128)(2,1)S(1)}, bf16[192,384]{1,0:T(8,128)(2,1)S(1)}, u32[]{:S(2)}, u32[]{:S(2)}) collective-permute-start(bf16[192,384]{1,0:T(8,128)(2,1)S(1)} %pad_maximum_fusion.19), channel_id=1, source_target_pairs={{0,16},{4,20},{8,24},{12,28},{16,0},{20,4},{24,8},{28,12},{1,17},{... | collective-permute-start | bytes 442376 | tf_op jit(solution)/shard_map/ppermute | solution.py:42

commit v5 on v4

--- a/solution.py
+++ b/solution.py
@@ -116,7 +116,7 @@
     b2_first, b2_second = from_x(b1[: 2 * n], 1), from_x(b3[2 * n :], 3)
     early = dot(b0, w[0]) + dot(b1, w[1]) + dot(b3, w[3])
     at_1 = dot(a1, turned)
-    sent1 = lax.ppermute(after_done(piece1, early, at_1), BOTH, exchange_pairs(1))
+    sent1 = lax.ppermute(after_done(piece1, at_1), BOTH, exchange_pairs(1))
     a2 = jnp.concatenate([a2_first, a2_second], 0)
 
     def over_core(first, second):
@@ -154,9 +154,9 @@
 
     first, second = back_core(gr_a, there_a)
     g0, g2, g1, g3 = first[:n], first[n:], second[:n], second[n:]
-    gb0, gb1 = back_core(gr_b, there_b)
-
     d2 = dot(g2, turned, (1, 1)).astype(bf16)
+    gb0, gb1 = back_core(gr_b, after_done(there_b, d2))
+
     c2_first, c2_second = dot(gb0, w[2], (1, 1)).astype(bf16), dot(gb1, w[2], (1, 1)).astype(bf16)
     up_a, down_a = to_z(d2[:half], 1), to_z(d2[half:], 3)
     up_b, down_b = to_x(c2_first, 1), to_x(c2_second, 3)
@@ -176,9 +176,10 @@
         return lax.ppermute(piece, BOTH, [(t, s) for s, t in exchange_pairs(turn)])
 
     back0 = give_back(0, d2, c2_first, c2_second)
-    up_a, down_a, up_b, down_b, back0 = together(up_a, down_a, up_b, down_b, back0)
+    up_a, down_a, up_b, down_b = together(up_a, down_a, up_b, down_b)
     d1 = (dot(g1, turned, (1, 1)) + before(up_a, half)).astype(bf16)
     d3 = (dot(g3, turned, (1, 1)) + after(down_a, half)).astype(bf16)
+    up_b, down_b, back0 = together(up_b, down_b, back0)
     c1 = (dot(gb, w[1], (1, 1)) + before(up_b, 2 * n)).astype(bf16)
     c3 = (dot(gb, w[3], (1, 1)) + after(down_b, 2 * n)).astype(bf16)
     added = (d1, d3, c1, c3)
@@ -191,9 +192,10 @@
     gb = after_done(gb, d1, c1)
     all_a = jnp.concatenate([a0, a1, a2, a3], 0)
     b2 = jnp.concatenate([b2_first, b2_second], 0)
+    of_a = lax.optimization_barrier(dot(all_a, ga, (0, 0)))
     blocks = []
     for r, b in enumerate((b0, b1, b2, b3)):
-        block = dot(all_a[:, r * cols : (r + 1) * cols], ga, (0, 0)) + dot(b, gb, (0, 0))
+        block = of_a[r * cols : (r + 1) * cols] + dot(b, gb, (0, 0))
         blocks.append(block.astype(bf16))
 
     back1 = give_back(1, *added)

time: 160 us -> 156 us (0.975)
  waiting for transfers between devices: 70 us -> 65.6 us
    ppermute x14, waiting for transfers between devices: 16.6 us -> 7.55 us  [from_z(): lax.ppermute(v, 'ja', [(y * 4 + (z + r) % N_RING, y * 4 + z) for y in ran...]
    ppermute x2, waiting for transfers between devices: 0.91 us -> 5.02 us  [give_back(): return lax.ppermute(piece, BOTH, [(t, s) for s, t in exchange_pairs(turn)])]
    ppermute x4, waiting for transfers between devices: 22.3 us -> 19.3 us  [swap_y_hi(): return lax.ppermute(v, 'ka', [(k, k ^ 2) for k in range(4)])]
    ppermute x14, waiting for transfers between devices: 13.1 us -> 15.7 us  [from_x(): return lax.ppermute(v, 'ia', [((i + r) % N_RING, i) for i in range(N_RING)])]
    ppermute x14, starting transfers between devices: 19 us -> 20.7 us  [from_z(): lax.ppermute(v, 'ja', [(y * 4 + (z + r) % N_RING, y * 4 + z) for y in ran...]
    dot_general x26 -> x23, matrix products: 18.2 us -> 17.7 us  [dot(): lax.dot_general(a, b, (((dims[0],), (dims[1],)), ((), ())), preferred_ele...]
  transfers between devices with their start and end apart: 42 -> 42, of which waited for: 24 -> 23; matrix products, arithmetic and copies ran while one was open for 13% -> 14% of each run, Pallas kernels for 0% -> 0%
where the time goes in v5:
time: 156 us; the launch traced here: 153 us
  waiting for transfers between devices  65.6 us (42%)
  starting transfers between devices  61.2 us (39%)
  matrix products  17.7 us (11%)
  other arithmetic  5.03 us (3%)
  local copies, waits for them, and re-layouts  2.34 us (2%)
    ppermute x14, starting transfers between devices, from_z(): lax.ppermute(v, 'ja', [(y * 4 + (z + r) % N_RING, y * 4 + z) for y in ran...  20.7 us
    ppermute x4, waiting for transfers between devices, swap_y_hi(): return lax.ppermute(v, 'ka', [(k, k ^ 2) for k in range(4)])  19.3 us
    ppermute x14, starting transfers between devices, from_x(): return lax.ppermute(v, 'ia', [((i + r) % N_RING, i) for i in range(N_RING)])  19.1 us
    dot_general x23, matrix products, dot(): lax.dot_general(a, b, (((dims[0],), (dims[1],)), ((), ())), preferred_ele...  17.7 us
    ppermute x14, waiting for transfers between devices, from_x(): return lax.ppermute(v, 'ia', [((i + r) % N_RING, i) for i in range(N_RING)])  15.7 us
    ppermute x1, waiting for transfers between devices, on_device(): sent0 = lax.ppermute(after_done(piece0, a0, b0), BOTH, exchange_pairs(0))  9.08 us
    ppermute x2, starting transfers between devices, give_back(): return lax.ppermute(piece, BOTH, [(t, s) for s, t in exchange_pairs(turn)])  7.64 us
    ppermute x14, waiting for transfers between devices, from_z(): lax.ppermute(v, 'ja', [(y * 4 + (z + r) % N_RING, y * 4 + z) for y in ran...  7.55 us
  transfers between devices with their start and end apart: 42, of which 23 were waited for; matrix products, arithmetic and copies ran while one was open for 14% of the time, Pallas kernels for 0%

profile of v5, /device:TPU:40, one launch (start us, length us, event | category | flops | bytes accessed | tf_op | source)
XLA Modules:
  0.0 153.3 jit_solution(2319268460890991646)
XLA Ops:
  2.1 4.4 %collective-permute-done = bf16[192,384]{1,0:T(8,128)(2,1)S(1)} collective-permute-done((bf16[192,384]{1,0:T(8,128)(2,1)}, bf16[192,384]{1,0:T(8,128)(2,1)S(1)}, u32[]{:S(2)}, u32[]{:S(2)}) %collective-permute-start) | collective-permute-done | bytes 147488 | tf_op jit(solution)/shard_map/ppermute | solution.py:42
  6.6 1.6 %collective-permute-start.3 = (bf16[192,384]{1,0:T(8,128)(2,1)S(1)}, bf16[192,384]{1,0:T(8,128)(2,1)S(1)}, u32[]{:S(2)}, u32[]{:S(2)}) collective-permute-start(bf16[192,384]{1,0:T(8,128)(2,1)S(1)} %pad_maximum_fusion.17), channel_id=1, source_target_pairs={{96,0},{0,32},{32,64},{64,96},{97,1},{1,33},{33,65},{65,97},{98,2}... | collective-permute-start | bytes 442376 | tf_op jit(solution)/shard_map/ppermute | solution.py:24
  8.1 2.7 %collective-permute-start.2 = (bf16[192,384]{1,0:T(8,128)(2,1)S(1)}, bf16[192,384]{1,0:T(8,128)(2,1)S(1)}, u32[]{:S(2)}, u32[]{:S(2)}) collective-permute-start(bf16[192,384]{1,0:T(8,128)(2,1)S(1)} %pad_maximum_fusion.17), channel_id=1, source_target_pairs={{64,0},{96,32},{0,64},{32,96},{65,1},{97,33},{1,65},{33,97},{66,2}... | collective-permute-start | bytes 442376 | tf_op jit(solution)/shard_map/ppermute | solution.py:24
  10.9 1.4 collective-permute-start.1
  12.5 3.1 %collective-permute-start.6 = (bf16[192,384]{1,0:T(8,128)(2,1)S(1)}, bf16[192,384]{1,0:T(8,128)(2,1)S(1)}, u32[]{:S(2)}, u32[]{:S(2)}) collective-permute-start(bf16[192,384]{1,0:T(8,128)(2,1)S(1)} %pad_maximum_fusion.18), channel_id=1, source_target_pairs={{8,0},{12,4},{0,8},{4,12},{24,16},{28,20},{16,24},{20,28},{9,1},{1... | collective-permute-start | bytes 442376 | tf_op jit(solution)/shard_map/ppermute | solution.py:32
  15.5 1.0 collective-permute-start.7
  16.6 1.0 collective-permute-start.8
  17.7 1.1 collective-permute-start.4
  18.8 1.0 collective-permute-start.5
  20.3 2.7 %collective-permute-done.7 = bf16[192,384]{1,0:T(8,128)(2,1)S(1)} collective-permute-done((bf16[192,384]{1,0:T(8,128)(2,1)S(1)}, bf16[192,384]{1,0:T(8,128)(2,1)S(1)}, u32[]{:S(2)}, u32[]{:S(2)}) %collective-permute-start.7) | collective-permute-done | bytes 147488 | tf_op jit(solution)/shard_map/ppermute | solution.py:32
  23.7 2.0 %collective-permute-start.10 = (bf16[768,384]{1,0:T(8,128)(2,1)S(1)}, bf16[768,384]{1,0:T(8,128)(2,1)S(1)}, u32[]{:S(2)}, u32[]{:S(2)}) collective-permute-start(bf16[768,384]{1,0:T(8,128)(2,1)S(1)} %constant_dynamic-update-slice_fusion), channel_id=1, source_target_pairs={{96,0},{0,32},{32,64},{64,96},{97,1},{1,33},{33,65},{65,97},{98,2}... | collective-permute-start | bytes 1769480 | tf_op jit(solution)/shard_map/ppermute | solution.py:24
  25.7 1.9 %collective-permute-start.11 = (bf16[192,768]{1,0:T(8,128)(2,1)S(1)}, bf16[192,768]{1,0:T(8,128)(2,1)S(1)}, u32[]{:S(2)}, u32[]{:S(2)}) collective-permute-start(bf16[192,768]{1,0:T(8,128)(2,1)S(1)} %get-tuple-element.34), channel_id=1, source_target_pairs={{0,0},{1,10},{2,18},{3,24},{4,1},{5,11},{6,19},{7,25},{8,5},{9,15}... | collective-permute-start | bytes 884744 | tf_op jit(solution)/shard_map/ppermute | solution.py:111
  29.4 9.1 %collective-permute-done.11 = bf16[192,768]{1,0:T(8,128)(2,1)S(1)} collective-permute-done((bf16[192,768]{1,0:T(8,128)(2,1)S(1)}, bf16[192,768]{1,0:T(8,128)(2,1)S(1)}, u32[]{:S(2)}, u32[]{:S(2)}) %collective-permute-start.11) | collective-permute-done | bytes 294944 | tf_op jit(solution)/shard_map/ppermute | solution.py:111
  38.5 1.6 %collective-permute-done.4 = bf16[192,1536]{1,0:T(8,128)(2,1)S(1)} collective-permute-done((bf16[192,1536]{1,0:T(8,128)(2,1)S(1)}, bf16[192,1536]{1,0:T(8,128)(2,1)S(1)}, u32[]{:S(2)}, u32[]{:S(2)}) %collective-permute-start.4) | collective-permute-done | bytes 589856 | tf_op jit(solution)/shard_map/ppermute | solution.py:32
  41.6 2.0 %collective-permute-start.13 = (bf16[96,1536]{1,0:T(8,128)(2,1)S(1)}, bf16[96,1536]{1,0:T(8,128)(2,1)S(1)}, u32[]{:S(2)}, u32[]{:S(2)}) collective-permute-start(bf16[96,1536]{1,0:T(8,128)(2,1)S(1)} %slice.181), channel_id=1, source_target_pairs={{12,0},{0,4},{4,8},{8,12},{28,16},{16,20},{20,24},{24,28},{13,1},{... | collective-permute-start | bytes 884744 | tf_op jit(solution)/shard_map/ppermute | solution.py:32
  43.7 3.5 %collective-permute-start.15 = (bf16[192,768]{1,0:T(8,128)(2,1)S(1)}, bf16[192,768]{1,0:T(8,128)(2,1)S(1)}, u32[]{:S(2)}, u32[]{:S(2)}) collective-permute-start(bf16[192,768]{1,0:T(8,128)(2,1)S(1)} %get-tuple-element.39), channel_id=1, source_target_pairs={{0,5},{1,15},{2,23},{3,29},{4,4},{5,14},{6,22},{7,28},{8,0},{9,10}... | collective-permute-start | bytes 884744 | tf_op jit(solution)/shard_map/ppermute | solution.py:119
  47.2 1.2 collective-permute-start.21
  48.4 1.0 collective-permute-start.22
  51.7 4.3 %collective-permute-done.21 = bf16[384,384]{1,0:T(8,128)(2,1)S(1)} collective-permute-done((bf16[384,384]{1,0:T(8,128)(2,1)S(1)}, bf16[384,384]{1,0:T(8,128)(2,1)S(1)}, u32[]{:S(2)}, u32[]{:S(2)}) %collective-permute-start.21) | collective-permute-done | bytes 294944 | tf_op jit(solution)/shard_map/ppermute | solution.py:24
  58.5 1.1 collective-permute-start.16
  60.3 2.1 %collective-permute-start.24 = (bf16[2,96,768]{2,1,0:T(8,128)(2,1)S(1)}, bf16[2,96,768]{2,1,0:T(8,128)(2,1)S(1)}, u32[]{:S(2)}, u32[]{:S(2)}) collective-permute-start(bf16[2,96,768]{2,1,0:T(8,128)(2,1)S(1)} %fusion.37), channel_id=1, source_target_pairs={{0,2},{1,3},{2,0},{3,1},{4,6},{5,7},{6,4},{7,5},{8,10},{9,11},{10,... | collective-permute-start | bytes 884744 | tf_op jit(solution)/shard_map/ppermute | solution.py:46
  62.6 7.3 %collective-permute-done.16 = bf16[2,96,768]{2,1,0:T(8,128)(2,1)S(1)} collective-permute-done((bf16[2,96,768]{2,1,0:T(8,128)(2,1)S(1)}, bf16[2,96,768]{2,1,0:T(8,128)(2,1)S(1)}, u32[]{:S(2)}, u32[]{:S(2)}) %collective-permute-start.16) | collective-permute-done | bytes 294944 | tf_op jit(solution)/shard_map/ppermute | solution.py:46
  70.4 1.1 collective-permute-start.17
  71.5 4.7 %collective-permute-done.24 = bf16[2,96,768]{2,1,0:T(8,128)(2,1)S(1)} collective-permute-done((bf16[2,96,768]{2,1,0:T(8,128)(2,1)S(1)}, bf16[2,96,768]{2,1,0:T(8,128)(2,1)S(1)}, u32[]{:S(2)}, u32[]{:S(2)}) %collective-permute-start.24) | collective-permute-done | bytes 294944 | tf_op jit(solution)/shard_map/ppermute | solution.py:46
  76.7 1.1 collective-permute-start.25
  77.8 4.8 %collective-permute-done.17 = bf16[2,96,768]{2,1,0:T(8,128)(2,1)S(1)} collective-permute-done((bf16[2,96,768]{2,1,0:T(8,128)(2,1)S(1)}, bf16[2,96,768]{2,1,0:T(8,128)(2,1)S(1)}, u32[]{:S(2)}, u32[]{:S(2)}) %collective-permute-start.17) | collective-permute-done | bytes 294944 | tf_op jit(solution)/shard_map/ppermute | solution.py:46
  82.9 1.8 %collective-permute-done.18 = bf16[384,768]{1,0:T(8,128)(2,1)S(1)} collective-permute-done((bf16[384,768]{1,0:T(8,128)(2,1)S(1)}, bf16[384,768]{1,0:T(8,128)(2,1)S(1)}, u32[]{:S(2)}, u32[]{:S(2)}) %collective-permute-start.18) | collective-permute-done | bytes 589856 | tf_op jit(solution)/shard_map/ppermute | solution.py:50
  85.9 2.5 %collective-permute-done.25 = bf16[2,96,768]{2,1,0:T(8,128)(2,1)S(1)} collective-permute-done((bf16[2,96,768]{2,1,0:T(8,128)(2,1)S(1)}, bf16[2,96,768]{2,1,0:T(8,128)(2,1)S(1)}, u32[]{:S(2)}, u32[]{:S(2)}) %collective-permute-start.25) | collective-permute-done | bytes 294944 | tf_op jit(solution)/shard_map/ppermute | solution.py:46
  88.7 1.1 collective-permute-start.19
  92.7 2.8 %collective-permute-start.28 = (bf16[384,384]{1,0:T(8,128)(2,1)S(1)}, bf16[384,384]{1,0:T(8,128)(2,1)S(1)}, u32[]{:S(2)}, u32[]{:S(2)}) collective-permute-start(bf16[384,384]{1,0:T(8,128)(2,1)S(1)} %convolution_convert_fusion.1), channel_id=1, source_target_pairs={{32,0},{64,32},{96,64},{0,96},{33,1},{65,33},{97,65},{1,97},{34,2}... | collective-permute-start | bytes 884744 | tf_op jit(solution)/shard_map/ppermute | solution.py:24
  95.5 3.1 %collective-permute-start.29 = (bf16[192,768]{1,0:T(8,128)(2,1)S(1)}, bf16[192,768]{1,0:T(8,128)(2,1)S(1)}, u32[]{:S(2)}, u32[]{:S(2)}) collective-permute-start(bf16[192,768]{1,0:T(8,128)(2,1)S(1)} %get-tuple-element.47), channel_id=1, source_target_pairs={{0,0},{10,1},{18,2},{24,3},{1,4},{11,5},{19,6},{25,7},{5,8},{15,9}... | collective-permute-start | bytes 884744 | tf_op jit(solution)/shard_map/ppermute | solution.py:176
  99.0 2.8 %collective-permute-done.27 = bf16[384,384]{1,0:T(8,128)(2,1)S(1)} collective-permute-done((bf16[384,384]{1,0:T(8,128)(2,1)S(1)}, bf16[384,384]{1,0:T(8,128)(2,1)S(1)}, u32[]{:S(2)}, u32[]{:S(2)}) %collective-permute-start.27) | collective-permute-done | bytes 294944 | tf_op jit(solution)/shard_map/ppermute | solution.py:24
  101.8 5.0 %collective-permute-done.29 = bf16[192,768]{1,0:T(8,128)(2,1)S(1)} collective-permute-done((bf16[192,768]{1,0:T(8,128)(2,1)S(1)}, bf16[192,768]{1,0:T(8,128)(2,1)S(1)}, u32[]{:S(2)}, u32[]{:S(2)}) %collective-permute-start.29) | collective-permute-done | bytes 294944 | tf_op jit(solution)/shard_map/ppermute | solution.py:176
  107.7 1.8 %collective-permute-start.30 = (bf16[192,1536]{1,0:T(8,128)(2,1)S(1)}, bf16[192,1536]{1,0:T(8,128)(2,1)S(1)}, u32[]{:S(2)}, u32[]{:S(2)}) collective-permute-start(bf16[192,1536]{1,0:T(8,128)(2,1)S(1)} %fusion.1), channel_id=1, source_target_pairs={{12,0},{0,4},{4,8},{8,12},{28,16},{16,20},{20,24},{24,28},{13,1},{... | collective-permute-start | bytes 1769480 | tf_op jit(solution)/shard_map/ppermute | solution.py:32
  112.5 3.3 %collective-permute-start.33 = (bf16[768,384]{1,0:T(8,128)(2,1)S(1)}, bf16[768,384]{1,0:T(8,128)(2,1)S(1)}, u32[]{:S(2)}, u32[]{:S(2)}) collective-permute-start(bf16[768,384]{1,0:T(8,128)(2,1)S(1)} %add_convert_fusion), channel_id=1, source_target_pairs={{32,0},{64,32},{96,64},{0,96},{33,1},{65,33},{97,65},{1,97},{34,2}... | collective-permute-start | bytes 1769480 | tf_op jit(solution)/shard_map/ppermute | solution.py:24
  116.6 4.6 %collective-permute-start.34 = (bf16[192,768]{1,0:T(8,128)(2,1)S(1)}, bf16[192,768]{1,0:T(8,128)(2,1)S(1)}, u32[]{:S(2)}, u32[]{:S(2)}) collective-permute-start(bf16[192,768]{1,0:T(8,128)(2,1)S(1)} %get-tuple-element.59), channel_id=1, source_target_pairs={{5,0},{15,1},{23,2},{29,3},{4,4},{14,5},{22,6},{28,7},{0,8},{10,9}... | collective-permute-start | bytes 884744 | tf_op jit(solution)/shard_map/ppermute | solution.py:176
  121.2 2.1 %fusion.60 = f32[1536,768]{1,0:T(8,128)S(1)} fusion(bf16[768,1536]{1,0:T(8,128)(2,1)S(1)} %constant_dynamic-update-slice_fusion.7, bf16[768,768]{1,0:T(8,128)(2,1)S(1)} %pad_maximum_fusion.3), kind=kOutput, calls=%fused_computation.158 | convolution fusion | flops 1811939328 | bytes 8257536 | tf_op jit(solution)/shard_map/dot_general | solution.py:67
  123.3 2.0 %collective-permute-done.31 = bf16[192,1536]{1,0:T(8,128)(2,1)S(1)} collective-permute-done((bf16[192,1536]{1,0:T(8,128)(2,1)S(1)}, bf16[192,1536]{1,0:T(8,128)(2,1)S(1)}, u32[]{:S(2)}, u32[]{:S(2)}) %collective-permute-start.31) | collective-permute-done | bytes 589856 | tf_op jit(solution)/shard_map/ppermute | solution.py:32
  125.3 2.2 %collective-permute-done.32 = bf16[768,384]{1,0:T(8,128)(2,1)S(1)} collective-permute-done((bf16[768,384]{1,0:T(8,128)(2,1)S(1)}, bf16[768,384]{1,0:T(8,128)(2,1)S(1)}, u32[]{:S(2)}, u32[]{:S(2)}) %collective-permute-start.32) | collective-permute-done | bytes 589856 | tf_op jit(solution)/shard_map/ppermute | solution.py:24
  128.9 3.1 %collective-permute-start.40 = (bf16[192,384]{1,0:T(8,128)(2,1)S(1)}, bf16[192,384]{1,0:T(8,128)(2,1)S(1)}, u32[]{:S(2)}, u32[]{:S(2)}) collective-permute-start(bf16[192,384]{1,0:T(8,128)(2,1)S(1)} %get-tuple-element.85), channel_id=1, source_target_pairs={{4,0},{8,4},{12,8},{0,12},{20,16},{24,20},{28,24},{16,28},{5,1},{9... | collective-permute-start | bytes 442376 | tf_op jit(solution)/shard_map/ppermute | solution.py:32
  132.0 2.3 %collective-permute-start.39 = (bf16[192,384]{1,0:T(8,128)(2,1)S(1)}, bf16[192,384]{1,0:T(8,128)(2,1)S(1)}, u32[]{:S(2)}, u32[]{:S(2)}) collective-permute-start(bf16[192,384]{1,0:T(8,128)(2,1)S(1)} %get-tuple-element.86), channel_id=1, source_target_pairs={{8,0},{12,4},{0,8},{4,12},{24,16},{28,20},{16,24},{20,28},{9,1},{1... | collective-permute-start | bytes 442376 | tf_op jit(solution)/shard_map/ppermute | solution.py:32
  134.3 1.7 %collective-permute-start.38 = (bf16[192,384]{1,0:T(8,128)(2,1)S(1)}, bf16[192,384]{1,0:T(8,128)(2,1)S(1)}, u32[]{:S(2)}, u32[]{:S(2)}) collective-permute-start(bf16[192,384]{1,0:T(8,128)(2,1)S(1)} %get-tuple-element.84), channel_id=1, source_target_pairs={{12,0},{0,4},{4,8},{8,12},{28,16},{16,20},{20,24},{24,28},{13,1},{... | collective-permute-start | bytes 442376 | tf_op jit(solution)/shard_map/ppermute | solution.py:32
  136.2 1.4 collective-permute-start.37
  140.6 1.0 collective-permute-start.35
  141.9 3.9 %collective-permute-done.36 = bf16[192,384]{1,0:T(8,128)(2,1)S(1)} collective-permute-done((bf16[192,384]{1,0:T(8,128)(2,1)S(1)}, bf16[192,384]{1,0:T(8,128)(2,1)S(1)}, u32[]{:S(2)}, u32[]{:S(2)}) %collective-permute-start.36) | collective-permute-done | bytes 147488 | tf_op jit(solution)/shard_map/ppermute | solution.py:24
  145.8 1.5 collective-permute-done.35
  147.4 2.1 %collective-permute-start.41 = (bf16[192,384]{1,0:T(8,128)(2,1)S(1)}, bf16[192,384]{1,0:T(8,128)(2,1)S(1)}, u32[]{:S(2)}, u32[]{:S(2)}) collective-permute-start(bf16[192,384]{1,0:T(8,128)(2,1)S(1)} %pad_maximum_fusion.19), channel_id=1, source_target_pairs={{0,16},{4,20},{8,24},{12,28},{16,0},{20,4},{24,8},{28,12},{1,17},{... | collective-permute-start | bytes 442376 | tf_op jit(solution)/shard_map/ppermute | solution.py:42
  150.4 2.3 %collective-permute-done.41 = bf16[192,384]{1,0:T(8,128)(2,1)S(1)} collective-permute-done((bf16[192,384]{1,0:T(8,128)(2,1)S(1)}, bf16[192,384]{1,0:T(8,128)(2,1)S(1)}, u32[]{:S(2)}, u32[]{:S(2)}) %collective-permute-start.41) | collective-permute-done | bytes 147488 | tf_op jit(solution)/shard_map/ppermute | solution.py:42
  (130 shorter events, 29.0 us)
Async XLA Ops:
  0.6 11.7 %copy-start.2 = (bf16[192,1536]{1,0:T(8,128)(2,1)S(1)}, bf16[192,1536]{1,0:T(8,128)(2,1)}, u32[]{:S(2)}) copy-start(bf16[192,1536]{1,0:T(8,128)(2,1)} %param.5) | copy-start | bytes 1769476
  0.6 5.9 %collective-permute-start = (bf16[192,384]{1,0:T(8,128)(2,1)}, bf16[192,384]{1,0:T(8,128)(2,1)S(1)}, u32[]{:S(2)}, u32[]{:S(2)}) collective-permute-start(bf16[192,384]{1,0:T(8,128)(2,1)} %param.3), channel_id=1, source_target_pairs={{0,16},{4,20},{8,24},{12,28},{16,0},{20,4},{24,8},{28,12},{1,17},{... | collective-permute-start | bytes 442376 | tf_op jit(solution)/shard_map/ppermute | solution.py:42
  6.6 10.0 %collective-permute-start.3 = (bf16[192,384]{1,0:T(8,128)(2,1)S(1)}, bf16[192,384]{1,0:T(8,128)(2,1)S(1)}, u32[]{:S(2)}, u32[]{:S(2)}) collective-permute-start(bf16[192,384]{1,0:T(8,128)(2,1)S(1)} %pad_maximum_fusion.17), channel_id=1, source_target_pairs={{96,0},{0,32},{32,64},{64,96},{97,1},{1,33},{33,65},{65,97},{98,2}... | collective-permute-start | bytes 442376 | tf_op jit(solution)/shard_map/ppermute | solution.py:24
  8.1 9.4 %collective-permute-start.2 = (bf16[192,384]{1,0:T(8,128)(2,1)S(1)}, bf16[192,384]{1,0:T(8,128)(2,1)S(1)}, u32[]{:S(2)}, u32[]{:S(2)}) collective-permute-start(bf16[192,384]{1,0:T(8,128)(2,1)S(1)} %pad_maximum_fusion.17), channel_id=1, source_target_pairs={{64,0},{96,32},{0,64},{32,96},{65,1},{97,33},{1,65},{33,97},{66,2}... | collective-permute-start | bytes 442376 | tf_op jit(solution)/shard_map/ppermute | solution.py:24
  10.9 6.7 %collective-permute-start.1 = (bf16[192,384]{1,0:T(8,128)(2,1)S(1)}, bf16[192,384]{1,0:T(8,128)(2,1)S(1)}, u32[]{:S(2)}, u32[]{:S(2)}) collective-permute-start(bf16[192,384]{1,0:T(8,128)(2,1)S(1)} %pad_maximum_fusion.17), channel_id=1, source_target_pairs={{32,0},{64,32},{96,64},{0,96},{33,1},{65,33},{97,65},{1,97},{34,2}... | collective-permute-start | bytes 442376 | tf_op jit(solution)/shard_map/ppermute | solution.py:24
  12.5 15.1 %copy-start.1 = (bf16[1536,768]{1,0:T(8,128)(2,1)S(1)}, bf16[1536,768]{1,0:T(8,128)(2,1)}, u32[]{:S(2)}) copy-start(bf16[1536,768]{1,0:T(8,128)(2,1)} %param.4) | copy-start | bytes 7077892
  12.5 7.8 %collective-permute-start.6 = (bf16[192,384]{1,0:T(8,128)(2,1)S(1)}, bf16[192,384]{1,0:T(8,128)(2,1)S(1)}, u32[]{:S(2)}, u32[]{:S(2)}) collective-permute-start(bf16[192,384]{1,0:T(8,128)(2,1)S(1)} %pad_maximum_fusion.18), channel_id=1, source_target_pairs={{8,0},{12,4},{0,8},{4,12},{24,16},{28,20},{16,24},{20,28},{9,1},{1... | collective-permute-start | bytes 442376 | tf_op jit(solution)/shard_map/ppermute | solution.py:32
  15.5 7.5 %collective-permute-start.7 = (bf16[192,384]{1,0:T(8,128)(2,1)S(1)}, bf16[192,384]{1,0:T(8,128)(2,1)S(1)}, u32[]{:S(2)}, u32[]{:S(2)}) collective-permute-start(bf16[192,384]{1,0:T(8,128)(2,1)S(1)} %pad_maximum_fusion.18), channel_id=1, source_target_pairs={{4,0},{8,4},{12,8},{0,12},{20,16},{24,20},{28,24},{16,28},{5,1},{9... | collective-permute-start | bytes 442376 | tf_op jit(solution)/shard_map/ppermute | solution.py:32
  16.6 7.0 %collective-permute-start.8 = (bf16[192,384]{1,0:T(8,128)(2,1)S(1)}, bf16[192,384]{1,0:T(8,128)(2,1)S(1)}, u32[]{:S(2)}, u32[]{:S(2)}) collective-permute-start(bf16[192,384]{1,0:T(8,128)(2,1)S(1)} %pad_maximum_fusion.18), channel_id=1, source_target_pairs={{12,0},{0,4},{4,8},{8,12},{28,16},{16,20},{20,24},{24,28},{13,1},{... | collective-permute-start | bytes 442376 | tf_op jit(solution)/shard_map/ppermute | solution.py:32
  17.7 22.4 %collective-permute-start.4 = (bf16[192,1536]{1,0:T(8,128)(2,1)S(1)}, bf16[192,1536]{1,0:T(8,128)(2,1)S(1)}, u32[]{:S(2)}, u32[]{:S(2)}) collective-permute-start(bf16[192,1536]{1,0:T(8,128)(2,1)S(1)} %get-tuple-element.102), channel_id=1, source_target_pairs={{4,0},{8,4},{12,8},{0,12},{20,16},{24,20},{28,24},{16,28},{5,1},{9... | collective-permute-start | bytes 1769480 | tf_op jit(solution)/shard_map/ppermute | solution.py:32
  18.8 21.3 %collective-permute-start.5 = (bf16[192,1536]{1,0:T(8,128)(2,1)S(1)}, bf16[192,1536]{1,0:T(8,128)(2,1)S(1)}, u32[]{:S(2)}, u32[]{:S(2)}) collective-permute-start(bf16[192,1536]{1,0:T(8,128)(2,1)S(1)} %get-tuple-element.102), channel_id=1, source_target_pairs={{12,0},{0,4},{4,8},{8,12},{28,16},{16,20},{20,24},{24,28},{13,1},{... | collective-permute-start | bytes 1769480 | tf_op jit(solution)/shard_map/ppermute | solution.py:32
  23.6 16.5 %collective-permute-start.9 = (bf16[768,384]{1,0:T(8,128)(2,1)S(1)}, bf16[768,384]{1,0:T(8,128)(2,1)S(1)}, u32[]{:S(2)}, u32[]{:S(2)}) collective-permute-start(bf16[768,384]{1,0:T(8,128)(2,1)S(1)} %constant_dynamic-update-slice_fusion), channel_id=1, source_target_pairs={{32,0},{64,32},{96,64},{0,96},{33,1},{65,33},{97,65},{1,97},{34,2}... | collective-permute-start | bytes 1769480 | tf_op jit(solution)/shard_map/ppermute | solution.py:24
  23.7 16.4 %collective-permute-start.10 = (bf16[768,384]{1,0:T(8,128)(2,1)S(1)}, bf16[768,384]{1,0:T(8,128)(2,1)S(1)}, u32[]{:S(2)}, u32[]{:S(2)}) collective-permute-start(bf16[768,384]{1,0:T(8,128)(2,1)S(1)} %constant_dynamic-update-slice_fusion), channel_id=1, source_target_pairs={{96,0},{0,32},{32,64},{64,96},{97,1},{1,33},{33,65},{65,97},{98,2}... | collective-permute-start | bytes 1769480 | tf_op jit(solution)/shard_map/ppermute | solution.py:24
  25.7 12.8 %collective-permute-start.11 = (bf16[192,768]{1,0:T(8,128)(2,1)S(1)}, bf16[192,768]{1,0:T(8,128)(2,1)S(1)}, u32[]{:S(2)}, u32[]{:S(2)}) collective-permute-start(bf16[192,768]{1,0:T(8,128)(2,1)S(1)} %get-tuple-element.34), channel_id=1, source_target_pairs={{0,0},{1,10},{2,18},{3,24},{4,1},{5,11},{6,19},{7,25},{8,5},{9,15}... | collective-permute-start | bytes 884744 | tf_op jit(solution)/shard_map/ppermute | solution.py:111
  41.6 9.2 %collective-permute-start.13 = (bf16[96,1536]{1,0:T(8,128)(2,1)S(1)}, bf16[96,1536]{1,0:T(8,128)(2,1)S(1)}, u32[]{:S(2)}, u32[]{:S(2)}) collective-permute-start(bf16[96,1536]{1,0:T(8,128)(2,1)S(1)} %slice.181), channel_id=1, source_target_pairs={{12,0},{0,4},{4,8},{8,12},{28,16},{16,20},{20,24},{24,28},{13,1},{... | collective-permute-start | bytes 884744 | tf_op jit(solution)/shard_map/ppermute | solution.py:32
  43.6 7.3 %collective-permute-start.12 = (bf16[96,1536]{1,0:T(8,128)(2,1)S(1)}, bf16[96,1536]{1,0:T(8,128)(2,1)S(1)}, u32[]{:S(2)}, u32[]{:S(2)}) collective-permute-start(bf16[96,1536]{1,0:T(8,128)(2,1)S(1)} %slice.180), channel_id=1, source_target_pairs={{4,0},{8,4},{12,8},{0,12},{20,16},{24,20},{28,24},{16,28},{5,1},{9... | collective-permute-start | bytes 884744 | tf_op jit(solution)/shard_map/ppermute | solution.py:32
  43.7 14.7 %collective-permute-start.15 = (bf16[192,768]{1,0:T(8,128)(2,1)S(1)}, bf16[192,768]{1,0:T(8,128)(2,1)S(1)}, u32[]{:S(2)}, u32[]{:S(2)}) collective-permute-start(bf16[192,768]{1,0:T(8,128)(2,1)S(1)} %get-tuple-element.39), channel_id=1, source_target_pairs={{0,5},{1,15},{2,23},{3,29},{4,4},{5,14},{6,22},{7,28},{8,0},{9,10}... | collective-permute-start | bytes 884744 | tf_op jit(solution)/shard_map/ppermute | solution.py:119
  47.2 8.8 %collective-permute-start.21 = (bf16[384,384]{1,0:T(8,128)(2,1)S(1)}, bf16[384,384]{1,0:T(8,128)(2,1)S(1)}, u32[]{:S(2)}, u32[]{:S(2)}) collective-permute-start(bf16[384,384]{1,0:T(8,128)(2,1)S(1)} %slice.196), channel_id=1, source_target_pairs={{32,0},{64,32},{96,64},{0,96},{33,1},{65,33},{97,65},{1,97},{34,2}... | collective-permute-start | bytes 884744 | tf_op jit(solution)/shard_map/ppermute | solution.py:24
  48.4 9.0 %collective-permute-start.22 = (bf16[384,384]{1,0:T(8,128)(2,1)S(1)}, bf16[384,384]{1,0:T(8,128)(2,1)S(1)}, u32[]{:S(2)}, u32[]{:S(2)}) collective-permute-start(bf16[384,384]{1,0:T(8,128)(2,1)S(1)} %slice.198), channel_id=1, source_target_pairs={{96,0},{0,32},{32,64},{64,96},{97,1},{1,33},{33,65},{65,97},{98,2}... | collective-permute-start | bytes 884744 | tf_op jit(solution)/shard_map/ppermute | solution.py:24
  51.6 6.6 %collective-permute-start.14 = (bf16[384,768]{1,0:T(8,128)(2,1)S(1)}, bf16[384,768]{1,0:T(8,128)(2,1)S(1)}, u32[]{:S(2)}, u32[]{:S(2)}) collective-permute-start(bf16[384,768]{1,0:T(8,128)(2,1)S(1)} %select_convert_fusion.1), channel_id=1, source_target_pairs={{0,1},{1,0},{2,3},{3,2},{4,5},{5,4},{6,7},{7,6},{8,9},{9,8},{10,11... | collective-permute-start | bytes 1769480 | tf_op jit(solution)/shard_map/ppermute | solution.py:50
  57.8 2.3 %collective-permute-start.23 = (bf16[384,768]{1,0:T(8,128)(2,1)S(1)}, bf16[384,768]{1,0:T(8,128)(2,1)S(1)}, u32[]{:S(2)}, u32[]{:S(2)}) collective-permute-start(bf16[384,768]{1,0:T(8,128)(2,1)S(1)} %get-tuple-element.125), channel_id=1, source_target_pairs={{0,1},{1,0},{2,3},{3,2},{4,5},{5,4},{6,7},{7,6},{8,9},{9,8},{10,11... | collective-permute-start | bytes 1769480 | tf_op jit(solution)/shard_map/ppermute | solution.py:50
  58.5 11.4 %collective-permute-start.16 = (bf16[2,96,768]{2,1,0:T(8,128)(2,1)S(1)}, bf16[2,96,768]{2,1,0:T(8,128)(2,1)S(1)}, u32[]{:S(2)}, u32[]{:S(2)}) collective-permute-start(bf16[2,96,768]{2,1,0:T(8,128)(2,1)S(1)} %fusion.36), channel_id=1, source_target_pairs={{0,2},{1,3},{2,0},{3,1},{4,6},{5,7},{6,4},{7,5},{8,10},{9,11},{10,... | collective-permute-start | bytes 884744 | tf_op jit(solution)/shard_map/ppermute | solution.py:46
  60.3 15.9 %collective-permute-start.24 = (bf16[2,96,768]{2,1,0:T(8,128)(2,1)S(1)}, bf16[2,96,768]{2,1,0:T(8,128)(2,1)S(1)}, u32[]{:S(2)}, u32[]{:S(2)}) collective-permute-start(bf16[2,96,768]{2,1,0:T(8,128)(2,1)S(1)} %fusion.37), channel_id=1, source_target_pairs={{0,2},{1,3},{2,0},{3,1},{4,6},{5,7},{6,4},{7,5},{8,10},{9,11},{10,... | collective-permute-start | bytes 884744 | tf_op jit(solution)/shard_map/ppermute | solution.py:46
  70.4 12.1 %collective-permute-start.17 = (bf16[2,96,768]{2,1,0:T(8,128)(2,1)S(1)}, bf16[2,96,768]{2,1,0:T(8,128)(2,1)S(1)}, u32[]{:S(2)}, u32[]{:S(2)}) collective-permute-start(bf16[2,96,768]{2,1,0:T(8,128)(2,1)S(1)} %get-tuple-element.70), channel_id=1, source_target_pairs={{0,2},{1,3},{2,0},{3,1},{4,6},{5,7},{6,4},{7,5},{8,10},{9,11},{10,... | collective-permute-start | bytes 884744 | tf_op jit(solution)/shard_map/ppermute | solution.py:46
  76.7 11.7 %collective-permute-start.25 = (bf16[2,96,768]{2,1,0:T(8,128)(2,1)S(1)}, bf16[2,96,768]{2,1,0:T(8,128)(2,1)S(1)}, u32[]{:S(2)}, u32[]{:S(2)}) collective-permute-start(bf16[2,96,768]{2,1,0:T(8,128)(2,1)S(1)} %get-tuple-element.72), channel_id=1, source_target_pairs={{0,2},{1,3},{2,0},{3,1},{4,6},{5,7},{6,4},{7,5},{8,10},{9,11},{10,... | collective-permute-start | bytes 884744 | tf_op jit(solution)/shard_map/ppermute | solution.py:46
  82.7 2.1 %collective-permute-start.18 = (bf16[384,768]{1,0:T(8,128)(2,1)S(1)}, bf16[384,768]{1,0:T(8,128)(2,1)S(1)}, u32[]{:S(2)}, u32[]{:S(2)}) collective-permute-start(bf16[384,768]{1,0:T(8,128)(2,1)S(1)} %pad_maximum_fusion.10), channel_id=1, source_target_pairs={{0,1},{1,0},{2,3},{3,2},{4,5},{5,4},{6,7},{7,6},{8,9},{9,8},{10,11... | collective-permute-start | bytes 1769480 | tf_op jit(solution)/shard_map/ppermute | solution.py:50
  88.6 2.3 %collective-permute-start.26 = (bf16[384,768]{1,0:T(8,128)(2,1)S(1)}, bf16[384,768]{1,0:T(8,128)(2,1)S(1)}, u32[]{:S(2)}, u32[]{:S(2)}) collective-permute-start(bf16[384,768]{1,0:T(8,128)(2,1)S(1)} %pad_maximum_fusion.11), channel_id=1, source_target_pairs={{0,1},{1,0},{2,3},{3,2},{4,5},{5,4},{6,7},{7,6},{8,9},{9,8},{10,11... | collective-permute-start | bytes 1769480 | tf_op jit(solution)/shard_map/ppermute | solution.py:50
  88.7 10.0 %collective-permute-start.19 = (bf16[96,1536]{1,0:T(8,128)(2,1)S(1)}, bf16[96,1536]{1,0:T(8,128)(2,1)S(1)}, u32[]{:S(2)}, u32[]{:S(2)}) collective-permute-start(bf16[96,1536]{1,0:T(8,128)(2,1)S(1)} %get-tuple-element.94), channel_id=1, source_target_pairs={{12,0},{0,4},{4,8},{8,12},{28,16},{16,20},{20,24},{24,28},{13,1},{... | collective-permute-start | bytes 884744 | tf_op jit(solution)/shard_map/ppermute | solution.py:32
  89.9 9.1 %collective-permute-start.20 = (bf16[96,1536]{1,0:T(8,128)(2,1)S(1)}, bf16[96,1536]{1,0:T(8,128)(2,1)S(1)}, u32[]{:S(2)}, u32[]{:S(2)}) collective-permute-start(bf16[96,1536]{1,0:T(8,128)(2,1)S(1)} %get-tuple-element.93), channel_id=1, source_target_pairs={{4,0},{8,4},{12,8},{0,12},{20,16},{24,20},{28,24},{16,28},{5,1},{9... | collective-permute-start | bytes 884744 | tf_op jit(solution)/shard_map/ppermute | solution.py:32
  91.7 10.1 %collective-permute-start.27 = (bf16[384,384]{1,0:T(8,128)(2,1)S(1)}, bf16[384,384]{1,0:T(8,128)(2,1)S(1)}, u32[]{:S(2)}, u32[]{:S(2)}) collective-permute-start(bf16[384,384]{1,0:T(8,128)(2,1)S(1)} %convolution_convert_fusion.2), channel_id=1, source_target_pairs={{96,0},{0,32},{32,64},{64,96},{97,1},{1,33},{33,65},{65,97},{98,2}... | collective-permute-start | bytes 884744 | tf_op jit(solution)/shard_map/ppermute | solution.py:24
  92.7 9.0 %collective-permute-start.28 = (bf16[384,384]{1,0:T(8,128)(2,1)S(1)}, bf16[384,384]{1,0:T(8,128)(2,1)S(1)}, u32[]{:S(2)}, u32[]{:S(2)}) collective-permute-start(bf16[384,384]{1,0:T(8,128)(2,1)S(1)} %convolution_convert_fusion.1), channel_id=1, source_target_pairs={{32,0},{64,32},{96,64},{0,96},{33,1},{65,33},{97,65},{1,97},{34,2}... | collective-permute-start | bytes 884744 | tf_op jit(solution)/shard_map/ppermute | solution.py:24
  95.5 11.3 %collective-permute-start.29 = (bf16[192,768]{1,0:T(8,128)(2,1)S(1)}, bf16[192,768]{1,0:T(8,128)(2,1)S(1)}, u32[]{:S(2)}, u32[]{:S(2)}) collective-permute-start(bf16[192,768]{1,0:T(8,128)(2,1)S(1)} %get-tuple-element.47), channel_id=1, source_target_pairs={{0,0},{10,1},{18,2},{24,3},{1,4},{11,5},{19,6},{25,7},{5,8},{15,9}... | collective-permute-start | bytes 884744 | tf_op jit(solution)/shard_map/ppermute | solution.py:176
  107.7 15.6 %collective-permute-start.30 = (bf16[192,1536]{1,0:T(8,128)(2,1)S(1)}, bf16[192,1536]{1,0:T(8,128)(2,1)S(1)}, u32[]{:S(2)}, u32[]{:S(2)}) collective-permute-start(bf16[192,1536]{1,0:T(8,128)(2,1)S(1)} %fusion.1), channel_id=1, source_target_pairs={{12,0},{0,4},{4,8},{8,12},{28,16},{16,20},{20,24},{24,28},{13,1},{... | collective-permute-start | bytes 1769480 | tf_op jit(solution)/shard_map/ppermute | solution.py:32
  110.5 14.8 %collective-permute-start.31 = (bf16[192,1536]{1,0:T(8,128)(2,1)S(1)}, bf16[192,1536]{1,0:T(8,128)(2,1)S(1)}, u32[]{:S(2)}, u32[]{:S(2)}) collective-permute-start(bf16[192,1536]{1,0:T(8,128)(2,1)S(1)} %fusion.2), channel_id=1, source_target_pairs={{4,0},{8,4},{12,8},{0,12},{20,16},{24,20},{28,24},{16,28},{5,1},{9... | collective-permute-start | bytes 1769480 | tf_op jit(solution)/shard_map/ppermute | solution.py:32
  111.6 15.9 %collective-permute-start.32 = (bf16[768,384]{1,0:T(8,128)(2,1)S(1)}, bf16[768,384]{1,0:T(8,128)(2,1)S(1)}, u32[]{:S(2)}, u32[]{:S(2)}) collective-permute-start(bf16[768,384]{1,0:T(8,128)(2,1)S(1)} %add_convert_fusion.1), channel_id=1, source_target_pairs={{96,0},{0,32},{32,64},{64,96},{97,1},{1,33},{33,65},{65,97},{98,2}... | collective-permute-start | bytes 1769480 | tf_op jit(solution)/shard_map/ppermute | solution.py:24
  112.5 15.1 %collective-permute-start.33 = (bf16[768,384]{1,0:T(8,128)(2,1)S(1)}, bf16[768,384]{1,0:T(8,128)(2,1)S(1)}, u32[]{:S(2)}, u32[]{:S(2)}) collective-permute-start(bf16[768,384]{1,0:T(8,128)(2,1)S(1)} %add_convert_fusion), channel_id=1, source_target_pairs={{32,0},{64,32},{96,64},{0,96},{33,1},{65,33},{97,65},{1,97},{34,2}... | collective-permute-start | bytes 1769480 | tf_op jit(solution)/shard_map/ppermute | solution.py:24
  116.6 12.2 %collective-permute-start.34 = (bf16[192,768]{1,0:T(8,128)(2,1)S(1)}, bf16[192,768]{1,0:T(8,128)(2,1)S(1)}, u32[]{:S(2)}, u32[]{:S(2)}) collective-permute-start(bf16[192,768]{1,0:T(8,128)(2,1)S(1)} %get-tuple-element.59), channel_id=1, source_target_pairs={{5,0},{15,1},{23,2},{29,3},{4,4},{14,5},{22,6},{28,7},{0,8},{10,9}... | collective-permute-start | bytes 884744 | tf_op jit(solution)/shard_map/ppermute | solution.py:176
  128.9 11.7 %collective-permute-start.40 = (bf16[192,384]{1,0:T(8,128)(2,1)S(1)}, bf16[192,384]{1,0:T(8,128)(2,1)S(1)}, u32[]{:S(2)}, u32[]{:S(2)}) collective-permute-start(bf16[192,384]{1,0:T(8,128)(2,1)S(1)} %get-tuple-element.85), channel_id=1, source_target_pairs={{4,0},{8,4},{12,8},{0,12},{20,16},{24,20},{28,24},{16,28},{5,1},{9... | collective-permute-start | bytes 442376 | tf_op jit(solution)/shard_map/ppermute | solution.py:32
  132.0 9.6 %collective-permute-start.39 = (bf16[192,384]{1,0:T(8,128)(2,1)S(1)}, bf16[192,384]{1,0:T(8,128)(2,1)S(1)}, u32[]{:S(2)}, u32[]{:S(2)}) collective-permute-start(bf16[192,384]{1,0:T(8,128)(2,1)S(1)} %get-tuple-element.86), channel_id=1, source_target_pairs={{8,0},{12,4},{0,8},{4,12},{24,16},{28,20},{16,24},{20,28},{9,1},{1... | collective-permute-start | bytes 442376 | tf_op jit(solution)/shard_map/ppermute | solution.py:32
  134.3 7.3 %collective-permute-start.38 = (bf16[192,384]{1,0:T(8,128)(2,1)S(1)}, bf16[192,384]{1,0:T(8,128)(2,1)S(1)}, u32[]{:S(2)}, u32[]{:S(2)}) collective-permute-start(bf16[192,384]{1,0:T(8,128)(2,1)S(1)} %get-tuple-element.84), channel_id=1, source_target_pairs={{12,0},{0,4},{4,8},{8,12},{28,16},{16,20},{20,24},{24,28},{13,1},{... | collective-permute-start | bytes 442376 | tf_op jit(solution)/shard_map/ppermute | solution.py:32
  136.2 5.8 %collective-permute-start.37 = (bf16[192,384]{1,0:T(8,128)(2,1)S(1)}, bf16[192,384]{1,0:T(8,128)(2,1)S(1)}, u32[]{:S(2)}, u32[]{:S(2)}) collective-permute-start(bf16[192,384]{1,0:T(8,128)(2,1)S(1)} %get-tuple-element.82), channel_id=1, source_target_pairs={{32,0},{64,32},{96,64},{0,96},{33,1},{65,33},{97,65},{1,97},{34,2}... | collective-permute-start | bytes 442376 | tf_op jit(solution)/shard_map/ppermute | solution.py:24
  137.6 8.2 %collective-permute-start.36 = (bf16[192,384]{1,0:T(8,128)(2,1)S(1)}, bf16[192,384]{1,0:T(8,128)(2,1)S(1)}, u32[]{:S(2)}, u32[]{:S(2)}) collective-permute-start(bf16[192,384]{1,0:T(8,128)(2,1)S(1)} %get-tuple-element.83), channel_id=1, source_target_pairs={{64,0},{96,32},{0,64},{32,96},{65,1},{97,33},{1,65},{33,97},{66,2}... | collective-permute-start | bytes 442376 | tf_op jit(solution)/shard_map/ppermute | solution.py:24
  140.5 1.4 copy-start
  140.6 6.7 %collective-permute-start.35 = (bf16[192,384]{1,0:T(8,128)(2,1)S(1)}, bf16[192,384]{1,0:T(8,128)(2,1)S(1)}, u32[]{:S(2)}, u32[]{:S(2)}) collective-permute-start(bf16[192,384]{1,0:T(8,128)(2,1)S(1)} %get-tuple-element.81), channel_id=1, source_target_pairs={{96,0},{0,32},{32,64},{64,96},{97,1},{1,33},{33,65},{65,97},{98,2}... | collective-permute-start | bytes 442376 | tf_op jit(solution)/shard_map/ppermute | solution.py:24
  147.4 5.2 %collective-permute-start.41 = (bf16[192,384]{1,0:T(8,128)(2,1)S(1)}, bf16[192,384]{1,0:T(8,128)(2,1)S(1)}, u32[]{:S(2)}, u32[]{:S(2)}) collective-permute-start(bf16[192,384]{1,0:T(8,128)(2,1)S(1)} %pad_maximum_fusion.19), channel_id=1, source_target_pairs={{0,16},{4,20},{8,24},{12,28},{16,0},{20,4},{24,8},{28,12},{1,17},{... | collective-permute-start | bytes 442376 | tf_op jit(solution)/shard_map/ppermute | solution.py:42

commit v6 on v5

--- a/solution.py
+++ b/solution.py
@@ -177,11 +177,13 @@
 
     back0 = give_back(0, d2, c2_first, c2_second)
     up_a, down_a, up_b, down_b = together(up_a, down_a, up_b, down_b)
-    d1 = (dot(g1, turned, (1, 1)) + before(up_a, half)).astype(bf16)
-    d3 = (dot(g3, turned, (1, 1)) + after(down_a, half)).astype(bf16)
+    p1, p3 = together(dot(g1, turned, (1, 1)), dot(g3, turned, (1, 1)))
+    d1 = (p1 + before(up_a, half)).astype(bf16)
+    d3 = (p3 + after(down_a, half)).astype(bf16)
     up_b, down_b, back0 = together(up_b, down_b, back0)
-    c1 = (dot(gb, w[1], (1, 1)) + before(up_b, 2 * n)).astype(bf16)
-    c3 = (dot(gb, w[3], (1, 1)) + after(down_b, 2 * n)).astype(bf16)
+    q1, q3 = together(dot(gb, w[1], (1, 1)), dot(gb, w[3], (1, 1)))
+    c1 = (q1 + before(up_b, 2 * n)).astype(bf16)
+    c3 = (q3 + after(down_b, 2 * n)).astype(bf16)
     added = (d1, d3, c1, c3)
     d1, d3, c1, c3 = to_z(d1, 1), to_z(d3, 3), to_x(c1, 1), to_x(c3, 3)
     d1, d3, c1, c3 = together(d1, d3, c1, c3)

time: 156 us -> 154 us (0.987)
  starting transfers between devices: 61.2 us -> 59.3 us
    ppermute x14, waiting for transfers between devices: 15.7 us -> 11.6 us  [from_x(): return lax.ppermute(v, 'ia', [((i + r) % N_RING, i) for i in range(N_RING)])]
    ppermute x14, waiting for transfers between devices: 7.55 us -> 11.2 us  [from_z(): lax.ppermute(v, 'ja', [(y * 4 + (z + r) % N_RING, y * 4 + z) for y in ran...]
    ppermute x4, waiting for transfers between devices: 19.3 us -> 16.8 us  [swap_y_hi(): return lax.ppermute(v, 'ka', [(k, k ^ 2) for k in range(4)])]
    ppermute x4, waiting for transfers between devices: 2.33 us -> 4.13 us  [swap_core(): return lax.ppermute(v, 'ka', [(k, k ^ 1) for k in range(4)])]
  transfers between devices with their start and end apart: 42 -> 42, of which waited for: 23 -> 21; matrix products, arithmetic and copies ran while one was open for 14% -> 15% of each run, Pallas kernels for 0% -> 0%
where the time goes in v6:
time: 154 us; the launch traced here: 153 us
  waiting for transfers between devices  66.3 us (43%)
  starting transfers between devices  59.3 us (39%)
  matrix products  17.6 us (11%)
  other arithmetic  5.33 us (3%)
  local copies, waits for them, and re-layouts  2.67 us (2%)
    ppermute x14, starting transfers between devices, from_z(): lax.ppermute(v, 'ja', [(y * 4 + (z + r) % N_RING, y * 4 + z) for y in ran...  21.1 us
    ppermute x14, starting transfers between devices, from_x(): return lax.ppermute(v, 'ia', [((i + r) % N_RING, i) for i in range(N_RING)])  18.9 us
    dot_general x23, matrix products, dot(): lax.dot_general(a, b, (((dims[0],), (dims[1],)), ((), ())), preferred_ele...  17.6 us
    ppermute x4, waiting for transfers between devices, swap_y_hi(): return lax.ppermute(v, 'ka', [(k, k ^ 2) for k in range(4)])  16.8 us
    ppermute x14, waiting for transfers between devices, from_x(): return lax.ppermute(v, 'ia', [((i + r) % N_RING, i) for i in range(N_RING)])  11.6 us
    ppermute x14, waiting for transfers between devices, from_z(): lax.ppermute(v, 'ja', [(y * 4 + (z + r) % N_RING, y * 4 + z) for y in ran...  11.2 us
    ppermute x1, waiting for transfers between devices, on_device(): sent0 = lax.ppermute(after_done(piece0, a0, b0), BOTH, exchange_pairs(0))  9.08 us
    ppermute x2, waiting for transfers between devices, swap_y_lo(): return lax.ppermute(v, 'ja', [(j, j ^ 4) for j in range(8)])  7.89 us
  transfers between devices with their start and end apart: 42, of which 21 were waited for; matrix products, arithmetic and copies ran while one was open for 15% of the time, Pallas kernels for 0%

profile of v6, /device:TPU:40, one launch (start us, length us, event | category | flops | bytes accessed | tf_op | source)
XLA Modules:
  0.0 152.7 jit_solution(1844786319961602132)
XLA Ops:
  2.1 4.4 %collective-permute-done = bf16[192,384]{1,0:T(8,128)(2,1)S(1)} collective-permute-done((bf16[192,384]{1,0:T(8,128)(2,1)}, bf16[192,384]{1,0:T(8,128)(2,1)S(1)}, u32[]{:S(2)}, u32[]{:S(2)}) %collective-permute-start) | collective-permute-done | bytes 147488 | tf_op jit(solution)/shard_map/ppermute | solution.py:42
  6.6 1.6 %collective-permute-start.3 = (bf16[192,384]{1,0:T(8,128)(2,1)S(1)}, bf16[192,384]{1,0:T(8,128)(2,1)S(1)}, u32[]{:S(2)}, u32[]{:S(2)}) collective-permute-start(bf16[192,384]{1,0:T(8,128)(2,1)S(1)} %pad_maximum_fusion.17), channel_id=1, source_target_pairs={{96,0},{0,32},{32,64},{64,96},{97,1},{1,33},{33,65},{65,97},{98,2}... | collective-permute-start | bytes 442376 | tf_op jit(solution)/shard_map/ppermute | solution.py:24
  8.1 2.7 %collective-permute-start.2 = (bf16[192,384]{1,0:T(8,128)(2,1)S(1)}, bf16[192,384]{1,0:T(8,128)(2,1)S(1)}, u32[]{:S(2)}, u32[]{:S(2)}) collective-permute-start(bf16[192,384]{1,0:T(8,128)(2,1)S(1)} %pad_maximum_fusion.17), channel_id=1, source_target_pairs={{64,0},{96,32},{0,64},{32,96},{65,1},{97,33},{1,65},{33,97},{66,2}... | collective-permute-start | bytes 442376 | tf_op jit(solution)/shard_map/ppermute | solution.py:24
  10.9 1.4 collective-permute-start.1
  12.5 3.1 %collective-permute-start.6 = (bf16[192,384]{1,0:T(8,128)(2,1)S(1)}, bf16[192,384]{1,0:T(8,128)(2,1)S(1)}, u32[]{:S(2)}, u32[]{:S(2)}) collective-permute-start(bf16[192,384]{1,0:T(8,128)(2,1)S(1)} %pad_maximum_fusion.18), channel_id=1, source_target_pairs={{8,0},{12,4},{0,8},{4,12},{24,16},{28,20},{16,24},{20,28},{9,1},{1... | collective-permute-start | bytes 442376 | tf_op jit(solution)/shard_map/ppermute | solution.py:32
  15.5 1.0 collective-permute-start.7
  16.6 1.0 collective-permute-start.8
  17.7 1.1 collective-permute-start.4
  18.8 1.0 collective-permute-start.5
  20.3 2.7 %collective-permute-done.7 = bf16[192,384]{1,0:T(8,128)(2,1)S(1)} collective-permute-done((bf16[192,384]{1,0:T(8,128)(2,1)S(1)}, bf16[192,384]{1,0:T(8,128)(2,1)S(1)}, u32[]{:S(2)}, u32[]{:S(2)}) %collective-permute-start.7) | collective-permute-done | bytes 147488 | tf_op jit(solution)/shard_map/ppermute | solution.py:32
  23.7 2.0 %collective-permute-start.10 = (bf16[768,384]{1,0:T(8,128)(2,1)S(1)}, bf16[768,384]{1,0:T(8,128)(2,1)S(1)}, u32[]{:S(2)}, u32[]{:S(2)}) collective-permute-start(bf16[768,384]{1,0:T(8,128)(2,1)S(1)} %constant_dynamic-update-slice_fusion), channel_id=1, source_target_pairs={{96,0},{0,32},{32,64},{64,96},{97,1},{1,33},{33,65},{65,97},{98,2}... | collective-permute-start | bytes 1769480 | tf_op jit(solution)/shard_map/ppermute | solution.py:24
  25.7 1.9 %collective-permute-start.11 = (bf16[192,768]{1,0:T(8,128)(2,1)S(1)}, bf16[192,768]{1,0:T(8,128)(2,1)S(1)}, u32[]{:S(2)}, u32[]{:S(2)}) collective-permute-start(bf16[192,768]{1,0:T(8,128)(2,1)S(1)} %get-tuple-element.38), channel_id=1, source_target_pairs={{0,0},{1,10},{2,18},{3,24},{4,1},{5,11},{6,19},{7,25},{8,5},{9,15}... | collective-permute-start | bytes 884744 | tf_op jit(solution)/shard_map/ppermute | solution.py:111
  29.4 9.1 %collective-permute-done.11 = bf16[192,768]{1,0:T(8,128)(2,1)S(1)} collective-permute-done((bf16[192,768]{1,0:T(8,128)(2,1)S(1)}, bf16[192,768]{1,0:T(8,128)(2,1)S(1)}, u32[]{:S(2)}, u32[]{:S(2)}) %collective-permute-start.11) | collective-permute-done | bytes 294944 | tf_op jit(solution)/shard_map/ppermute | solution.py:111
  38.5 1.6 %collective-permute-done.4 = bf16[192,1536]{1,0:T(8,128)(2,1)S(1)} collective-permute-done((bf16[192,1536]{1,0:T(8,128)(2,1)S(1)}, bf16[192,1536]{1,0:T(8,128)(2,1)S(1)}, u32[]{:S(2)}, u32[]{:S(2)}) %collective-permute-start.4) | collective-permute-done | bytes 589856 | tf_op jit(solution)/shard_map/ppermute | solution.py:32
  41.6 2.0 %collective-permute-start.13 = (bf16[96,1536]{1,0:T(8,128)(2,1)S(1)}, bf16[96,1536]{1,0:T(8,128)(2,1)S(1)}, u32[]{:S(2)}, u32[]{:S(2)}) collective-permute-start(bf16[96,1536]{1,0:T(8,128)(2,1)S(1)} %slice.181), channel_id=1, source_target_pairs={{12,0},{0,4},{4,8},{8,12},{28,16},{16,20},{20,24},{24,28},{13,1},{... | collective-permute-start | bytes 884744 | tf_op jit(solution)/shard_map/ppermute | solution.py:32
  43.7 3.5 %collective-permute-start.15 = (bf16[192,768]{1,0:T(8,128)(2,1)S(1)}, bf16[192,768]{1,0:T(8,128)(2,1)S(1)}, u32[]{:S(2)}, u32[]{:S(2)}) collective-permute-start(bf16[192,768]{1,0:T(8,128)(2,1)S(1)} %get-tuple-element.43), channel_id=1, source_target_pairs={{0,5},{1,15},{2,23},{3,29},{4,4},{5,14},{6,22},{7,28},{8,0},{9,10}... | collective-permute-start | bytes 884744 | tf_op jit(solution)/shard_map/ppermute | solution.py:119
  47.2 1.2 collective-permute-start.21
  48.4 1.0 collective-permute-start.22
  51.7 4.3 %collective-permute-done.21 = bf16[384,384]{1,0:T(8,128)(2,1)S(1)} collective-permute-done((bf16[384,384]{1,0:T(8,128)(2,1)S(1)}, bf16[384,384]{1,0:T(8,128)(2,1)S(1)}, u32[]{:S(2)}, u32[]{:S(2)}) %collective-permute-start.21) | collective-permute-done | bytes 294944 | tf_op jit(solution)/shard_map/ppermute | solution.py:24
  58.5 1.1 collective-permute-start.16
  60.3 2.1 %collective-permute-start.24 = (bf16[2,96,768]{2,1,0:T(8,128)(2,1)S(1)}, bf16[2,96,768]{2,1,0:T(8,128)(2,1)S(1)}, u32[]{:S(2)}, u32[]{:S(2)}) collective-permute-start(bf16[2,96,768]{2,1,0:T(8,128)(2,1)S(1)} %fusion.35), channel_id=1, source_target_pairs={{0,2},{1,3},{2,0},{3,1},{4,6},{5,7},{6,4},{7,5},{8,10},{9,11},{10,... | collective-permute-start | bytes 884744 | tf_op jit(solution)/shard_map/ppermute | solution.py:46
  62.6 7.3 %collective-permute-done.16 = bf16[2,96,768]{2,1,0:T(8,128)(2,1)S(1)} collective-permute-done((bf16[2,96,768]{2,1,0:T(8,128)(2,1)S(1)}, bf16[2,96,768]{2,1,0:T(8,128)(2,1)S(1)}, u32[]{:S(2)}, u32[]{:S(2)}) %collective-permute-start.16) | collective-permute-done | bytes 294944 | tf_op jit(solution)/shard_map/ppermute | solution.py:46
  70.4 1.1 collective-permute-start.17
  71.5 4.7 %collective-permute-done.24 = bf16[2,96,768]{2,1,0:T(8,128)(2,1)S(1)} collective-permute-done((bf16[2,96,768]{2,1,0:T(8,128)(2,1)S(1)}, bf16[2,96,768]{2,1,0:T(8,128)(2,1)S(1)}, u32[]{:S(2)}, u32[]{:S(2)}) %collective-permute-start.24) | collective-permute-done | bytes 294944 | tf_op jit(solution)/shard_map/ppermute | solution.py:46
  76.7 1.1 collective-permute-start.25
  77.8 4.8 %collective-permute-done.17 = bf16[2,96,768]{2,1,0:T(8,128)(2,1)S(1)} collective-permute-done((bf16[2,96,768]{2,1,0:T(8,128)(2,1)S(1)}, bf16[2,96,768]{2,1,0:T(8,128)(2,1)S(1)}, u32[]{:S(2)}, u32[]{:S(2)}) %collective-permute-start.17) | collective-permute-done | bytes 294944 | tf_op jit(solution)/shard_map/ppermute | solution.py:46
  82.9 1.8 %collective-permute-done.18 = bf16[384,768]{1,0:T(8,128)(2,1)S(1)} collective-permute-done((bf16[384,768]{1,0:T(8,128)(2,1)S(1)}, bf16[384,768]{1,0:T(8,128)(2,1)S(1)}, u32[]{:S(2)}, u32[]{:S(2)}) %collective-permute-start.18) | collective-permute-done | bytes 589856 | tf_op jit(solution)/shard_map/ppermute | solution.py:50
  86.0 1.1 collective-permute-start.19
  87.1 1.0 collective-permute-start.20
  90.3 1.8 %collective-permute-done.26 = bf16[384,768]{1,0:T(8,128)(2,1)S(1)} collective-permute-done((bf16[384,768]{1,0:T(8,128)(2,1)S(1)}, bf16[384,768]{1,0:T(8,128)(2,1)S(1)}, u32[]{:S(2)}, u32[]{:S(2)}) %collective-permute-start.26) | collective-permute-done | bytes 589856 | tf_op jit(solution)/shard_map/ppermute | solution.py:50
  94.0 2.8 %collective-permute-start.28 = (bf16[384,384]{1,0:T(8,128)(2,1)S(1)}, bf16[384,384]{1,0:T(8,128)(2,1)S(1)}, u32[]{:S(2)}, u32[]{:S(2)}) collective-permute-start(bf16[384,384]{1,0:T(8,128)(2,1)S(1)} %convolution_convert_fusion.1), channel_id=1, source_target_pairs={{32,0},{64,32},{96,64},{0,96},{33,1},{65,33},{97,65},{1,97},{34,2}... | collective-permute-start | bytes 884744 | tf_op jit(solution)/shard_map/ppermute | solution.py:24
  96.7 3.5 %collective-permute-start.29 = (bf16[192,768]{1,0:T(8,128)(2,1)S(1)}, bf16[192,768]{1,0:T(8,128)(2,1)S(1)}, u32[]{:S(2)}, u32[]{:S(2)}) collective-permute-start(bf16[192,768]{1,0:T(8,128)(2,1)S(1)} %get-tuple-element.51), channel_id=1, source_target_pairs={{0,0},{10,1},{18,2},{24,3},{1,4},{11,5},{19,6},{25,7},{5,8},{15,9}... | collective-permute-start | bytes 884744 | tf_op jit(solution)/shard_map/ppermute | solution.py:176
  102.0 1.2 collective-permute-done.27
  103.2 5.6 %collective-permute-done.29 = bf16[192,768]{1,0:T(8,128)(2,1)S(1)} collective-permute-done((bf16[192,768]{1,0:T(8,128)(2,1)S(1)}, bf16[192,768]{1,0:T(8,128)(2,1)S(1)}, u32[]{:S(2)}, u32[]{:S(2)}) %collective-permute-start.29) | collective-permute-done | bytes 294944 | tf_op jit(solution)/shard_map/ppermute | solution.py:176
  108.9 1.0 collective-permute-start.30
  110.0 1.1 collective-permute-start.31
  111.5 3.3 %collective-permute-start.33 = (bf16[768,384]{1,0:T(8,128)(2,1)S(1)}, bf16[768,384]{1,0:T(8,128)(2,1)S(1)}, u32[]{:S(2)}, u32[]{:S(2)}) collective-permute-start(bf16[768,384]{1,0:T(8,128)(2,1)S(1)} %add_convert_fusion), channel_id=1, source_target_pairs={{32,0},{64,32},{96,64},{0,96},{33,1},{65,33},{97,65},{1,97},{34,2}... | collective-permute-start | bytes 1769480 | tf_op jit(solution)/shard_map/ppermute | solution.py:24
  115.6 3.3 %collective-permute-start.34 = (bf16[192,768]{1,0:T(8,128)(2,1)S(1)}, bf16[192,768]{1,0:T(8,128)(2,1)S(1)}, u32[]{:S(2)}, u32[]{:S(2)}) collective-permute-start(bf16[192,768]{1,0:T(8,128)(2,1)S(1)} %get-tuple-element.67), channel_id=1, source_target_pairs={{5,0},{15,1},{23,2},{29,3},{4,4},{14,5},{22,6},{28,7},{0,8},{10,9}... | collective-permute-start | bytes 884744 | tf_op jit(solution)/shard_map/ppermute | solution.py:176
  118.9 2.1 %fusion.62 = f32[1536,768]{1,0:T(8,128)S(1)} fusion(bf16[768,1536]{1,0:T(8,128)(2,1)S(1)} %constant_dynamic-update-slice_fusion.7, bf16[768,768]{1,0:T(8,128)(2,1)S(1)} %pad_maximum_fusion.3), kind=kOutput, calls=%fused_computation.160 | convolution fusion | flops 1811939328 | bytes 8257536 | tf_op jit(solution)/shard_map/dot_general | solution.py:67
  120.9 3.1 %collective-permute-done.30 = bf16[192,1536]{1,0:T(8,128)(2,1)S(1)} collective-permute-done((bf16[192,1536]{1,0:T(8,128)(2,1)S(1)}, bf16[192,1536]{1,0:T(8,128)(2,1)S(1)}, u32[]{:S(2)}, u32[]{:S(2)}) %collective-permute-start.30) | collective-permute-done | bytes 589856 | tf_op jit(solution)/shard_map/ppermute | solution.py:32
  124.0 2.8 %collective-permute-done.31 = bf16[192,1536]{1,0:T(8,128)(2,1)S(1)} collective-permute-done((bf16[192,1536]{1,0:T(8,128)(2,1)S(1)}, bf16[192,1536]{1,0:T(8,128)(2,1)S(1)}, u32[]{:S(2)}, u32[]{:S(2)}) %collective-permute-start.31) | collective-permute-done | bytes 589856 | tf_op jit(solution)/shard_map/ppermute | solution.py:32
  128.1 2.9 %collective-permute-start.40 = (bf16[192,384]{1,0:T(8,128)(2,1)S(1)}, bf16[192,384]{1,0:T(8,128)(2,1)S(1)}, u32[]{:S(2)}, u32[]{:S(2)}) collective-permute-start(bf16[192,384]{1,0:T(8,128)(2,1)S(1)} %get-tuple-element.93), channel_id=1, source_target_pairs={{4,0},{8,4},{12,8},{0,12},{20,16},{24,20},{28,24},{16,28},{5,1},{9... | collective-permute-start | bytes 442376 | tf_op jit(solution)/shard_map/ppermute | solution.py:32
  131.0 2.0 %collective-permute-start.39 = (bf16[192,384]{1,0:T(8,128)(2,1)S(1)}, bf16[192,384]{1,0:T(8,128)(2,1)S(1)}, u32[]{:S(2)}, u32[]{:S(2)}) collective-permute-start(bf16[192,384]{1,0:T(8,128)(2,1)S(1)} %get-tuple-element.94), channel_id=1, source_target_pairs={{8,0},{12,4},{0,8},{4,12},{24,16},{28,20},{16,24},{20,28},{9,1},{1... | collective-permute-start | bytes 442376 | tf_op jit(solution)/shard_map/ppermute | solution.py:32
  133.1 2.5 %collective-permute-start.38 = (bf16[192,384]{1,0:T(8,128)(2,1)S(1)}, bf16[192,384]{1,0:T(8,128)(2,1)S(1)}, u32[]{:S(2)}, u32[]{:S(2)}) collective-permute-start(bf16[192,384]{1,0:T(8,128)(2,1)S(1)} %get-tuple-element.92), channel_id=1, source_target_pairs={{12,0},{0,4},{4,8},{8,12},{28,16},{16,20},{20,24},{24,28},{13,1},{... | collective-permute-start | bytes 442376 | tf_op jit(solution)/shard_map/ppermute | solution.py:32
  136.1 1.1 collective-permute-start.36
  141.5 1.3 collective-permute-done.36
  142.8 3.9 %collective-permute-done.35 = bf16[192,384]{1,0:T(8,128)(2,1)S(1)} collective-permute-done((bf16[192,384]{1,0:T(8,128)(2,1)S(1)}, bf16[192,384]{1,0:T(8,128)(2,1)S(1)}, u32[]{:S(2)}, u32[]{:S(2)}) %collective-permute-start.35) | collective-permute-done | bytes 147488 | tf_op jit(solution)/shard_map/ppermute | solution.py:24
  148.5 3.5 %collective-permute-done.41 = bf16[192,384]{1,0:T(8,128)(2,1)S(1)} collective-permute-done((bf16[192,384]{1,0:T(8,128)(2,1)S(1)}, bf16[192,384]{1,0:T(8,128)(2,1)S(1)}, u32[]{:S(2)}, u32[]{:S(2)}) %collective-permute-start.41) | collective-permute-done | bytes 147488 | tf_op jit(solution)/shard_map/ppermute | solution.py:42
  (134 shorter events, 29.9 us)
Async XLA Ops:
  0.6 11.7 %copy-start.2 = (bf16[192,1536]{1,0:T(8,128)(2,1)S(1)}, bf16[192,1536]{1,0:T(8,128)(2,1)}, u32[]{:S(2)}) copy-start(bf16[192,1536]{1,0:T(8,128)(2,1)} %param.5) | copy-start | bytes 1769476
  0.6 5.9 %collective-permute-start = (bf16[192,384]{1,0:T(8,128)(2,1)}, bf16[192,384]{1,0:T(8,128)(2,1)S(1)}, u32[]{:S(2)}, u32[]{:S(2)}) collective-permute-start(bf16[192,384]{1,0:T(8,128)(2,1)} %param.3), channel_id=1, source_target_pairs={{0,16},{4,20},{8,24},{12,28},{16,0},{20,4},{24,8},{28,12},{1,17},{... | collective-permute-start | bytes 442376 | tf_op jit(solution)/shard_map/ppermute | solution.py:42
  6.6 10.0 %collective-permute-start.3 = (bf16[192,384]{1,0:T(8,128)(2,1)S(1)}, bf16[192,384]{1,0:T(8,128)(2,1)S(1)}, u32[]{:S(2)}, u32[]{:S(2)}) collective-permute-start(bf16[192,384]{1,0:T(8,128)(2,1)S(1)} %pad_maximum_fusion.17), channel_id=1, source_target_pairs={{96,0},{0,32},{32,64},{64,96},{97,1},{1,33},{33,65},{65,97},{98,2}... | collective-permute-start | bytes 442376 | tf_op jit(solution)/shard_map/ppermute | solution.py:24
  8.1 9.4 %collective-permute-start.2 = (bf16[192,384]{1,0:T(8,128)(2,1)S(1)}, bf16[192,384]{1,0:T(8,128)(2,1)S(1)}, u32[]{:S(2)}, u32[]{:S(2)}) collective-permute-start(bf16[192,384]{1,0:T(8,128)(2,1)S(1)} %pad_maximum_fusion.17), channel_id=1, source_target_pairs={{64,0},{96,32},{0,64},{32,96},{65,1},{97,33},{1,65},{33,97},{66,2}... | collective-permute-start | bytes 442376 | tf_op jit(solution)/shard_map/ppermute | solution.py:24
  10.9 6.7 %collective-permute-start.1 = (bf16[192,384]{1,0:T(8,128)(2,1)S(1)}, bf16[192,384]{1,0:T(8,128)(2,1)S(1)}, u32[]{:S(2)}, u32[]{:S(2)}) collective-permute-start(bf16[192,384]{1,0:T(8,128)(2,1)S(1)} %pad_maximum_fusion.17), channel_id=1, source_target_pairs={{32,0},{64,32},{96,64},{0,96},{33,1},{65,33},{97,65},{1,97},{34,2}... | collective-permute-start | bytes 442376 | tf_op jit(solution)/shard_map/ppermute | solution.py:24
  12.5 15.1 %copy-start.1 = (bf16[1536,768]{1,0:T(8,128)(2,1)S(1)}, bf16[1536,768]{1,0:T(8,128)(2,1)}, u32[]{:S(2)}) copy-start(bf16[1536,768]{1,0:T(8,128)(2,1)} %param.4) | copy-start | bytes 7077892
  12.5 7.8 %collective-permute-start.6 = (bf16[192,384]{1,0:T(8,128)(2,1)S(1)}, bf16[192,384]{1,0:T(8,128)(2,1)S(1)}, u32[]{:S(2)}, u32[]{:S(2)}) collective-permute-start(bf16[192,384]{1,0:T(8,128)(2,1)S(1)} %pad_maximum_fusion.18), channel_id=1, source_target_pairs={{8,0},{12,4},{0,8},{4,12},{24,16},{28,20},{16,24},{20,28},{9,1},{1... | collective-permute-start | bytes 442376 | tf_op jit(solution)/shard_map/ppermute | solution.py:32
  15.5 7.5 %collective-permute-start.7 = (bf16[192,384]{1,0:T(8,128)(2,1)S(1)}, bf16[192,384]{1,0:T(8,128)(2,1)S(1)}, u32[]{:S(2)}, u32[]{:S(2)}) collective-permute-start(bf16[192,384]{1,0:T(8,128)(2,1)S(1)} %pad_maximum_fusion.18), channel_id=1, source_target_pairs={{4,0},{8,4},{12,8},{0,12},{20,16},{24,20},{28,24},{16,28},{5,1},{9... | collective-permute-start | bytes 442376 | tf_op jit(solution)/shard_map/ppermute | solution.py:32
  16.6 7.0 %collective-permute-start.8 = (bf16[192,384]{1,0:T(8,128)(2,1)S(1)}, bf16[192,384]{1,0:T(8,128)(2,1)S(1)}, u32[]{:S(2)}, u32[]{:S(2)}) collective-permute-start(bf16[192,384]{1,0:T(8,128)(2,1)S(1)} %pad_maximum_fusion.18), channel_id=1, source_target_pairs={{12,0},{0,4},{4,8},{8,12},{28,16},{16,20},{20,24},{24,28},{13,1},{... | collective-permute-start | bytes 442376 | tf_op jit(solution)/shard_map/ppermute | solution.py:32
  17.7 22.4 %collective-permute-start.4 = (bf16[192,1536]{1,0:T(8,128)(2,1)S(1)}, bf16[192,1536]{1,0:T(8,128)(2,1)S(1)}, u32[]{:S(2)}, u32[]{:S(2)}) collective-permute-start(bf16[192,1536]{1,0:T(8,128)(2,1)S(1)} %get-tuple-element.110), channel_id=1, source_target_pairs={{4,0},{8,4},{12,8},{0,12},{20,16},{24,20},{28,24},{16,28},{5,1},{9... | collective-permute-start | bytes 1769480 | tf_op jit(solution)/shard_map/ppermute | solution.py:32
  18.8 21.3 %collective-permute-start.5 = (bf16[192,1536]{1,0:T(8,128)(2,1)S(1)}, bf16[192,1536]{1,0:T(8,128)(2,1)S(1)}, u32[]{:S(2)}, u32[]{:S(2)}) collective-permute-start(bf16[192,1536]{1,0:T(8,128)(2,1)S(1)} %get-tuple-element.110), channel_id=1, source_target_pairs={{12,0},{0,4},{4,8},{8,12},{28,16},{16,20},{20,24},{24,28},{13,1},{... | collective-permute-start | bytes 1769480 | tf_op jit(solution)/shard_map/ppermute | solution.py:32
  23.6 16.5 %collective-permute-start.9 = (bf16[768,384]{1,0:T(8,128)(2,1)S(1)}, bf16[768,384]{1,0:T(8,128)(2,1)S(1)}, u32[]{:S(2)}, u32[]{:S(2)}) collective-permute-start(bf16[768,384]{1,0:T(8,128)(2,1)S(1)} %constant_dynamic-update-slice_fusion), channel_id=1, source_target_pairs={{32,0},{64,32},{96,64},{0,96},{33,1},{65,33},{97,65},{1,97},{34,2}... | collective-permute-start | bytes 1769480 | tf_op jit(solution)/shard_map/ppermute | solution.py:24
  23.7 16.4 %collective-permute-start.10 = (bf16[768,384]{1,0:T(8,128)(2,1)S(1)}, bf16[768,384]{1,0:T(8,128)(2,1)S(1)}, u32[]{:S(2)}, u32[]{:S(2)}) collective-permute-start(bf16[768,384]{1,0:T(8,128)(2,1)S(1)} %constant_dynamic-update-slice_fusion), channel_id=1, source_target_pairs={{96,0},{0,32},{32,64},{64,96},{97,1},{1,33},{33,65},{65,97},{98,2}... | collective-permute-start | bytes 1769480 | tf_op jit(solution)/shard_map/ppermute | solution.py:24
  25.7 12.8 %collective-permute-start.11 = (bf16[192,768]{1,0:T(8,128)(2,1)S(1)}, bf16[192,768]{1,0:T(8,128)(2,1)S(1)}, u32[]{:S(2)}, u32[]{:S(2)}) collective-permute-start(bf16[192,768]{1,0:T(8,128)(2,1)S(1)} %get-tuple-element.38), channel_id=1, source_target_pairs={{0,0},{1,10},{2,18},{3,24},{4,1},{5,11},{6,19},{7,25},{8,5},{9,15}... | collective-permute-start | bytes 884744 | tf_op jit(solution)/shard_map/ppermute | solution.py:111
  41.6 9.2 %collective-permute-start.13 = (bf16[96,1536]{1,0:T(8,128)(2,1)S(1)}, bf16[96,1536]{1,0:T(8,128)(2,1)S(1)}, u32[]{:S(2)}, u32[]{:S(2)}) collective-permute-start(bf16[96,1536]{1,0:T(8,128)(2,1)S(1)} %slice.181), channel_id=1, source_target_pairs={{12,0},{0,4},{4,8},{8,12},{28,16},{16,20},{20,24},{24,28},{13,1},{... | collective-permute-start | bytes 884744 | tf_op jit(solution)/shard_map/ppermute | solution.py:32
  43.6 7.3 %collective-permute-start.12 = (bf16[96,1536]{1,0:T(8,128)(2,1)S(1)}, bf16[96,1536]{1,0:T(8,128)(2,1)S(1)}, u32[]{:S(2)}, u32[]{:S(2)}) collective-permute-start(bf16[96,1536]{1,0:T(8,128)(2,1)S(1)} %slice.180), channel_id=1, source_target_pairs={{4,0},{8,4},{12,8},{0,12},{20,16},{24,20},{28,24},{16,28},{5,1},{9... | collective-permute-start | bytes 884744 | tf_op jit(solution)/shard_map/ppermute | solution.py:32
  43.7 14.7 %collective-permute-start.15 = (bf16[192,768]{1,0:T(8,128)(2,1)S(1)}, bf16[192,768]{1,0:T(8,128)(2,1)S(1)}, u32[]{:S(2)}, u32[]{:S(2)}) collective-permute-start(bf16[192,768]{1,0:T(8,128)(2,1)S(1)} %get-tuple-element.43), channel_id=1, source_target_pairs={{0,5},{1,15},{2,23},{3,29},{4,4},{5,14},{6,22},{7,28},{8,0},{9,10}... | collective-permute-start | bytes 884744 | tf_op jit(solution)/shard_map/ppermute | solution.py:119
  47.2 8.8 %collective-permute-start.21 = (bf16[384,384]{1,0:T(8,128)(2,1)S(1)}, bf16[384,384]{1,0:T(8,128)(2,1)S(1)}, u32[]{:S(2)}, u32[]{:S(2)}) collective-permute-start(bf16[384,384]{1,0:T(8,128)(2,1)S(1)} %slice.196), channel_id=1, source_target_pairs={{32,0},{64,32},{96,64},{0,96},{33,1},{65,33},{97,65},{1,97},{34,2}... | collective-permute-start | bytes 884744 | tf_op jit(solution)/shard_map/ppermute | solution.py:24
  48.4 9.0 %collective-permute-start.22 = (bf16[384,384]{1,0:T(8,128)(2,1)S(1)}, bf16[384,384]{1,0:T(8,128)(2,1)S(1)}, u32[]{:S(2)}, u32[]{:S(2)}) collective-permute-start(bf16[384,384]{1,0:T(8,128)(2,1)S(1)} %slice.198), channel_id=1, source_target_pairs={{96,0},{0,32},{32,64},{64,96},{97,1},{1,33},{33,65},{65,97},{98,2}... | collective-permute-start | bytes 884744 | tf_op jit(solution)/shard_map/ppermute | solution.py:24
  51.6 6.6 %collective-permute-start.14 = (bf16[384,768]{1,0:T(8,128)(2,1)S(1)}, bf16[384,768]{1,0:T(8,128)(2,1)S(1)}, u32[]{:S(2)}, u32[]{:S(2)}) collective-permute-start(bf16[384,768]{1,0:T(8,128)(2,1)S(1)} %select_convert_fusion.1), channel_id=1, source_target_pairs={{0,1},{1,0},{2,3},{3,2},{4,5},{5,4},{6,7},{7,6},{8,9},{9,8},{10,11... | collective-permute-start | bytes 1769480 | tf_op jit(solution)/shard_map/ppermute | solution.py:50
  57.8 2.3 %collective-permute-start.23 = (bf16[384,768]{1,0:T(8,128)(2,1)S(1)}, bf16[384,768]{1,0:T(8,128)(2,1)S(1)}, u32[]{:S(2)}, u32[]{:S(2)}) collective-permute-start(bf16[384,768]{1,0:T(8,128)(2,1)S(1)} %get-tuple-element.133), channel_id=1, source_target_pairs={{0,1},{1,0},{2,3},{3,2},{4,5},{5,4},{6,7},{7,6},{8,9},{9,8},{10,11... | collective-permute-start | bytes 1769480 | tf_op jit(solution)/shard_map/ppermute | solution.py:50
  58.5 11.4 %collective-permute-start.16 = (bf16[2,96,768]{2,1,0:T(8,128)(2,1)S(1)}, bf16[2,96,768]{2,1,0:T(8,128)(2,1)S(1)}, u32[]{:S(2)}, u32[]{:S(2)}) collective-permute-start(bf16[2,96,768]{2,1,0:T(8,128)(2,1)S(1)} %fusion.34), channel_id=1, source_target_pairs={{0,2},{1,3},{2,0},{3,1},{4,6},{5,7},{6,4},{7,5},{8,10},{9,11},{10,... | collective-permute-start | bytes 884744 | tf_op jit(solution)/shard_map/ppermute | solution.py:46
  60.3 15.9 %collective-permute-start.24 = (bf16[2,96,768]{2,1,0:T(8,128)(2,1)S(1)}, bf16[2,96,768]{2,1,0:T(8,128)(2,1)S(1)}, u32[]{:S(2)}, u32[]{:S(2)}) collective-permute-start(bf16[2,96,768]{2,1,0:T(8,128)(2,1)S(1)} %fusion.35), channel_id=1, source_target_pairs={{0,2},{1,3},{2,0},{3,1},{4,6},{5,7},{6,4},{7,5},{8,10},{9,11},{10,... | collective-permute-start | bytes 884744 | tf_op jit(solution)/shard_map/ppermute | solution.py:46
  70.4 12.1 %collective-permute-start.17 = (bf16[2,96,768]{2,1,0:T(8,128)(2,1)S(1)}, bf16[2,96,768]{2,1,0:T(8,128)(2,1)S(1)}, u32[]{:S(2)}, u32[]{:S(2)}) collective-permute-start(bf16[2,96,768]{2,1,0:T(8,128)(2,1)S(1)} %get-tuple-element.78), channel_id=1, source_target_pairs={{0,2},{1,3},{2,0},{3,1},{4,6},{5,7},{6,4},{7,5},{8,10},{9,11},{10,... | collective-permute-start | bytes 884744 | tf_op jit(solution)/shard_map/ppermute | solution.py:46
  76.7 13.2 %collective-permute-start.25 = (bf16[2,96,768]{2,1,0:T(8,128)(2,1)S(1)}, bf16[2,96,768]{2,1,0:T(8,128)(2,1)S(1)}, u32[]{:S(2)}, u32[]{:S(2)}) collective-permute-start(bf16[2,96,768]{2,1,0:T(8,128)(2,1)S(1)} %get-tuple-element.80), channel_id=1, source_target_pairs={{0,2},{1,3},{2,0},{3,1},{4,6},{5,7},{6,4},{7,5},{8,10},{9,11},{10,... | collective-permute-start | bytes 884744 | tf_op jit(solution)/shard_map/ppermute | solution.py:46
  82.7 2.1 %collective-permute-start.18 = (bf16[384,768]{1,0:T(8,128)(2,1)S(1)}, bf16[384,768]{1,0:T(8,128)(2,1)S(1)}, u32[]{:S(2)}, u32[]{:S(2)}) collective-permute-start(bf16[384,768]{1,0:T(8,128)(2,1)S(1)} %pad_maximum_fusion.10), channel_id=1, source_target_pairs={{0,1},{1,0},{2,3},{3,2},{4,5},{5,4},{6,7},{7,6},{8,9},{9,8},{10,11... | collective-permute-start | bytes 1769480 | tf_op jit(solution)/shard_map/ppermute | solution.py:50
  86.0 16.0 %collective-permute-start.19 = (bf16[96,1536]{1,0:T(8,128)(2,1)S(1)}, bf16[96,1536]{1,0:T(8,128)(2,1)S(1)}, u32[]{:S(2)}, u32[]{:S(2)}) collective-permute-start(bf16[96,1536]{1,0:T(8,128)(2,1)S(1)} %get-tuple-element.102), channel_id=1, source_target_pairs={{12,0},{0,4},{4,8},{8,12},{28,16},{16,20},{20,24},{24,28},{13,1},{... | collective-permute-start | bytes 884744 | tf_op jit(solution)/shard_map/ppermute | solution.py:32
  87.1 14.9 %collective-permute-start.20 = (bf16[96,1536]{1,0:T(8,128)(2,1)S(1)}, bf16[96,1536]{1,0:T(8,128)(2,1)S(1)}, u32[]{:S(2)}, u32[]{:S(2)}) collective-permute-start(bf16[96,1536]{1,0:T(8,128)(2,1)S(1)} %get-tuple-element.101), channel_id=1, source_target_pairs={{4,0},{8,4},{12,8},{0,12},{20,16},{24,20},{28,24},{16,28},{5,1},{9... | collective-permute-start | bytes 884744 | tf_op jit(solution)/shard_map/ppermute | solution.py:32
  90.1 2.1 %collective-permute-start.26 = (bf16[384,768]{1,0:T(8,128)(2,1)S(1)}, bf16[384,768]{1,0:T(8,128)(2,1)S(1)}, u32[]{:S(2)}, u32[]{:S(2)}) collective-permute-start(bf16[384,768]{1,0:T(8,128)(2,1)S(1)} %pad_maximum_fusion.11), channel_id=1, source_target_pairs={{0,1},{1,0},{2,3},{3,2},{4,5},{5,4},{6,7},{7,6},{8,9},{9,8},{10,11... | collective-permute-start | bytes 1769480 | tf_op jit(solution)/shard_map/ppermute | solution.py:50
  92.9 10.3 %collective-permute-start.27 = (bf16[384,384]{1,0:T(8,128)(2,1)S(1)}, bf16[384,384]{1,0:T(8,128)(2,1)S(1)}, u32[]{:S(2)}, u32[]{:S(2)}) collective-permute-start(bf16[384,384]{1,0:T(8,128)(2,1)S(1)} %convolution_convert_fusion.2), channel_id=1, source_target_pairs={{96,0},{0,32},{32,64},{64,96},{97,1},{1,33},{33,65},{65,97},{98,2}... | collective-permute-start | bytes 884744 | tf_op jit(solution)/shard_map/ppermute | solution.py:24
  94.0 9.2 %collective-permute-start.28 = (bf16[384,384]{1,0:T(8,128)(2,1)S(1)}, bf16[384,384]{1,0:T(8,128)(2,1)S(1)}, u32[]{:S(2)}, u32[]{:S(2)}) collective-permute-start(bf16[384,384]{1,0:T(8,128)(2,1)S(1)} %convolution_convert_fusion.1), channel_id=1, source_target_pairs={{32,0},{64,32},{96,64},{0,96},{33,1},{65,33},{97,65},{1,97},{34,2}... | collective-permute-start | bytes 884744 | tf_op jit(solution)/shard_map/ppermute | solution.py:24
  96.7 12.1 %collective-permute-start.29 = (bf16[192,768]{1,0:T(8,128)(2,1)S(1)}, bf16[192,768]{1,0:T(8,128)(2,1)S(1)}, u32[]{:S(2)}, u32[]{:S(2)}) collective-permute-start(bf16[192,768]{1,0:T(8,128)(2,1)S(1)} %get-tuple-element.51), channel_id=1, source_target_pairs={{0,0},{10,1},{18,2},{24,3},{1,4},{11,5},{19,6},{25,7},{5,8},{15,9}... | collective-permute-start | bytes 884744 | tf_op jit(solution)/shard_map/ppermute | solution.py:176
  108.9 15.1 %collective-permute-start.30 = (bf16[192,1536]{1,0:T(8,128)(2,1)S(1)}, bf16[192,1536]{1,0:T(8,128)(2,1)S(1)}, u32[]{:S(2)}, u32[]{:S(2)}) collective-permute-start(bf16[192,1536]{1,0:T(8,128)(2,1)S(1)} %add_convert_fusion.3), channel_id=1, source_target_pairs={{12,0},{0,4},{4,8},{8,12},{28,16},{16,20},{20,24},{24,28},{13,1},{... | collective-permute-start | bytes 1769480 | tf_op jit(solution)/shard_map/ppermute | solution.py:32
  110.0 16.7 %collective-permute-start.31 = (bf16[192,1536]{1,0:T(8,128)(2,1)S(1)}, bf16[192,1536]{1,0:T(8,128)(2,1)S(1)}, u32[]{:S(2)}, u32[]{:S(2)}) collective-permute-start(bf16[192,1536]{1,0:T(8,128)(2,1)S(1)} %add_convert_fusion.2), channel_id=1, source_target_pairs={{4,0},{8,4},{12,8},{0,12},{20,16},{24,20},{28,24},{16,28},{5,1},{9... | collective-permute-start | bytes 1769480 | tf_op jit(solution)/shard_map/ppermute | solution.py:32
  111.3 15.5 %collective-permute-start.32 = (bf16[768,384]{1,0:T(8,128)(2,1)S(1)}, bf16[768,384]{1,0:T(8,128)(2,1)S(1)}, u32[]{:S(2)}, u32[]{:S(2)}) collective-permute-start(bf16[768,384]{1,0:T(8,128)(2,1)S(1)} %add_convert_fusion.1), channel_id=1, source_target_pairs={{96,0},{0,32},{32,64},{64,96},{97,1},{1,33},{33,65},{65,97},{98,2}... | collective-permute-start | bytes 1769480 | tf_op jit(solution)/shard_map/ppermute | solution.py:24
  111.5 15.3 %collective-permute-start.33 = (bf16[768,384]{1,0:T(8,128)(2,1)S(1)}, bf16[768,384]{1,0:T(8,128)(2,1)S(1)}, u32[]{:S(2)}, u32[]{:S(2)}) collective-permute-start(bf16[768,384]{1,0:T(8,128)(2,1)S(1)} %add_convert_fusion), channel_id=1, source_target_pairs={{32,0},{64,32},{96,64},{0,96},{33,1},{65,33},{97,65},{1,97},{34,2}... | collective-permute-start | bytes 1769480 | tf_op jit(solution)/shard_map/ppermute | solution.py:24
  115.6 12.4 %collective-permute-start.34 = (bf16[192,768]{1,0:T(8,128)(2,1)S(1)}, bf16[192,768]{1,0:T(8,128)(2,1)S(1)}, u32[]{:S(2)}, u32[]{:S(2)}) collective-permute-start(bf16[192,768]{1,0:T(8,128)(2,1)S(1)} %get-tuple-element.67), channel_id=1, source_target_pairs={{5,0},{15,1},{23,2},{29,3},{4,4},{14,5},{22,6},{28,7},{0,8},{10,9}... | collective-permute-start | bytes 884744 | tf_op jit(solution)/shard_map/ppermute | solution.py:176
  128.1 12.1 %collective-permute-start.40 = (bf16[192,384]{1,0:T(8,128)(2,1)S(1)}, bf16[192,384]{1,0:T(8,128)(2,1)S(1)}, u32[]{:S(2)}, u32[]{:S(2)}) collective-permute-start(bf16[192,384]{1,0:T(8,128)(2,1)S(1)} %get-tuple-element.93), channel_id=1, source_target_pairs={{4,0},{8,4},{12,8},{0,12},{20,16},{24,20},{28,24},{16,28},{5,1},{9... | collective-permute-start | bytes 442376 | tf_op jit(solution)/shard_map/ppermute | solution.py:32
  131.0 9.9 %collective-permute-start.39 = (bf16[192,384]{1,0:T(8,128)(2,1)S(1)}, bf16[192,384]{1,0:T(8,128)(2,1)S(1)}, u32[]{:S(2)}, u32[]{:S(2)}) collective-permute-start(bf16[192,384]{1,0:T(8,128)(2,1)S(1)} %get-tuple-element.94), channel_id=1, source_target_pairs={{8,0},{12,4},{0,8},{4,12},{24,16},{28,20},{16,24},{20,28},{9,1},{1... | collective-permute-start | bytes 442376 | tf_op jit(solution)/shard_map/ppermute | solution.py:32
  133.1 7.9 %collective-permute-start.38 = (bf16[192,384]{1,0:T(8,128)(2,1)S(1)}, bf16[192,384]{1,0:T(8,128)(2,1)S(1)}, u32[]{:S(2)}, u32[]{:S(2)}) collective-permute-start(bf16[192,384]{1,0:T(8,128)(2,1)S(1)} %get-tuple-element.92), channel_id=1, source_target_pairs={{12,0},{0,4},{4,8},{8,12},{28,16},{16,20},{20,24},{24,28},{13,1},{... | collective-permute-start | bytes 442376 | tf_op jit(solution)/shard_map/ppermute | solution.py:32
  135.7 5.8 %collective-permute-start.37 = (bf16[192,384]{1,0:T(8,128)(2,1)S(1)}, bf16[192,384]{1,0:T(8,128)(2,1)S(1)}, u32[]{:S(2)}, u32[]{:S(2)}) collective-permute-start(bf16[192,384]{1,0:T(8,128)(2,1)S(1)} %get-tuple-element.90), channel_id=1, source_target_pairs={{32,0},{64,32},{96,64},{0,96},{33,1},{65,33},{97,65},{1,97},{34,2}... | collective-permute-start | bytes 442376 | tf_op jit(solution)/shard_map/ppermute | solution.py:24
  136.1 6.7 %collective-permute-start.36 = (bf16[192,384]{1,0:T(8,128)(2,1)S(1)}, bf16[192,384]{1,0:T(8,128)(2,1)S(1)}, u32[]{:S(2)}, u32[]{:S(2)}) collective-permute-start(bf16[192,384]{1,0:T(8,128)(2,1)S(1)} %get-tuple-element.91), channel_id=1, source_target_pairs={{64,0},{96,32},{0,64},{32,96},{65,1},{97,33},{1,65},{33,97},{66,2}... | collective-permute-start | bytes 442376 | tf_op jit(solution)/shard_map/ppermute | solution.py:24
  140.1 1.4 copy-start
  140.2 6.5 %collective-permute-start.35 = (bf16[192,384]{1,0:T(8,128)(2,1)S(1)}, bf16[192,384]{1,0:T(8,128)(2,1)S(1)}, u32[]{:S(2)}, u32[]{:S(2)}) collective-permute-start(bf16[192,384]{1,0:T(8,128)(2,1)S(1)} %get-tuple-element.89), channel_id=1, source_target_pairs={{96,0},{0,32},{32,64},{64,96},{97,1},{1,33},{33,65},{65,97},{98,2}... | collective-permute-start | bytes 442376 | tf_op jit(solution)/shard_map/ppermute | solution.py:24
  146.8 5.2 %collective-permute-start.41 = (bf16[192,384]{1,0:T(8,128)(2,1)S(1)}, bf16[192,384]{1,0:T(8,128)(2,1)S(1)}, u32[]{:S(2)}, u32[]{:S(2)}) collective-permute-start(bf16[192,384]{1,0:T(8,128)(2,1)S(1)} %pad_maximum_fusion.19), channel_id=1, source_target_pairs={{0,16},{4,20},{8,24},{12,28},{16,0},{20,4},{24,8},{28,12},{1,17},{... | collective-permute-start | bytes 442376 | tf_op jit(solution)/shard_map/ppermute | solution.py:42

commit v7 on v6

--- a/solution.py
+++ b/solution.py
@@ -103,7 +103,7 @@
     b0 = jnp.concatenate([tok_b, b2, b1, b3], 0)
     n = 2 * half
 
-    held = after_done(weight, a0, b0)
+    held = after_done(weight, a0)
     w = [lax.dynamic_slice_in_dim(held, ((x + r) % N_RING) * cols, cols, 0) for r in range(4)]
     turned = jnp.concatenate(w, 0)
     w = [turned[r * cols : (r + 1) * cols] for r in range(4)]

time: 154 us -> 154 us (level)
  no operation moved by 1% of the time
where the time goes in v7:
time: 154 us; the launch traced here: 153 us
  waiting for transfers between devices  66.3 us (43%)
  starting transfers between devices  59.3 us (39%)
  matrix products  17.6 us (11%)
  other arithmetic  5.33 us (3%)
  local copies, waits for them, and re-layouts  2.67 us (2%)
    ppermute x14, starting transfers between devices, from_z(): lax.ppermute(v, 'ja', [(y * 4 + (z + r) % N_RING, y * 4 + z) for y in ran...  21.1 us
    ppermute x14, starting transfers between devices, from_x(): return lax.ppermute(v, 'ia', [((i + r) % N_RING, i) for i in range(N_RING)])  18.9 us
    dot_general x23, matrix products, dot(): lax.dot_general(a, b, (((dims[0],), (dims[1],)), ((), ())), preferred_ele...  17.6 us
    ppermute x4, waiting for transfers between devices, swap_y_hi(): return lax.ppermute(v, 'ka', [(k, k ^ 2) for k in range(4)])  16.8 us
    ppermute x14, waiting for transfers between devices, from_x(): return lax.ppermute(v, 'ia', [((i + r) % N_RING, i) for i in range(N_RING)])  11.6 us
    ppermute x14, waiting for transfers between devices, from_z(): lax.ppermute(v, 'ja', [(y * 4 + (z + r) % N_RING, y * 4 + z) for y in ran...  11.2 us
    ppermute x1, waiting for transfers between devices, on_device(): sent0 = lax.ppermute(after_done(piece0, a0, b0), BOTH, exchange_pairs(0))  9.08 us
    ppermute x2, waiting for transfers between devices, swap_y_lo(): return lax.ppermute(v, 'ja', [(j, j ^ 4) for j in range(8)])  7.89 us
  transfers between devices with their start and end apart: 42, of which 21 were waited for; matrix products, arithmetic and copies ran while one was open for 15% of the time, Pallas kernels for 0%

profile of v7, /device:TPU:40, one launch (start us, length us, event | category | flops | bytes accessed | tf_op | source)
XLA Modules:
  0.0 152.7 jit_solution(1844786319961602132)
XLA Ops:
  2.1 4.4 %collective-permute-done = bf16[192,384]{1,0:T(8,128)(2,1)S(1)} collective-permute-done((bf16[192,384]{1,0:T(8,128)(2,1)}, bf16[192,384]{1,0:T(8,128)(2,1)S(1)}, u32[]{:S(2)}, u32[]{:S(2)}) %collective-permute-start) | collective-permute-done | bytes 147488 | tf_op jit(solution)/shard_map/ppermute | solution.py:42
  6.6 1.6 %collective-permute-start.3 = (bf16[192,384]{1,0:T(8,128)(2,1)S(1)}, bf16[192,384]{1,0:T(8,128)(2,1)S(1)}, u32[]{:S(2)}, u32[]{:S(2)}) collective-permute-start(bf16[192,384]{1,0:T(8,128)(2,1)S(1)} %pad_maximum_fusion.17), channel_id=1, source_target_pairs={{96,0},{0,32},{32,64},{64,96},{97,1},{1,33},{33,65},{65,97},{98,2}... | collective-permute-start | bytes 442376 | tf_op jit(solution)/shard_map/ppermute | solution.py:24
  8.1 2.7 %collective-permute-start.2 = (bf16[192,384]{1,0:T(8,128)(2,1)S(1)}, bf16[192,384]{1,0:T(8,128)(2,1)S(1)}, u32[]{:S(2)}, u32[]{:S(2)}) collective-permute-start(bf16[192,384]{1,0:T(8,128)(2,1)S(1)} %pad_maximum_fusion.17), channel_id=1, source_target_pairs={{64,0},{96,32},{0,64},{32,96},{65,1},{97,33},{1,65},{33,97},{66,2}... | collective-permute-start | bytes 442376 | tf_op jit(solution)/shard_map/ppermute | solution.py:24
  10.9 1.4 collective-permute-start.1
  12.5 3.1 %collective-permute-start.6 = (bf16[192,384]{1,0:T(8,128)(2,1)S(1)}, bf16[192,384]{1,0:T(8,128)(2,1)S(1)}, u32[]{:S(2)}, u32[]{:S(2)}) collective-permute-start(bf16[192,384]{1,0:T(8,128)(2,1)S(1)} %pad_maximum_fusion.18), channel_id=1, source_target_pairs={{8,0},{12,4},{0,8},{4,12},{24,16},{28,20},{16,24},{20,28},{9,1},{1... | collective-permute-start | bytes 442376 | tf_op jit(solution)/shard_map/ppermute | solution.py:32
  15.5 1.0 collective-permute-start.7
  16.6 1.0 collective-permute-start.8
  17.7 1.1 collective-permute-start.4
  18.8 1.0 collective-permute-start.5
  20.3 2.7 %collective-permute-done.7 = bf16[192,384]{1,0:T(8,128)(2,1)S(1)} collective-permute-done((bf16[192,384]{1,0:T(8,128)(2,1)S(1)}, bf16[192,384]{1,0:T(8,128)(2,1)S(1)}, u32[]{:S(2)}, u32[]{:S(2)}) %collective-permute-start.7) | collective-permute-done | bytes 147488 | tf_op jit(solution)/shard_map/ppermute | solution.py:32
  23.7 2.0 %collective-permute-start.10 = (bf16[768,384]{1,0:T(8,128)(2,1)S(1)}, bf16[768,384]{1,0:T(8,128)(2,1)S(1)}, u32[]{:S(2)}, u32[]{:S(2)}) collective-permute-start(bf16[768,384]{1,0:T(8,128)(2,1)S(1)} %constant_dynamic-update-slice_fusion), channel_id=1, source_target_pairs={{96,0},{0,32},{32,64},{64,96},{97,1},{1,33},{33,65},{65,97},{98,2}... | collective-permute-start | bytes 1769480 | tf_op jit(solution)/shard_map/ppermute | solution.py:24
  25.7 1.9 %collective-permute-start.11 = (bf16[192,768]{1,0:T(8,128)(2,1)S(1)}, bf16[192,768]{1,0:T(8,128)(2,1)S(1)}, u32[]{:S(2)}, u32[]{:S(2)}) collective-permute-start(bf16[192,768]{1,0:T(8,128)(2,1)S(1)} %get-tuple-element.38), channel_id=1, source_target_pairs={{0,0},{1,10},{2,18},{3,24},{4,1},{5,11},{6,19},{7,25},{8,5},{9,15}... | collective-permute-start | bytes 884744 | tf_op jit(solution)/shard_map/ppermute | solution.py:111
  29.4 9.1 %collective-permute-done.11 = bf16[192,768]{1,0:T(8,128)(2,1)S(1)} collective-permute-done((bf16[192,768]{1,0:T(8,128)(2,1)S(1)}, bf16[192,768]{1,0:T(8,128)(2,1)S(1)}, u32[]{:S(2)}, u32[]{:S(2)}) %collective-permute-start.11) | collective-permute-done | bytes 294944 | tf_op jit(solution)/shard_map/ppermute | solution.py:111
  38.5 1.6 %collective-permute-done.4 = bf16[192,1536]{1,0:T(8,128)(2,1)S(1)} collective-permute-done((bf16[192,1536]{1,0:T(8,128)(2,1)S(1)}, bf16[192,1536]{1,0:T(8,128)(2,1)S(1)}, u32[]{:S(2)}, u32[]{:S(2)}) %collective-permute-start.4) | collective-permute-done | bytes 589856 | tf_op jit(solution)/shard_map/ppermute | solution.py:32
  41.6 2.0 %collective-permute-start.13 = (bf16[96,1536]{1,0:T(8,128)(2,1)S(1)}, bf16[96,1536]{1,0:T(8,128)(2,1)S(1)}, u32[]{:S(2)}, u32[]{:S(2)}) collective-permute-start(bf16[96,1536]{1,0:T(8,128)(2,1)S(1)} %slice.181), channel_id=1, source_target_pairs={{12,0},{0,4},{4,8},{8,12},{28,16},{16,20},{20,24},{24,28},{13,1},{... | collective-permute-start | bytes 884744 | tf_op jit(solution)/shard_map/ppermute | solution.py:32
  43.7 3.5 %collective-permute-start.15 = (bf16[192,768]{1,0:T(8,128)(2,1)S(1)}, bf16[192,768]{1,0:T(8,128)(2,1)S(1)}, u32[]{:S(2)}, u32[]{:S(2)}) collective-permute-start(bf16[192,768]{1,0:T(8,128)(2,1)S(1)} %get-tuple-element.43), channel_id=1, source_target_pairs={{0,5},{1,15},{2,23},{3,29},{4,4},{5,14},{6,22},{7,28},{8,0},{9,10}... | collective-permute-start | bytes 884744 | tf_op jit(solution)/shard_map/ppermute | solution.py:119
  47.2 1.2 collective-permute-start.21
  48.4 1.0 collective-permute-start.22
  51.7 4.3 %collective-permute-done.21 = bf16[384,384]{1,0:T(8,128)(2,1)S(1)} collective-permute-done((bf16[384,384]{1,0:T(8,128)(2,1)S(1)}, bf16[384,384]{1,0:T(8,128)(2,1)S(1)}, u32[]{:S(2)}, u32[]{:S(2)}) %collective-permute-start.21) | collective-permute-done | bytes 294944 | tf_op jit(solution)/shard_map/ppermute | solution.py:24
  58.5 1.1 collective-permute-start.16
  60.3 2.1 %collective-permute-start.24 = (bf16[2,96,768]{2,1,0:T(8,128)(2,1)S(1)}, bf16[2,96,768]{2,1,0:T(8,128)(2,1)S(1)}, u32[]{:S(2)}, u32[]{:S(2)}) collective-permute-start(bf16[2,96,768]{2,1,0:T(8,128)(2,1)S(1)} %fusion.35), channel_id=1, source_target_pairs={{0,2},{1,3},{2,0},{3,1},{4,6},{5,7},{6,4},{7,5},{8,10},{9,11},{10,... | collective-permute-start | bytes 884744 | tf_op jit(solution)/shard_map/ppermute | solution.py:46
  62.6 7.3 %collective-permute-done.16 = bf16[2,96,768]{2,1,0:T(8,128)(2,1)S(1)} collective-permute-done((bf16[2,96,768]{2,1,0:T(8,128)(2,1)S(1)}, bf16[2,96,768]{2,1,0:T(8,128)(2,1)S(1)}, u32[]{:S(2)}, u32[]{:S(2)}) %collective-permute-start.16) | collective-permute-done | bytes 294944 | tf_op jit(solution)/shard_map/ppermute | solution.py:46
  70.4 1.1 collective-permute-start.17
  71.5 4.7 %collective-permute-done.24 = bf16[2,96,768]{2,1,0:T(8,128)(2,1)S(1)} collective-permute-done((bf16[2,96,768]{2,1,0:T(8,128)(2,1)S(1)}, bf16[2,96,768]{2,1,0:T(8,128)(2,1)S(1)}, u32[]{:S(2)}, u32[]{:S(2)}) %collective-permute-start.24) | collective-permute-done | bytes 294944 | tf_op jit(solution)/shard_map/ppermute | solution.py:46
  76.7 1.1 collective-permute-start.25
  77.8 4.8 %collective-permute-done.17 = bf16[2,96,768]{2,1,0:T(8,128)(2,1)S(1)} collective-permute-done((bf16[2,96,768]{2,1,0:T(8,128)(2,1)S(1)}, bf16[2,96,768]{2,1,0:T(8,128)(2,1)S(1)}, u32[]{:S(2)}, u32[]{:S(2)}) %collective-permute-start.17) | collective-permute-done | bytes 294944 | tf_op jit(solution)/shard_map/ppermute | solution.py:46
  82.9 1.8 %collective-permute-done.18 = bf16[384,768]{1,0:T(8,128)(2,1)S(1)} collective-permute-done((bf16[384,768]{1,0:T(8,128)(2,1)S(1)}, bf16[384,768]{1,0:T(8,128)(2,1)S(1)}, u32[]{:S(2)}, u32[]{:S(2)}) %collective-permute-start.18) | collective-permute-done | bytes 589856 | tf_op jit(solution)/shard_map/ppermute | solution.py:50
  86.0 1.1 collective-permute-start.19
  87.1 1.0 collective-permute-start.20
  90.3 1.8 %collective-permute-done.26 = bf16[384,768]{1,0:T(8,128)(2,1)S(1)} collective-permute-done((bf16[384,768]{1,0:T(8,128)(2,1)S(1)}, bf16[384,768]{1,0:T(8,128)(2,1)S(1)}, u32[]{:S(2)}, u32[]{:S(2)}) %collective-permute-start.26) | collective-permute-done | bytes 589856 | tf_op jit(solution)/shard_map/ppermute | solution.py:50
  94.0 2.8 %collective-permute-start.28 = (bf16[384,384]{1,0:T(8,128)(2,1)S(1)}, bf16[384,384]{1,0:T(8,128)(2,1)S(1)}, u32[]{:S(2)}, u32[]{:S(2)}) collective-permute-start(bf16[384,384]{1,0:T(8,128)(2,1)S(1)} %convolution_convert_fusion.1), channel_id=1, source_target_pairs={{32,0},{64,32},{96,64},{0,96},{33,1},{65,33},{97,65},{1,97},{34,2}... | collective-permute-start | bytes 884744 | tf_op jit(solution)/shard_map/ppermute | solution.py:24
  96.7 3.5 %collective-permute-start.29 = (bf16[192,768]{1,0:T(8,128)(2,1)S(1)}, bf16[192,768]{1,0:T(8,128)(2,1)S(1)}, u32[]{:S(2)}, u32[]{:S(2)}) collective-permute-start(bf16[192,768]{1,0:T(8,128)(2,1)S(1)} %get-tuple-element.51), channel_id=1, source_target_pairs={{0,0},{10,1},{18,2},{24,3},{1,4},{11,5},{19,6},{25,7},{5,8},{15,9}... | collective-permute-start | bytes 884744 | tf_op jit(solution)/shard_map/ppermute | solution.py:176
  102.0 1.2 collective-permute-done.27
  103.2 5.6 %collective-permute-done.29 = bf16[192,768]{1,0:T(8,128)(2,1)S(1)} collective-permute-done((bf16[192,768]{1,0:T(8,128)(2,1)S(1)}, bf16[192,768]{1,0:T(8,128)(2,1)S(1)}, u32[]{:S(2)}, u32[]{:S(2)}) %collective-permute-start.29) | collective-permute-done | bytes 294944 | tf_op jit(solution)/shard_map/ppermute | solution.py:176
  108.9 1.0 collective-permute-start.30
  110.0 1.1 collective-permute-start.31
  111.5 3.3 %collective-permute-start.33 = (bf16[768,384]{1,0:T(8,128)(2,1)S(1)}, bf16[768,384]{1,0:T(8,128)(2,1)S(1)}, u32[]{:S(2)}, u32[]{:S(2)}) collective-permute-start(bf16[768,384]{1,0:T(8,128)(2,1)S(1)} %add_convert_fusion), channel_id=1, source_target_pairs={{32,0},{64,32},{96,64},{0,96},{33,1},{65,33},{97,65},{1,97},{34,2}... | collective-permute-start | bytes 1769480 | tf_op jit(solution)/shard_map/ppermute | solution.py:24
  115.6 3.3 %collective-permute-start.34 = (bf16[192,768]{1,0:T(8,128)(2,1)S(1)}, bf16[192,768]{1,0:T(8,128)(2,1)S(1)}, u32[]{:S(2)}, u32[]{:S(2)}) collective-permute-start(bf16[192,768]{1,0:T(8,128)(2,1)S(1)} %get-tuple-element.67), channel_id=1, source_target_pairs={{5,0},{15,1},{23,2},{29,3},{4,4},{14,5},{22,6},{28,7},{0,8},{10,9}... | collective-permute-start | bytes 884744 | tf_op jit(solution)/shard_map/ppermute | solution.py:176
  118.9 2.1 %fusion.62 = f32[1536,768]{1,0:T(8,128)S(1)} fusion(bf16[768,1536]{1,0:T(8,128)(2,1)S(1)} %constant_dynamic-update-slice_fusion.7, bf16[768,768]{1,0:T(8,128)(2,1)S(1)} %pad_maximum_fusion.3), kind=kOutput, calls=%fused_computation.160 | convolution fusion | flops 1811939328 | bytes 8257536 | tf_op jit(solution)/shard_map/dot_general | solution.py:67
  120.9 3.1 %collective-permute-done.30 = bf16[192,1536]{1,0:T(8,128)(2,1)S(1)} collective-permute-done((bf16[192,1536]{1,0:T(8,128)(2,1)S(1)}, bf16[192,1536]{1,0:T(8,128)(2,1)S(1)}, u32[]{:S(2)}, u32[]{:S(2)}) %collective-permute-start.30) | collective-permute-done | bytes 589856 | tf_op jit(solution)/shard_map/ppermute | solution.py:32
  124.0 2.8 %collective-permute-done.31 = bf16[192,1536]{1,0:T(8,128)(2,1)S(1)} collective-permute-done((bf16[192,1536]{1,0:T(8,128)(2,1)S(1)}, bf16[192,1536]{1,0:T(8,128)(2,1)S(1)}, u32[]{:S(2)}, u32[]{:S(2)}) %collective-permute-start.31) | collective-permute-done | bytes 589856 | tf_op jit(solution)/shard_map/ppermute | solution.py:32
  128.1 2.9 %collective-permute-start.40 = (bf16[192,384]{1,0:T(8,128)(2,1)S(1)}, bf16[192,384]{1,0:T(8,128)(2,1)S(1)}, u32[]{:S(2)}, u32[]{:S(2)}) collective-permute-start(bf16[192,384]{1,0:T(8,128)(2,1)S(1)} %get-tuple-element.93), channel_id=1, source_target_pairs={{4,0},{8,4},{12,8},{0,12},{20,16},{24,20},{28,24},{16,28},{5,1},{9... | collective-permute-start | bytes 442376 | tf_op jit(solution)/shard_map/ppermute | solution.py:32
  131.0 2.0 %collective-permute-start.39 = (bf16[192,384]{1,0:T(8,128)(2,1)S(1)}, bf16[192,384]{1,0:T(8,128)(2,1)S(1)}, u32[]{:S(2)}, u32[]{:S(2)}) collective-permute-start(bf16[192,384]{1,0:T(8,128)(2,1)S(1)} %get-tuple-element.94), channel_id=1, source_target_pairs={{8,0},{12,4},{0,8},{4,12},{24,16},{28,20},{16,24},{20,28},{9,1},{1... | collective-permute-start | bytes 442376 | tf_op jit(solution)/shard_map/ppermute | solution.py:32
  133.1 2.5 %collective-permute-start.38 = (bf16[192,384]{1,0:T(8,128)(2,1)S(1)}, bf16[192,384]{1,0:T(8,128)(2,1)S(1)}, u32[]{:S(2)}, u32[]{:S(2)}) collective-permute-start(bf16[192,384]{1,0:T(8,128)(2,1)S(1)} %get-tuple-element.92), channel_id=1, source_target_pairs={{12,0},{0,4},{4,8},{8,12},{28,16},{16,20},{20,24},{24,28},{13,1},{... | collective-permute-start | bytes 442376 | tf_op jit(solution)/shard_map/ppermute | solution.py:32
  136.1 1.1 collective-permute-start.36
  141.5 1.3 collective-permute-done.36
  142.8 3.9 %collective-permute-done.35 = bf16[192,384]{1,0:T(8,128)(2,1)S(1)} collective-permute-done((bf16[192,384]{1,0:T(8,128)(2,1)S(1)}, bf16[192,384]{1,0:T(8,128)(2,1)S(1)}, u32[]{:S(2)}, u32[]{:S(2)}) %collective-permute-start.35) | collective-permute-done | bytes 147488 | tf_op jit(solution)/shard_map/ppermute | solution.py:24
  148.5 3.5 %collective-permute-done.41 = bf16[192,384]{1,0:T(8,128)(2,1)S(1)} collective-permute-done((bf16[192,384]{1,0:T(8,128)(2,1)S(1)}, bf16[192,384]{1,0:T(8,128)(2,1)S(1)}, u32[]{:S(2)}, u32[]{:S(2)}) %collective-permute-start.41) | collective-permute-done | bytes 147488 | tf_op jit(solution)/shard_map/ppermute | solution.py:42
  (134 shorter events, 29.9 us)
Async XLA Ops:
  0.6 11.7 %copy-start.2 = (bf16[192,1536]{1,0:T(8,128)(2,1)S(1)}, bf16[192,1536]{1,0:T(8,128)(2,1)}, u32[]{:S(2)}) copy-start(bf16[192,1536]{1,0:T(8,128)(2,1)} %param.5) | copy-start | bytes 1769476
  0.6 5.9 %collective-permute-start = (bf16[192,384]{1,0:T(8,128)(2,1)}, bf16[192,384]{1,0:T(8,128)(2,1)S(1)}, u32[]{:S(2)}, u32[]{:S(2)}) collective-permute-start(bf16[192,384]{1,0:T(8,128)(2,1)} %param.3), channel_id=1, source_target_pairs={{0,16},{4,20},{8,24},{12,28},{16,0},{20,4},{24,8},{28,12},{1,17},{... | collective-permute-start | bytes 442376 | tf_op jit(solution)/shard_map/ppermute | solution.py:42
  6.6 10.0 %collective-permute-start.3 = (bf16[192,384]{1,0:T(8,128)(2,1)S(1)}, bf16[192,384]{1,0:T(8,128)(2,1)S(1)}, u32[]{:S(2)}, u32[]{:S(2)}) collective-permute-start(bf16[192,384]{1,0:T(8,128)(2,1)S(1)} %pad_maximum_fusion.17), channel_id=1, source_target_pairs={{96,0},{0,32},{32,64},{64,96},{97,1},{1,33},{33,65},{65,97},{98,2}... | collective-permute-start | bytes 442376 | tf_op jit(solution)/shard_map/ppermute | solution.py:24
  8.1 9.4 %collective-permute-start.2 = (bf16[192,384]{1,0:T(8,128)(2,1)S(1)}, bf16[192,384]{1,0:T(8,128)(2,1)S(1)}, u32[]{:S(2)}, u32[]{:S(2)}) collective-permute-start(bf16[192,384]{1,0:T(8,128)(2,1)S(1)} %pad_maximum_fusion.17), channel_id=1, source_target_pairs={{64,0},{96,32},{0,64},{32,96},{65,1},{97,33},{1,65},{33,97},{66,2}... | collective-permute-start | bytes 442376 | tf_op jit(solution)/shard_map/ppermute | solution.py:24
  10.9 6.7 %collective-permute-start.1 = (bf16[192,384]{1,0:T(8,128)(2,1)S(1)}, bf16[192,384]{1,0:T(8,128)(2,1)S(1)}, u32[]{:S(2)}, u32[]{:S(2)}) collective-permute-start(bf16[192,384]{1,0:T(8,128)(2,1)S(1)} %pad_maximum_fusion.17), channel_id=1, source_target_pairs={{32,0},{64,32},{96,64},{0,96},{33,1},{65,33},{97,65},{1,97},{34,2}... | collective-permute-start | bytes 442376 | tf_op jit(solution)/shard_map/ppermute | solution.py:24
  12.5 15.1 %copy-start.1 = (bf16[1536,768]{1,0:T(8,128)(2,1)S(1)}, bf16[1536,768]{1,0:T(8,128)(2,1)}, u32[]{:S(2)}) copy-start(bf16[1536,768]{1,0:T(8,128)(2,1)} %param.4) | copy-start | bytes 7077892
  12.5 7.8 %collective-permute-start.6 = (bf16[192,384]{1,0:T(8,128)(2,1)S(1)}, bf16[192,384]{1,0:T(8,128)(2,1)S(1)}, u32[]{:S(2)}, u32[]{:S(2)}) collective-permute-start(bf16[192,384]{1,0:T(8,128)(2,1)S(1)} %pad_maximum_fusion.18), channel_id=1, source_target_pairs={{8,0},{12,4},{0,8},{4,12},{24,16},{28,20},{16,24},{20,28},{9,1},{1... | collective-permute-start | bytes 442376 | tf_op jit(solution)/shard_map/ppermute | solution.py:32
  15.5 7.5 %collective-permute-start.7 = (bf16[192,384]{1,0:T(8,128)(2,1)S(1)}, bf16[192,384]{1,0:T(8,128)(2,1)S(1)}, u32[]{:S(2)}, u32[]{:S(2)}) collective-permute-start(bf16[192,384]{1,0:T(8,128)(2,1)S(1)} %pad_maximum_fusion.18), channel_id=1, source_target_pairs={{4,0},{8,4},{12,8},{0,12},{20,16},{24,20},{28,24},{16,28},{5,1},{9... | collective-permute-start | bytes 442376 | tf_op jit(solution)/shard_map/ppermute | solution.py:32
  16.6 7.0 %collective-permute-start.8 = (bf16[192,384]{1,0:T(8,128)(2,1)S(1)}, bf16[192,384]{1,0:T(8,128)(2,1)S(1)}, u32[]{:S(2)}, u32[]{:S(2)}) collective-permute-start(bf16[192,384]{1,0:T(8,128)(2,1)S(1)} %pad_maximum_fusion.18), channel_id=1, source_target_pairs={{12,0},{0,4},{4,8},{8,12},{28,16},{16,20},{20,24},{24,28},{13,1},{... | collective-permute-start | bytes 442376 | tf_op jit(solution)/shard_map/ppermute | solution.py:32
  17.7 22.4 %collective-permute-start.4 = (bf16[192,1536]{1,0:T(8,128)(2,1)S(1)}, bf16[192,1536]{1,0:T(8,128)(2,1)S(1)}, u32[]{:S(2)}, u32[]{:S(2)}) collective-permute-start(bf16[192,1536]{1,0:T(8,128)(2,1)S(1)} %get-tuple-element.110), channel_id=1, source_target_pairs={{4,0},{8,4},{12,8},{0,12},{20,16},{24,20},{28,24},{16,28},{5,1},{9... | collective-permute-start | bytes 1769480 | tf_op jit(solution)/shard_map/ppermute | solution.py:32
  18.8 21.3 %collective-permute-start.5 = (bf16[192,1536]{1,0:T(8,128)(2,1)S(1)}, bf16[192,1536]{1,0:T(8,128)(2,1)S(1)}, u32[]{:S(2)}, u32[]{:S(2)}) collective-permute-start(bf16[192,1536]{1,0:T(8,128)(2,1)S(1)} %get-tuple-element.110), channel_id=1, source_target_pairs={{12,0},{0,4},{4,8},{8,12},{28,16},{16,20},{20,24},{24,28},{13,1},{... | collective-permute-start | bytes 1769480 | tf_op jit(solution)/shard_map/ppermute | solution.py:32
  23.6 16.5 %collective-permute-start.9 = (bf16[768,384]{1,0:T(8,128)(2,1)S(1)}, bf16[768,384]{1,0:T(8,128)(2,1)S(1)}, u32[]{:S(2)}, u32[]{:S(2)}) collective-permute-start(bf16[768,384]{1,0:T(8,128)(2,1)S(1)} %constant_dynamic-update-slice_fusion), channel_id=1, source_target_pairs={{32,0},{64,32},{96,64},{0,96},{33,1},{65,33},{97,65},{1,97},{34,2}... | collective-permute-start | bytes 1769480 | tf_op jit(solution)/shard_map/ppermute | solution.py:24
  23.7 16.4 %collective-permute-start.10 = (bf16[768,384]{1,0:T(8,128)(2,1)S(1)}, bf16[768,384]{1,0:T(8,128)(2,1)S(1)}, u32[]{:S(2)}, u32[]{:S(2)}) collective-permute-start(bf16[768,384]{1,0:T(8,128)(2,1)S(1)} %constant_dynamic-update-slice_fusion), channel_id=1, source_target_pairs={{96,0},{0,32},{32,64},{64,96},{97,1},{1,33},{33,65},{65,97},{98,2}... | collective-permute-start | bytes 1769480 | tf_op jit(solution)/shard_map/ppermute | solution.py:24
  25.7 12.8 %collective-permute-start.11 = (bf16[192,768]{1,0:T(8,128)(2,1)S(1)}, bf16[192,768]{1,0:T(8,128)(2,1)S(1)}, u32[]{:S(2)}, u32[]{:S(2)}) collective-permute-start(bf16[192,768]{1,0:T(8,128)(2,1)S(1)} %get-tuple-element.38), channel_id=1, source_target_pairs={{0,0},{1,10},{2,18},{3,24},{4,1},{5,11},{6,19},{7,25},{8,5},{9,15}... | collective-permute-start | bytes 884744 | tf_op jit(solution)/shard_map/ppermute | solution.py:111
  41.6 9.2 %collective-permute-start.13 = (bf16[96,1536]{1,0:T(8,128)(2,1)S(1)}, bf16[96,1536]{1,0:T(8,128)(2,1)S(1)}, u32[]{:S(2)}, u32[]{:S(2)}) collective-permute-start(bf16[96,1536]{1,0:T(8,128)(2,1)S(1)} %slice.181), channel_id=1, source_target_pairs={{12,0},{0,4},{4,8},{8,12},{28,16},{16,20},{20,24},{24,28},{13,1},{... | collective-permute-start | bytes 884744 | tf_op jit(solution)/shard_map/ppermute | solution.py:32
  43.6 7.3 %collective-permute-start.12 = (bf16[96,1536]{1,0:T(8,128)(2,1)S(1)}, bf16[96,1536]{1,0:T(8,128)(2,1)S(1)}, u32[]{:S(2)}, u32[]{:S(2)}) collective-permute-start(bf16[96,1536]{1,0:T(8,128)(2,1)S(1)} %slice.180), channel_id=1, source_target_pairs={{4,0},{8,4},{12,8},{0,12},{20,16},{24,20},{28,24},{16,28},{5,1},{9... | collective-permute-start | bytes 884744 | tf_op jit(solution)/shard_map/ppermute | solution.py:32
  43.7 14.7 %collective-permute-start.15 = (bf16[192,768]{1,0:T(8,128)(2,1)S(1)}, bf16[192,768]{1,0:T(8,128)(2,1)S(1)}, u32[]{:S(2)}, u32[]{:S(2)}) collective-permute-start(bf16[192,768]{1,0:T(8,128)(2,1)S(1)} %get-tuple-element.43), channel_id=1, source_target_pairs={{0,5},{1,15},{2,23},{3,29},{4,4},{5,14},{6,22},{7,28},{8,0},{9,10}... | collective-permute-start | bytes 884744 | tf_op jit(solution)/shard_map/ppermute | solution.py:119
  47.2 8.8 %collective-permute-start.21 = (bf16[384,384]{1,0:T(8,128)(2,1)S(1)}, bf16[384,384]{1,0:T(8,128)(2,1)S(1)}, u32[]{:S(2)}, u32[]{:S(2)}) collective-permute-start(bf16[384,384]{1,0:T(8,128)(2,1)S(1)} %slice.196), channel_id=1, source_target_pairs={{32,0},{64,32},{96,64},{0,96},{33,1},{65,33},{97,65},{1,97},{34,2}... | collective-permute-start | bytes 884744 | tf_op jit(solution)/shard_map/ppermute | solution.py:24
  48.4 9.0 %collective-permute-start.22 = (bf16[384,384]{1,0:T(8,128)(2,1)S(1)}, bf16[384,384]{1,0:T(8,128)(2,1)S(1)}, u32[]{:S(2)}, u32[]{:S(2)}) collective-permute-start(bf16[384,384]{1,0:T(8,128)(2,1)S(1)} %slice.198), channel_id=1, source_target_pairs={{96,0},{0,32},{32,64},{64,96},{97,1},{1,33},{33,65},{65,97},{98,2}... | collective-permute-start | bytes 884744 | tf_op jit(solution)/shard_map/ppermute | solution.py:24
  51.6 6.6 %collective-permute-start.14 = (bf16[384,768]{1,0:T(8,128)(2,1)S(1)}, bf16[384,768]{1,0:T(8,128)(2,1)S(1)}, u32[]{:S(2)}, u32[]{:S(2)}) collective-permute-start(bf16[384,768]{1,0:T(8,128)(2,1)S(1)} %select_convert_fusion.1), channel_id=1, source_target_pairs={{0,1},{1,0},{2,3},{3,2},{4,5},{5,4},{6,7},{7,6},{8,9},{9,8},{10,11... | collective-permute-start | bytes 1769480 | tf_op jit(solution)/shard_map/ppermute | solution.py:50
  57.8 2.3 %collective-permute-start.23 = (bf16[384,768]{1,0:T(8,128)(2,1)S(1)}, bf16[384,768]{1,0:T(8,128)(2,1)S(1)}, u32[]{:S(2)}, u32[]{:S(2)}) collective-permute-start(bf16[384,768]{1,0:T(8,128)(2,1)S(1)} %get-tuple-element.133), channel_id=1, source_target_pairs={{0,1},{1,0},{2,3},{3,2},{4,5},{5,4},{6,7},{7,6},{8,9},{9,8},{10,11... | collective-permute-start | bytes 1769480 | tf_op jit(solution)/shard_map/ppermute | solution.py:50
  58.5 11.4 %collective-permute-start.16 = (bf16[2,96,768]{2,1,0:T(8,128)(2,1)S(1)}, bf16[2,96,768]{2,1,0:T(8,128)(2,1)S(1)}, u32[]{:S(2)}, u32[]{:S(2)}) collective-permute-start(bf16[2,96,768]{2,1,0:T(8,128)(2,1)S(1)} %fusion.34), channel_id=1, source_target_pairs={{0,2},{1,3},{2,0},{3,1},{4,6},{5,7},{6,4},{7,5},{8,10},{9,11},{10,... | collective-permute-start | bytes 884744 | tf_op jit(solution)/shard_map/ppermute | solution.py:46
  60.3 15.9 %collective-permute-start.24 = (bf16[2,96,768]{2,1,0:T(8,128)(2,1)S(1)}, bf16[2,96,768]{2,1,0:T(8,128)(2,1)S(1)}, u32[]{:S(2)}, u32[]{:S(2)}) collective-permute-start(bf16[2,96,768]{2,1,0:T(8,128)(2,1)S(1)} %fusion.35), channel_id=1, source_target_pairs={{0,2},{1,3},{2,0},{3,1},{4,6},{5,7},{6,4},{7,5},{8,10},{9,11},{10,... | collective-permute-start | bytes 884744 | tf_op jit(solution)/shard_map/ppermute | solution.py:46
  70.4 12.1 %collective-permute-start.17 = (bf16[2,96,768]{2,1,0:T(8,128)(2,1)S(1)}, bf16[2,96,768]{2,1,0:T(8,128)(2,1)S(1)}, u32[]{:S(2)}, u32[]{:S(2)}) collective-permute-start(bf16[2,96,768]{2,1,0:T(8,128)(2,1)S(1)} %get-tuple-element.78), channel_id=1, source_target_pairs={{0,2},{1,3},{2,0},{3,1},{4,6},{5,7},{6,4},{7,5},{8,10},{9,11},{10,... | collective-permute-start | bytes 884744 | tf_op jit(solution)/shard_map/ppermute | solution.py:46
  76.7 13.2 %collective-permute-start.25 = (bf16[2,96,768]{2,1,0:T(8,128)(2,1)S(1)}, bf16[2,96,768]{2,1,0:T(8,128)(2,1)S(1)}, u32[]{:S(2)}, u32[]{:S(2)}) collective-permute-start(bf16[2,96,768]{2,1,0:T(8,128)(2,1)S(1)} %get-tuple-element.80), channel_id=1, source_target_pairs={{0,2},{1,3},{2,0},{3,1},{4,6},{5,7},{6,4},{7,5},{8,10},{9,11},{10,... | collective-permute-start | bytes 884744 | tf_op jit(solution)/shard_map/ppermute | solution.py:46
  82.7 2.1 %collective-permute-start.18 = (bf16[384,768]{1,0:T(8,128)(2,1)S(1)}, bf16[384,768]{1,0:T(8,128)(2,1)S(1)}, u32[]{:S(2)}, u32[]{:S(2)}) collective-permute-start(bf16[384,768]{1,0:T(8,128)(2,1)S(1)} %pad_maximum_fusion.10), channel_id=1, source_target_pairs={{0,1},{1,0},{2,3},{3,2},{4,5},{5,4},{6,7},{7,6},{8,9},{9,8},{10,11... | collective-permute-start | bytes 1769480 | tf_op jit(solution)/shard_map/ppermute | solution.py:50
  86.0 16.0 %collective-permute-start.19 = (bf16[96,1536]{1,0:T(8,128)(2,1)S(1)}, bf16[96,1536]{1,0:T(8,128)(2,1)S(1)}, u32[]{:S(2)}, u32[]{:S(2)}) collective-permute-start(bf16[96,1536]{1,0:T(8,128)(2,1)S(1)} %get-tuple-element.102), channel_id=1, source_target_pairs={{12,0},{0,4},{4,8},{8,12},{28,16},{16,20},{20,24},{24,28},{13,1},{... | collective-permute-start | bytes 884744 | tf_op jit(solution)/shard_map/ppermute | solution.py:32
  87.1 14.9 %collective-permute-start.20 = (bf16[96,1536]{1,0:T(8,128)(2,1)S(1)}, bf16[96,1536]{1,0:T(8,128)(2,1)S(1)}, u32[]{:S(2)}, u32[]{:S(2)}) collective-permute-start(bf16[96,1536]{1,0:T(8,128)(2,1)S(1)} %get-tuple-element.101), channel_id=1, source_target_pairs={{4,0},{8,4},{12,8},{0,12},{20,16},{24,20},{28,24},{16,28},{5,1},{9... | collective-permute-start | bytes 884744 | tf_op jit(solution)/shard_map/ppermute | solution.py:32
  90.1 2.1 %collective-permute-start.26 = (bf16[384,768]{1,0:T(8,128)(2,1)S(1)}, bf16[384,768]{1,0:T(8,128)(2,1)S(1)}, u32[]{:S(2)}, u32[]{:S(2)}) collective-permute-start(bf16[384,768]{1,0:T(8,128)(2,1)S(1)} %pad_maximum_fusion.11), channel_id=1, source_target_pairs={{0,1},{1,0},{2,3},{3,2},{4,5},{5,4},{6,7},{7,6},{8,9},{9,8},{10,11... | collective-permute-start | bytes 1769480 | tf_op jit(solution)/shard_map/ppermute | solution.py:50
  92.9 10.3 %collective-permute-start.27 = (bf16[384,384]{1,0:T(8,128)(2,1)S(1)}, bf16[384,384]{1,0:T(8,128)(2,1)S(1)}, u32[]{:S(2)}, u32[]{:S(2)}) collective-permute-start(bf16[384,384]{1,0:T(8,128)(2,1)S(1)} %convolution_convert_fusion.2), channel_id=1, source_target_pairs={{96,0},{0,32},{32,64},{64,96},{97,1},{1,33},{33,65},{65,97},{98,2}... | collective-permute-start | bytes 884744 | tf_op jit(solution)/shard_map/ppermute | solution.py:24
  94.0 9.2 %collective-permute-start.28 = (bf16[384,384]{1,0:T(8,128)(2,1)S(1)}, bf16[384,384]{1,0:T(8,128)(2,1)S(1)}, u32[]{:S(2)}, u32[]{:S(2)}) collective-permute-start(bf16[384,384]{1,0:T(8,128)(2,1)S(1)} %convolution_convert_fusion.1), channel_id=1, source_target_pairs={{32,0},{64,32},{96,64},{0,96},{33,1},{65,33},{97,65},{1,97},{34,2}... | collective-permute-start | bytes 884744 | tf_op jit(solution)/shard_map/ppermute | solution.py:24
  96.7 12.1 %collective-permute-start.29 = (bf16[192,768]{1,0:T(8,128)(2,1)S(1)}, bf16[192,768]{1,0:T(8,128)(2,1)S(1)}, u32[]{:S(2)}, u32[]{:S(2)}) collective-permute-start(bf16[192,768]{1,0:T(8,128)(2,1)S(1)} %get-tuple-element.51), channel_id=1, source_target_pairs={{0,0},{10,1},{18,2},{24,3},{1,4},{11,5},{19,6},{25,7},{5,8},{15,9}... | collective-permute-start | bytes 884744 | tf_op jit(solution)/shard_map/ppermute | solution.py:176
  108.9 15.1 %collective-permute-start.30 = (bf16[192,1536]{1,0:T(8,128)(2,1)S(1)}, bf16[192,1536]{1,0:T(8,128)(2,1)S(1)}, u32[]{:S(2)}, u32[]{:S(2)}) collective-permute-start(bf16[192,1536]{1,0:T(8,128)(2,1)S(1)} %add_convert_fusion.3), channel_id=1, source_target_pairs={{12,0},{0,4},{4,8},{8,12},{28,16},{16,20},{20,24},{24,28},{13,1},{... | collective-permute-start | bytes 1769480 | tf_op jit(solution)/shard_map/ppermute | solution.py:32
  110.0 16.7 %collective-permute-start.31 = (bf16[192,1536]{1,0:T(8,128)(2,1)S(1)}, bf16[192,1536]{1,0:T(8,128)(2,1)S(1)}, u32[]{:S(2)}, u32[]{:S(2)}) collective-permute-start(bf16[192,1536]{1,0:T(8,128)(2,1)S(1)} %add_convert_fusion.2), channel_id=1, source_target_pairs={{4,0},{8,4},{12,8},{0,12},{20,16},{24,20},{28,24},{16,28},{5,1},{9... | collective-permute-start | bytes 1769480 | tf_op jit(solution)/shard_map/ppermute | solution.py:32
  111.3 15.5 %collective-permute-start.32 = (bf16[768,384]{1,0:T(8,128)(2,1)S(1)}, bf16[768,384]{1,0:T(8,128)(2,1)S(1)}, u32[]{:S(2)}, u32[]{:S(2)}) collective-permute-start(bf16[768,384]{1,0:T(8,128)(2,1)S(1)} %add_convert_fusion.1), channel_id=1, source_target_pairs={{96,0},{0,32},{32,64},{64,96},{97,1},{1,33},{33,65},{65,97},{98,2}... | collective-permute-start | bytes 1769480 | tf_op jit(solution)/shard_map/ppermute | solution.py:24
  111.5 15.3 %collective-permute-start.33 = (bf16[768,384]{1,0:T(8,128)(2,1)S(1)}, bf16[768,384]{1,0:T(8,128)(2,1)S(1)}, u32[]{:S(2)}, u32[]{:S(2)}) collective-permute-start(bf16[768,384]{1,0:T(8,128)(2,1)S(1)} %add_convert_fusion), channel_id=1, source_target_pairs={{32,0},{64,32},{96,64},{0,96},{33,1},{65,33},{97,65},{1,97},{34,2}... | collective-permute-start | bytes 1769480 | tf_op jit(solution)/shard_map/ppermute | solution.py:24
  115.6 12.4 %collective-permute-start.34 = (bf16[192,768]{1,0:T(8,128)(2,1)S(1)}, bf16[192,768]{1,0:T(8,128)(2,1)S(1)}, u32[]{:S(2)}, u32[]{:S(2)}) collective-permute-start(bf16[192,768]{1,0:T(8,128)(2,1)S(1)} %get-tuple-element.67), channel_id=1, source_target_pairs={{5,0},{15,1},{23,2},{29,3},{4,4},{14,5},{22,6},{28,7},{0,8},{10,9}... | collective-permute-start | bytes 884744 | tf_op jit(solution)/shard_map/ppermute | solution.py:176
  128.1 12.1 %collective-permute-start.40 = (bf16[192,384]{1,0:T(8,128)(2,1)S(1)}, bf16[192,384]{1,0:T(8,128)(2,1)S(1)}, u32[]{:S(2)}, u32[]{:S(2)}) collective-permute-start(bf16[192,384]{1,0:T(8,128)(2,1)S(1)} %get-tuple-element.93), channel_id=1, source_target_pairs={{4,0},{8,4},{12,8},{0,12},{20,16},{24,20},{28,24},{16,28},{5,1},{9... | collective-permute-start | bytes 442376 | tf_op jit(solution)/shard_map/ppermute | solution.py:32
  131.0 9.9 %collective-permute-start.39 = (bf16[192,384]{1,0:T(8,128)(2,1)S(1)}, bf16[192,384]{1,0:T(8,128)(2,1)S(1)}, u32[]{:S(2)}, u32[]{:S(2)}) collective-permute-start(bf16[192,384]{1,0:T(8,128)(2,1)S(1)} %get-tuple-element.94), channel_id=1, source_target_pairs={{8,0},{12,4},{0,8},{4,12},{24,16},{28,20},{16,24},{20,28},{9,1},{1... | collective-permute-start | bytes 442376 | tf_op jit(solution)/shard_map/ppermute | solution.py:32
  133.1 7.9 %collective-permute-start.38 = (bf16[192,384]{1,0:T(8,128)(2,1)S(1)}, bf16[192,384]{1,0:T(8,128)(2,1)S(1)}, u32[]{:S(2)}, u32[]{:S(2)}) collective-permute-start(bf16[192,384]{1,0:T(8,128)(2,1)S(1)} %get-tuple-element.92), channel_id=1, source_target_pairs={{12,0},{0,4},{4,8},{8,12},{28,16},{16,20},{20,24},{24,28},{13,1},{... | collective-permute-start | bytes 442376 | tf_op jit(solution)/shard_map/ppermute | solution.py:32
  135.7 5.8 %collective-permute-start.37 = (bf16[192,384]{1,0:T(8,128)(2,1)S(1)}, bf16[192,384]{1,0:T(8,128)(2,1)S(1)}, u32[]{:S(2)}, u32[]{:S(2)}) collective-permute-start(bf16[192,384]{1,0:T(8,128)(2,1)S(1)} %get-tuple-element.90), channel_id=1, source_target_pairs={{32,0},{64,32},{96,64},{0,96},{33,1},{65,33},{97,65},{1,97},{34,2}... | collective-permute-start | bytes 442376 | tf_op jit(solution)/shard_map/ppermute | solution.py:24
  136.1 6.7 %collective-permute-start.36 = (bf16[192,384]{1,0:T(8,128)(2,1)S(1)}, bf16[192,384]{1,0:T(8,128)(2,1)S(1)}, u32[]{:S(2)}, u32[]{:S(2)}) collective-permute-start(bf16[192,384]{1,0:T(8,128)(2,1)S(1)} %get-tuple-element.91), channel_id=1, source_target_pairs={{64,0},{96,32},{0,64},{32,96},{65,1},{97,33},{1,65},{33,97},{66,2}... | collective-permute-start | bytes 442376 | tf_op jit(solution)/shard_map/ppermute | solution.py:24
  140.1 1.4 copy-start
  140.2 6.5 %collective-permute-start.35 = (bf16[192,384]{1,0:T(8,128)(2,1)S(1)}, bf16[192,384]{1,0:T(8,128)(2,1)S(1)}, u32[]{:S(2)}, u32[]{:S(2)}) collective-permute-start(bf16[192,384]{1,0:T(8,128)(2,1)S(1)} %get-tuple-element.89), channel_id=1, source_target_pairs={{96,0},{0,32},{32,64},{64,96},{97,1},{1,33},{33,65},{65,97},{98,2}... | collective-permute-start | bytes 442376 | tf_op jit(solution)/shard_map/ppermute | solution.py:24
  146.8 5.2 %collective-permute-start.41 = (bf16[192,384]{1,0:T(8,128)(2,1)S(1)}, bf16[192,384]{1,0:T(8,128)(2,1)S(1)}, u32[]{:S(2)}, u32[]{:S(2)}) collective-permute-start(bf16[192,384]{1,0:T(8,128)(2,1)S(1)} %pad_maximum_fusion.19), channel_id=1, source_target_pairs={{0,16},{4,20},{8,24},{12,28},{16,0},{20,4},{24,8},{28,12},{1,17},{... | collective-permute-start | bytes 442376 | tf_op jit(solution)/shard_map/ppermute | solution.py:42
